TPU v7x, 32 devices: a whole 2x2x4 slice. The times are simulated.
32 devices in a mesh: fsdp: 8 (over z, y), tp: 4 (over x, core).
Axes of the slice: x: 2, y: 2, z: 4, core: 2. Of those that a mesh axis runs over, the one named last changes fastest.
Arguments:
- audio_states: bfloat16 [16, 1024, 1536], P('fsdp', 'tp'), may hold values from -6 to 6
- text_states: bfloat16 [16, 64, 1536], P('fsdp', 'tp'), may hold values from -6 to 6
- out_grad: bfloat16 [16, 1024, 1536], P('fsdp', 'tp'), may hold values from -6 to 6
- self_qkv: bfloat16 [3, 1536, 1536], P(None, 'fsdp', 'tp'), may hold values from -0.15625 to 0.15625
- self_out: bfloat16 [1536, 1536], P('tp', 'fsdp'), may hold values from -1.25 to 1.25
- cross_query: bfloat16 [1536, 1536], P('fsdp', 'tp'), may hold values from -0.15625 to 0.15625
- cross_kv: bfloat16 [2, 1536, 1536], P(None, 'fsdp', 'tp'), may hold values from -0.15625 to 0.15625
- cross_out: bfloat16 [1536, 1536], P('tp', 'fsdp'), may hold values from -0.625 to 0.625
- mlp_up: bfloat16 [1536, 6144], P('fsdp', 'tp'), may hold values from -0.15625 to 0.15625
- mlp_down: bfloat16 [6144, 1536], P('tp', 'fsdp'), may hold values from -0.15625 to 0.15625
- norm_gain: bfloat16 [3, 1536], P(None, 'fsdp'), may hold values from 0.099609375 to 1.8984375
- norm_bias: bfloat16 [3, 1536], P(None, 'fsdp'), may hold values from -3 to 3
Outputs:
- layer_out: bfloat16 [16, 1024, 1536], P('fsdp', 'tp')
- audio_grad: bfloat16 [16, 1024, 1536], P('fsdp', 'tp')
- text_grad: bfloat16 [16, 64, 1536], P('fsdp', 'tp')
- grad_self_qkv: float32 [3, 1536, 1536], P(None, 'fsdp', 'tp')
- grad_self_out: float32 [1536, 1536], P('tp', 'fsdp')
- grad_cross_query: float32 [1536, 1536], P('fsdp', 'tp')
- grad_cross_kv: float32 [2, 1536, 1536], P(None, 'fsdp', 'tp')
- grad_cross_out: float32 [1536, 1536], P('tp', 'fsdp')
- grad_mlp_up: float32 [1536, 6144], P('fsdp', 'tp')
- grad_mlp_down: float32 [6144, 1536], P('tp', 'fsdp')
- grad_norm_gain: float32 [3, 1536], P(None, 'fsdp')
- grad_norm_bias: float32 [3, 1536], P(None, 'fsdp')
All inputs are finite; a program needn't handle non-finite values.
Results may differ from a plain program's by a relative error of at most 0.02.
Values may be sent and summed in bfloat16 or wider, within the bound.
A program may use at most 200 MiB of HBM per device.

v0:
```python
from functools import partial

import jax
import jax.numpy as jnp
from jax import lax
from jax.sharding import PartitionSpec as P

HEAD = 64


epsilon = 1e-05


def norm_rows(stream, factor, offset):
    center = stream - jnp.mean(stream, axis=-1, keepdims=True)
    spread = jnp.mean(center * center, axis=-1, keepdims=True)
    return center * lax.rsqrt(spread + epsilon) * factor + offset


def masked_scores(query_heads, key_heads, begin_at, causal):
    factor = query_heads.shape[2] ** (-0.5)
    scores = (
        jnp.einsum("qhd,khd->hqk", query_heads, key_heads, preferred_element_type=jnp.float32)
        * factor
    )
    if causal:
        row_at = begin_at + lax.broadcasted_iota(jnp.int32, scores.shape, 1)
        col_at = lax.broadcasted_iota(jnp.int32, scores.shape, 2)
        scores = jnp.where(row_at >= col_at, scores, -1e30)
    return scores


def attend_forward(query_heads, key_heads, value_heads, causal):
    length = query_heads.shape[0]
    block_rows = min(512, length)
    blocked = []
    log_totals = []
    for begin_at in range(0, length, block_rows):
        scores = masked_scores(
            query_heads[begin_at : begin_at + block_rows], key_heads, begin_at, causal
        )
        row_peak = jnp.max(scores, axis=-1, keepdims=True)
        shifted = jnp.exp(scores - row_peak)
        row_total = jnp.sum(shifted, axis=-1, keepdims=True)
        attention = (shifted / row_total).astype(jnp.bfloat16)
        blocked.append(
            jnp.einsum("hqk,khd->qhd", attention, value_heads, preferred_element_type=jnp.float32)
        )
        log_totals.append(row_peak + jnp.log(row_total))
    return (jnp.concatenate(blocked, 0), jnp.concatenate(log_totals, 1))


def attend_backward(query_heads, key_heads, value_heads, log_totals, grad_heads, causal):
    factor = query_heads.shape[2] ** (-0.5)
    length = query_heads.shape[0]
    block_rows = min(512, length)
    key_grad = jnp.zeros(key_heads.shape, jnp.float32)
    value_grad = jnp.zeros(value_heads.shape, jnp.float32)
    query_parts = []
    for begin_at in range(0, length, block_rows):
        part_query = query_heads[begin_at : begin_at + block_rows]
        part_grad = grad_heads[begin_at : begin_at + block_rows]
        scores = masked_scores(part_query, key_heads, begin_at, causal)
        attention = jnp.exp(scores - log_totals[:, begin_at : begin_at + block_rows])
        attn_grad = jnp.einsum(
            "qhd,khd->hqk", part_grad, value_heads, preferred_element_type=jnp.float32
        )
        row_inner = jnp.sum(attention * attn_grad, axis=-1, keepdims=True)
        score_grad = (attention * (attn_grad - row_inner)).astype(jnp.bfloat16)
        query_parts.append(
            (
                jnp.einsum(
                    "hqk,khd->qhd", score_grad, key_heads, preferred_element_type=jnp.float32
                )
                * factor
            ).astype(jnp.bfloat16)
        )
        key_grad = (
            key_grad
            + jnp.einsum("hqk,qhd->khd", score_grad, part_query, preferred_element_type=jnp.float32)
            * factor
        )
        value_grad = value_grad + jnp.einsum(
            "hqk,qhd->khd",
            attention.astype(jnp.bfloat16),
            part_grad,
            preferred_element_type=jnp.float32,
        )
    return (
        jnp.concatenate(query_parts, 0),
        key_grad.astype(jnp.bfloat16),
        value_grad.astype(jnp.bfloat16),
    )


def row_product(left_rows, weight, left_dims, right_dims):
    return lax.dot_general(
        left_rows, weight, ((left_dims, right_dims), ((), ())), preferred_element_type=jnp.float32
    )


def gather_rows(values):
    return lax.all_gather(values, "tp", axis=0, tiled=True)


def gather_grads(values):
    return lax.all_gather(values, "tp", axis=0, tiled=True)


def sum_forward(left_rows, weight, left_dims, right_dims):
    return lax.psum_scatter(
        row_product(left_rows, weight, left_dims, right_dims), "tp", scatter_dimension=0, tiled=True
    )


def sum_backward(left_rows, weight, left_dims, right_dims):
    return lax.psum_scatter(
        row_product(left_rows, weight, left_dims, right_dims), "tp", scatter_dimension=0, tiled=True
    )


def sum_text(left_rows, weight, left_dims, right_dims):
    return lax.psum_scatter(
        row_product(left_rows, weight, left_dims, right_dims).astype(jnp.bfloat16),
        "tp",
        scatter_dimension=0,
        tiled=True,
    ).astype(jnp.float32)


def reduce_grads(parts):
    return (
        lax.psum_scatter(parts[0], "fsdp", scatter_dimension=1, tiled=True),
        lax.psum_scatter(parts[1], "fsdp", scatter_dimension=1, tiled=True),
        lax.psum_scatter(parts[2], "fsdp", scatter_dimension=0, tiled=True),
        lax.psum_scatter(parts[3], "fsdp", scatter_dimension=1, tiled=True),
        lax.psum_scatter(parts[4], "fsdp", scatter_dimension=1, tiled=True),
        lax.psum_scatter(parts[5], "fsdp", scatter_dimension=0, tiled=True),
        lax.psum_scatter(parts[6], "fsdp", scatter_dimension=1, tiled=True),
        lax.psum_scatter(parts[7], "fsdp", scatter_dimension=1, tiled=True),
        lax.psum_scatter(parts[8], "fsdp", scatter_dimension=1, tiled=True),
    )


def local(
    audio_states,
    text_states,
    out_grad,
    self_qkv,
    self_out,
    cross_query,
    cross_kv,
    cross_out,
    mlp_up,
    mlp_down,
    norm_gain,
    norm_bias,
):
    layer_rows = []
    audio_rows = []
    text_rows = []
    totals = None
    for sample in range(audio_states.shape[0]):
        gathered = (
            lax.all_gather(self_qkv, "fsdp", axis=1, tiled=True),
            lax.all_gather(self_out, "fsdp", axis=1, tiled=True),
            lax.all_gather(cross_query, "fsdp", axis=0, tiled=True),
            lax.all_gather(cross_kv, "fsdp", axis=1, tiled=True),
            lax.all_gather(cross_out, "fsdp", axis=1, tiled=True),
            lax.all_gather(mlp_up, "fsdp", axis=0, tiled=True),
            lax.all_gather(mlp_down, "fsdp", axis=1, tiled=True),
            lax.all_gather(norm_gain, "fsdp", axis=1, tiled=True),
            lax.all_gather(norm_bias, "fsdp", axis=1, tiled=True),
        )
        (
            qkv_weight,
            out_weight,
            query_weight,
            kv_weight,
            cross_weight,
            up_weight,
            down_weight,
            gain_rows,
            bias_rows,
        ) = gathered
        gain_rows = gain_rows.astype(jnp.float32)
        bias_rows = bias_rows.astype(jnp.float32)
        stream_in = audio_states[sample].astype(jnp.float32)
        full_self = gather_rows(
            norm_rows(stream_in, gain_rows[0], bias_rows[0]).astype(jnp.bfloat16)
        )
        length = full_self.shape[0]
        local_heads = qkv_weight.shape[2] // HEAD
        qkv_rows = jnp.einsum(
            "nd,cde->nce", full_self, qkv_weight, preferred_element_type=jnp.float32
        ).astype(jnp.bfloat16)
        query_heads = qkv_rows[:, 0].reshape(length, local_heads, HEAD)
        key_heads = qkv_rows[:, 1].reshape(length, local_heads, HEAD)
        value_heads = qkv_rows[:, 2].reshape(length, local_heads, HEAD)
        self_attn, self_log = attend_forward(query_heads, key_heads, value_heads, True)
        self_attn = self_attn.reshape(length, -1).astype(jnp.bfloat16)
        stream_mid = stream_in + sum_forward(self_attn, out_weight, (1,), (0,))
        full_cross = gather_rows(
            norm_rows(stream_mid, gain_rows[1], bias_rows[1]).astype(jnp.bfloat16)
        )
        cross_heads = (
            jnp.dot(full_cross, query_weight, preferred_element_type=jnp.float32)
            .astype(jnp.bfloat16)
            .reshape(length, local_heads, HEAD)
        )
        text_full = lax.all_gather(text_states[sample], "tp", axis=0, tiled=True)
        text_len = text_full.shape[0]
        text_kv = jnp.einsum(
            "td,cde->tce", text_full, kv_weight, preferred_element_type=jnp.float32
        ).astype(jnp.bfloat16)
        text_keys = text_kv[:, 0].reshape(text_len, local_heads, HEAD)
        text_values = text_kv[:, 1].reshape(text_len, local_heads, HEAD)
        cross_attn, cross_log = attend_forward(cross_heads, text_keys, text_values, False)
        cross_attn = cross_attn.reshape(length, -1).astype(jnp.bfloat16)
        stream_late = stream_mid + sum_forward(cross_attn, cross_weight, (1,), (0,))
        full_ffn = gather_rows(
            norm_rows(stream_late, gain_rows[2], bias_rows[2]).astype(jnp.bfloat16)
        )
        hidden = jnp.dot(full_ffn, up_weight, preferred_element_type=jnp.float32)
        active = jax.nn.gelu(hidden, approximate=False).astype(jnp.bfloat16)
        layer_rows.append(
            (stream_late + sum_forward(active, down_weight, (1,), (0,))).astype(jnp.bfloat16)
        )
        (
            qkv_weight,
            out_weight,
            query_weight,
            kv_weight,
            cross_weight,
            up_weight,
            down_weight,
            gain_rows,
            bias_rows,
        ) = gathered
        gain_rows = gain_rows.astype(jnp.float32)
        bias_rows = bias_rows.astype(jnp.float32)
        grad_late = out_grad[sample].astype(jnp.float32)
        seen_grad = gather_grads(grad_late.astype(jnp.bfloat16))
        down_grad = jnp.einsum("nf,nd->fd", active, seen_grad, preferred_element_type=jnp.float32)
        active_grad = jnp.einsum(
            "nd,fd->nf", seen_grad, down_weight, preferred_element_type=jnp.float32
        )
        gelu_pull = jax.vjp(partial(jax.nn.gelu, approximate=False), hidden)[1]
        hidden_grad = gelu_pull(active_grad)[0].astype(jnp.bfloat16)
        up_grad = jnp.einsum("nd,nf->df", full_ffn, hidden_grad, preferred_element_type=jnp.float32)
        ffn_grad = sum_backward(hidden_grad, up_weight, (1,), (1,))
        stream_grad, gain_late, bias_late = jax.vjp(
            norm_rows, stream_late, gain_rows[2], bias_rows[2]
        )[1](ffn_grad)
        grad_mid = grad_late + stream_grad
        seen_grad = gather_grads(grad_mid.astype(jnp.bfloat16))
        cross_out_grad = jnp.einsum(
            "ne,nd->ed", cross_attn, seen_grad, preferred_element_type=jnp.float32
        )
        heads_grad = (
            jnp.einsum("nd,ed->ne", seen_grad, cross_weight, preferred_element_type=jnp.float32)
            .astype(jnp.bfloat16)
            .reshape(length, local_heads, HEAD)
        )
        cross_q_grad, text_key_grad, text_value_grad = attend_backward(
            cross_heads, text_keys, text_values, cross_log, heads_grad, False
        )
        cross_flat = cross_q_grad.reshape(length, -1)
        query_grad = jnp.einsum(
            "nd,ne->de", full_cross, cross_flat, preferred_element_type=jnp.float32
        )
        text_pair_grad = jnp.stack(
            (text_key_grad.reshape(text_len, -1), text_value_grad.reshape(text_len, -1)), axis=1
        )
        text_kv_grad = jnp.einsum(
            "td,tce->cde", text_full, text_pair_grad, preferred_element_type=jnp.float32
        )
        text_rows.append(sum_text(text_pair_grad, kv_weight, (1, 2), (0, 2)).astype(jnp.bfloat16))
        cross_grad = sum_backward(cross_flat, query_weight, (1,), (1,))
        stream_grad, gain_mid, bias_mid = jax.vjp(
            norm_rows, stream_mid, gain_rows[1], bias_rows[1]
        )[1](cross_grad)
        grad_in = grad_mid + stream_grad
        seen_grad = gather_grads(grad_in.astype(jnp.bfloat16))
        self_out_grad = jnp.einsum(
            "ne,nd->ed", self_attn, seen_grad, preferred_element_type=jnp.float32
        )
        heads_grad = (
            jnp.einsum("nd,ed->ne", seen_grad, out_weight, preferred_element_type=jnp.float32)
            .astype(jnp.bfloat16)
            .reshape(length, local_heads, HEAD)
        )
        q_grad, k_grad, v_grad = attend_backward(
            query_heads, key_heads, value_heads, self_log, heads_grad, True
        )
        qkv_grad = jnp.stack(
            (q_grad.reshape(length, -1), k_grad.reshape(length, -1), v_grad.reshape(length, -1)),
            axis=1,
        )
        self_qkv_grad = jnp.einsum(
            "nd,nce->cde", full_self, qkv_grad, preferred_element_type=jnp.float32
        )
        self_grad = sum_backward(qkv_grad, qkv_weight, (1, 2), (0, 2))
        stream_grad, gain_in, bias_in = jax.vjp(norm_rows, stream_in, gain_rows[0], bias_rows[0])[
            1
        ](self_grad)
        audio_rows.append((grad_in + stream_grad).astype(jnp.bfloat16))
        grads = (
            self_qkv_grad,
            self_out_grad,
            query_grad,
            text_kv_grad,
            cross_out_grad,
            up_grad,
            down_grad,
            jnp.stack((gain_in, gain_mid, gain_late)),
            jnp.stack((bias_in, bias_mid, bias_late)),
        )
        totals = grads if totals is None else jax.tree.map(jnp.add, totals, grads)
    totals = reduce_grads(totals)
    gain_total, bias_total = lax.psum((totals[7], totals[8]), "tp")
    return (
        jnp.stack(layer_rows),
        jnp.stack(audio_rows),
        jnp.stack(text_rows),
        totals[0],
        totals[1],
        totals[2],
        totals[3],
        totals[4],
        totals[5],
        totals[6],
        gain_total,
        bias_total,
    )


def solution(mesh):
    return jax.shard_map(
        local,
        mesh=mesh,
        in_specs=(
            P("fsdp", "tp", None),
            P("fsdp", "tp", None),
            P("fsdp", "tp", None),
            P(None, "fsdp", "tp"),
            P("tp", "fsdp"),
            P("fsdp", "tp"),
            P(None, "fsdp", "tp"),
            P("tp", "fsdp"),
            P("fsdp", "tp"),
            P("tp", "fsdp"),
            P(None, "fsdp"),
            P(None, "fsdp"),
        ),
        out_specs=(
            P("fsdp", "tp", None),
            P("fsdp", "tp", None),
            P("fsdp", "tp", None),
            P(None, "fsdp", "tp"),
            P("tp", "fsdp"),
            P("fsdp", "tp"),
            P(None, "fsdp", "tp"),
            P("tp", "fsdp"),
            P("fsdp", "tp"),
            P("tp", "fsdp"),
            P(None, "fsdp"),
            P(None, "fsdp"),
        ),
        check_vma=False,
    )
```

profile of v0, /device:TPU:0, one launch (start us, length us, event | category | flops | bytes accessed | tf_op | source)
XLA Modules:
  0.0 2654.3 jit_solution(12395685966072783304)
XLA Ops:
  11.5 27.8 %all-gather.4 = bf16[8,192,3]{1,2,0:T(4,128)(2,1)S(1)} all-gather(bf16[1,192,3]{1,2,0:T(4,128)(2,1)S(1)} %bitcast.501), channel_id=1, replica_groups=mesh['fsdp'=8,'tp'=4] {'fsdp'}, dimensions={0}, use_global_device_ids=true | all-gather | bytes 10368 | tf_op jit(solution)/shard_map/all_gather | solution.py:172
  40.1 26.0 all-gather.5
  70.7 24.5 all-gather.26.cloned.1.call-done
  95.2 67.4 %all-gather.28.cloned.1.call-done = bf16[3,1536,384]{2,1,0:T(8,128)(2,1)} async-done(((bf16[3,192,384]{2,1,0:T(8,128)(2,1)}), bf16[3,1536,384]{2,1,0:T(8,128)(2,1)}) %all-gather.28.cloned.1.call-update) | async-done | bytes 3538960 | tf_op jit(solution)/shard_map/all_gather | solution.py:165
  265.8 28.8 %reduce-scatter.29.cloned.1.call-done = f32[256,1536]{1,0:T(8,128)} async-done(((f32[1024,1536]{1,0:T(8,128)}), f32[256,1536]{1,0:T(8,128)}) %reduce-scatter.29.cloned.1.call-update) | async-done | bytes 1572880 | tf_op jit(solution)/shard_map/reduce_scatter | solution.py:111
  294.6 60.9 %reduce-scatter.35.cloned.1.call-done = f32[256,1536]{1,0:T(8,128)} async-done(((f32[1024,1536]{1,0:T(8,128)}), f32[256,1536]{1,0:T(8,128)}) %reduce-scatter.35.cloned.1.call-update) | async-done | bytes 1572880 | tf_op jit(solution)/shard_map/reduce_scatter | solution.py:111
  367.8 42.0 %all-gather.32.cloned.1.call-done = bf16[2,1536,384]{2,1,0:T(8,128)(2,1)} async-done(((bf16[2,192,384]{2,1,0:T(8,128)(2,1)}), bf16[2,1536,384]{2,1,0:T(8,128)(2,1)}) %all-gather.32.cloned.1.call-update) | async-done | bytes 2359312 | tf_op jit(solution)/shard_map/all_gather | solution.py:168
  412.4 39.3 %all-gather.36.cloned.1.call-done = bf16[1536,384]{1,0:T(8,128)(2,1)} async-done(((bf16[192,384]{1,0:T(8,128)(2,1)}), bf16[1536,384]{1,0:T(8,128)(2,1)}) %all-gather.36.cloned.1.call-update) | async-done | bytes 1179664 | tf_op jit(solution)/shard_map/all_gather | solution.py:167
  451.7 29.5 %all-gather.48.cloned.1.call-done = bf16[1024,1536]{1,0:T(8,128)(2,1)} async-done(((bf16[256,1536]{1,0:T(8,128)(2,1)}), bf16[1024,1536]{1,0:T(8,128)(2,1)}) %all-gather.48.cloned.1.call-update) | async-done | bytes 3145744 | tf_op jit(solution)/shard_map/all_gather | solution.py:103
  487.1 37.1 %all-gather.38.cloned.1.call-done = bf16[384,1536]{0,1:T(8,128)(2,1)} async-done(((bf16[384,192]{0,1:T(8,128)(2,1)}), bf16[384,1536]{0,1:T(8,128)(2,1)}) %all-gather.38.cloned.1.call-update) | async-done | bytes 1179664 | tf_op jit(solution)/shard_map/all_gather | solution.py:169
  566.0 48.5 %reduce-scatter.37.cloned.1.call-done = f32[256,1536]{1,0:T(8,128)} async-done(((f32[1024,1536]{1,0:T(8,128)}), f32[256,1536]{1,0:T(8,128)}) %reduce-scatter.37.cloned.1.call-update) | async-done | bytes 1572880 | tf_op jit(solution)/shard_map/reduce_scatter | solution.py:111
  617.7 57.9 %reduce-scatter.31.cloned.1.call-done = f32[256,1536]{1,0:T(8,128)} async-done(((f32[1024,1536]{1,0:T(8,128)}), f32[256,1536]{1,0:T(8,128)}) %reduce-scatter.31.cloned.1.call-update) | async-done | bytes 1572880 | tf_op jit(solution)/shard_map/reduce_scatter | solution.py:111
  683.4 74.1 %all-gather.42.cloned.1.call-done = bf16[1536,1536]{1,0:T(8,128)(2,1)} async-done(((bf16[192,1536]{1,0:T(8,128)(2,1)}), bf16[1536,1536]{1,0:T(8,128)(2,1)}) %all-gather.42.cloned.1.call-update) | async-done | bytes 4718608 | tf_op jit(solution)/shard_map/all_gather | solution.py:170
  757.6 28.7 %all-gather.50.cloned.1.call-done = bf16[1024,1536]{1,0:T(8,128)(2,1)} async-done(((bf16[256,1536]{1,0:T(8,128)(2,1)}), bf16[1024,1536]{1,0:T(8,128)(2,1)}) %all-gather.50.cloned.1.call-update) | async-done | bytes 3145744 | tf_op jit(solution)/shard_map/all_gather | solution.py:103
  816.8 82.0 %all-gather.44.cloned.1.call-done = bf16[1536,1536]{0,1:T(8,128)(2,1)} async-done(((bf16[1536,192]{0,1:T(8,128)(2,1)}), bf16[1536,1536]{0,1:T(8,128)(2,1)}) %all-gather.44.cloned.1.call-update) | async-done | bytes 4718608 | tf_op jit(solution)/shard_map/all_gather | solution.py:171
  927.5 23.6 multiply_convert_fusion.5
  1018.4 61.1 %reduce-scatter.41.cloned.1.call-done = f32[256,1536]{1,0:T(8,128)} async-done(((f32[1024,1536]{1,0:T(8,128)}), f32[256,1536]{1,0:T(8,128)}) %reduce-scatter.41.cloned.1.call-update) | async-done | bytes 1572880 | tf_op jit(solution)/shard_map/reduce_scatter | solution.py:117
  1083.1 57.3 %reduce-scatter.39.cloned.1.call-done = f32[256,1536]{1,0:T(8,128)} async-done(((f32[1024,1536]{1,0:T(8,128)}), f32[256,1536]{1,0:T(8,128)}) %reduce-scatter.39.cloned.1.call-update) | async-done | bytes 1572880 | tf_op jit(solution)/shard_map/reduce_scatter | solution.py:111
  1140.4 61.1 %reduce-scatter.33.cloned.1.call-done = f32[256,1536]{1,0:T(8,128)} async-done(((f32[1024,1536]{1,0:T(8,128)}), f32[256,1536]{1,0:T(8,128)}) %reduce-scatter.33.cloned.1.call-update) | async-done | bytes 1572880 | tf_op jit(solution)/shard_map/reduce_scatter | solution.py:111
  1208.6 28.5 %all-gather.56.cloned.1.call-done = bf16[1024,1536]{1,0:T(8,128)(2,1)} async-done(((bf16[256,1536]{1,0:T(8,128)(2,1)}), bf16[1024,1536]{1,0:T(8,128)(2,1)}) %all-gather.56.cloned.1.call-update) | async-done | bytes 3145744 | tf_op jit(solution)/shard_map/all_gather | solution.py:107
  1249.2 58.5 %reduce-scatter.49.cloned.1.call-done = f32[256,1536]{1,0:T(8,128)} async-done(((f32[1024,1536]{1,0:T(8,128)}), f32[256,1536]{1,0:T(8,128)}) %reduce-scatter.49.cloned.1.call-update) | async-done | bytes 1572880 | tf_op jit(solution)/shard_map/reduce_scatter | solution.py:117
  1316.1 27.5 %all-gather.52.cloned.1.call-done = bf16[1024,1536]{1,0:T(8,128)(2,1)} async-done(((bf16[256,1536]{1,0:T(8,128)(2,1)}), bf16[1024,1536]{1,0:T(8,128)(2,1)}) %all-gather.52.cloned.1.call-update) | async-done | bytes 3145744 | tf_op jit(solution)/shard_map/all_gather | solution.py:107
  1407.1 28.3 %reduce-scatter.43.cloned.1.call-done = f32[256,1536]{1,0:T(8,128)} async-done(((f32[1024,1536]{1,0:T(8,128)}), f32[256,1536]{1,0:T(8,128)}) %reduce-scatter.43.cloned.1.call-update) | async-done | bytes 1572880 | tf_op jit(solution)/shard_map/reduce_scatter | solution.py:117
  1714.6 119.5 %all-reduce.4.cloned.1.call-done = f32[2,1536,384]{2,0,1:T(2,128)} async-done(((f32[2,1536,384]{2,0,1:T(2,128)}), f32[2,1536,384]{2,0,1:T(2,128)}) %all-reduce.4.cloned.1.call-update) | async-done | bytes 4718608
  1841.8 57.2 %reduce-scatter.69.cloned.1.call-done = f32[192,3]{1,0:T(8,128)} async-done(((f32[1536,3]{1,0:T(8,128)}), f32[192,3]{1,0:T(8,128)}) %reduce-scatter.69.cloned.1.call-update) | async-done | bytes 2320
  1900.0 64.1 %reduce-scatter.71.cloned.1.call-done = f32[192,3]{1,0:T(8,128)} async-done(((f32[1536,3]{1,0:T(8,128)}), f32[192,3]{1,0:T(8,128)}) %reduce-scatter.71.cloned.1.call-update) | async-done | bytes 2320
  1971.3 124.2 %reduce-scatter.67.cloned.1.call-done = f32[192,1152]{1,0:T(8,128)} async-done(((f32[1536,1152]{1,0:T(8,128)}), f32[192,1152]{1,0:T(8,128)}) %reduce-scatter.67.cloned.1.call-update) | async-done | bytes 884752
  2098.0 164.7 %reduce-scatter.63.cloned.1.call-done = f32[192,1536]{1,0:T(8,128)} async-done(((f32[1536,1536]{1,0:T(8,128)}), f32[192,1536]{1,0:T(8,128)}) %reduce-scatter.63.cloned.1.call-update) | async-done | bytes 1179664 | tf_op jit(solution)/shard_map/reduce_scatter | solution.py:138
  2262.7 167.0 %reduce-scatter.65.cloned.1.call-done = f32[1536,192]{0,1:T(8,128)} async-done(((f32[1536,1536]{0,1:T(8,128)}), f32[1536,192]{0,1:T(8,128)}) %reduce-scatter.65.cloned.1.call-update) | async-done | bytes 1179664 | tf_op jit(solution)/shard_map/reduce_scatter | solution.py:139
  2429.7 72.6 %reduce-scatter.61.cloned.1.call-done = f32[384,192]{0,1:T(8,128)} async-done(((f32[384,1536]{0,1:T(8,128)}), f32[384,192]{0,1:T(8,128)}) %reduce-scatter.61.cloned.1.call-update) | async-done | bytes 294928 | tf_op jit(solution)/shard_map/reduce_scatter | solution.py:137
  2502.3 72.6 %reduce-scatter.59.cloned.1.call-done = f32[192,384]{1,0:T(8,128)} async-done(((f32[1536,384]{1,0:T(8,128)}), f32[192,384]{1,0:T(8,128)}) %reduce-scatter.59.cloned.1.call-update) | async-done | bytes 294928 | tf_op jit(solution)/shard_map/reduce_scatter | solution.py:135
  2574.9 72.7 %reduce-scatter.57.cloned.1.call-done = f32[384,192]{0,1:T(8,128)} async-done(((f32[384,1536]{0,1:T(8,128)}), f32[384,192]{0,1:T(8,128)}) %reduce-scatter.57.cloned.1.call-update) | async-done | bytes 294928 | tf_op jit(solution)/shard_map/reduce_scatter | solution.py:134
  (837 shorter events, 700.4 us)
Async XLA Ops:
  70.1 163.7 %all-gather.46.cloned.1.call-start = ((), (), s32[]{:S(2)}) async-start(), calls=%async_computation.35 | async-start | bytes 3932160 | tf_op jit(solution)/shard_map/all_gather | solution.py:103
  70.6 224.0 %reduce-scatter.29.cloned.1.call-start = ((), (), s32[]{:S(2)}) async-start(), calls=%async_computation.25 | async-start | bytes 7864320 | tf_op jit(solution)/shard_map/reduce_scatter | solution.py:111
  210.2 145.3 %reduce-scatter.35.cloned.1.call-start = ((), (), s32[]{:S(2)}) async-start(), calls=%async_computation.36 | async-start | bytes 7864320 | tf_op jit(solution)/shard_map/reduce_scatter | solution.py:111
  264.3 145.6 %all-gather.32.cloned.1.call-start = ((), (), s32[]{:S(2)}) async-start(), calls=%async_computation.26 | async-start | bytes 2654208 | tf_op jit(solution)/shard_map/all_gather | solution.py:168
  265.0 186.6 %all-gather.36.cloned.1.call-start = ((), (), s32[]{:S(2)}) async-start(), calls=%async_computation.28 | async-start | bytes 1327104 | tf_op jit(solution)/shard_map/all_gather | solution.py:167
  265.8 215.4 %all-gather.48.cloned.1.call-start = ((), (), s32[]{:S(2)}) async-start(), calls=%async_computation.37 | async-start | bytes 3932160 | tf_op jit(solution)/shard_map/all_gather | solution.py:103
  360.8 163.5 %all-gather.38.cloned.1.call-start = ((), (), s32[]{:S(2)}) async-start(), calls=%async_computation.29 | async-start | bytes 1327104 | tf_op jit(solution)/shard_map/all_gather | solution.py:169
  361.4 192.5 %all-gather.34.cloned.1.call-start = ((), (), s32[]{:S(2)}) async-start(), calls=%async_computation.27 | async-start | bytes 3932160 | tf_op jit(solution)/shard_map/all_gather | solution.py:103
  362.2 252.4 %reduce-scatter.37.cloned.1.call-start = ((), (), s32[]{:S(2)}) async-start(), calls=%async_computation.38 | async-start | bytes 7864320 | tf_op jit(solution)/shard_map/reduce_scatter | solution.py:111
  530.0 145.6 %reduce-scatter.31.cloned.1.call-start = ((), (), s32[]{:S(2)}) async-start(), calls=%async_computation.30 | async-start | bytes 7864320 | tf_op jit(solution)/shard_map/reduce_scatter | solution.py:111
  565.4 192.2 %all-gather.42.cloned.1.call-start = ((), (), s32[]{:S(2)}) async-start(), calls=%async_computation.32 | async-start | bytes 5308416 | tf_op jit(solution)/shard_map/all_gather | solution.py:170
  565.9 220.3 %all-gather.50.cloned.1.call-start = ((), (), s32[]{:S(2)}) async-start(), calls=%async_computation.39 | async-start | bytes 3932160 | tf_op jit(solution)/shard_map/all_gather | solution.py:103
  681.5 217.3 %all-gather.44.cloned.1.call-start = ((), (), s32[]{:S(2)}) async-start(), calls=%async_computation.33 | async-start | bytes 5308416 | tf_op jit(solution)/shard_map/all_gather | solution.py:171
  682.1 245.4 %all-gather.40.cloned.1.call-start = ((), (), s32[]{:S(2)}) async-start(), calls=%async_computation.31 | async-start | bytes 3932160 | tf_op jit(solution)/shard_map/all_gather | solution.py:103
  682.6 275.0 %all-gather.60.cloned.1.call-start = ((), (), s32[]{:S(2)}) async-start(), calls=%async_computation.58 | async-start | bytes 3932160 | tf_op jit(solution)/shard_map/all_gather | solution.py:107
  683.4 335.0 %reduce-scatter.47.cloned.1.call-start = ((), (), s32[]{:S(2)}) async-start(), calls=%async_computation.46 | async-start | bytes 7864320 | tf_op jit(solution)/shard_map/reduce_scatter | solution.py:117
  919.7 159.7 %reduce-scatter.41.cloned.1.call-start = ((), (), s32[]{:S(2)}) async-start(), calls=%async_computation.41 | async-start | bytes 7864320 | tf_op jit(solution)/shard_map/reduce_scatter | solution.py:117
  981.0 159.4 %reduce-scatter.39.cloned.1.call-start = ((), (), s32[]{:S(2)}) async-start(), calls=%async_computation.40 | async-start | bytes 7864320 | tf_op jit(solution)/shard_map/reduce_scatter | solution.py:111
  990.9 210.7 %reduce-scatter.33.cloned.1.call-start = ((), (), s32[]{:S(2)}) async-start(), calls=%async_computation.34 | async-start | bytes 7864320 | tf_op jit(solution)/shard_map/reduce_scatter | solution.py:111
  1002.1 235.0 %all-gather.56.cloned.1.call-start = ((), (), s32[]{:S(2)}) async-start(), calls=%async_computation.47 | async-start | bytes 3932160 | tf_op jit(solution)/shard_map/all_gather | solution.py:107
  1441.1 165.2 %reduce-scatter.51.cloned.1.call-start = ((), (), s32[]{:S(2)}) async-start(), calls=%async_computation.50 | async-start | bytes 7864320 | tf_op jit(solution)/shard_map/reduce_scatter | solution.py:117
  1557.5 155.6 %reduce-scatter.55.cloned.1.call-start = ((), (), s32[]{:S(2)}) async-start(), calls=%async_computation.52 | async-start | bytes 245760 | tf_op jit(solution)/shard_map/reduce_scatter | solution.py:123
  1569.4 143.8 %reduce-scatter.53.cloned.1.call-start = ((), (), s32[]{:S(2)}) async-start(), calls=%async_computation.51 | async-start | bytes 245760 | tf_op jit(solution)/shard_map/reduce_scatter | solution.py:123
  1582.2 252.0 %all-reduce.4.cloned.1.call-start = ((), (), s32[]{:S(2)}) async-start(), calls=%async_computation.63 | async-start | bytes 9437184
  1595.8 303.2 %reduce-scatter.69.cloned.1.call-start = ((), (), s32[]{:S(2)}) async-start(), calls=%async_computation.61 | async-start | bytes 884736
  1621.8 342.3 %reduce-scatter.71.cloned.1.call-start = ((), (), s32[]{:S(2)}) async-start(), calls=%async_computation.62 | async-start | bytes 884736
  1623.1 472.5 %reduce-scatter.67.cloned.1.call-start = ((), (), s32[]{:S(2)}) async-start(), calls=%async_computation.60 | async-start | bytes 7962624
  1652.5 610.2 %reduce-scatter.63.cloned.1.call-start = ((), (), s32[]{:S(2)}) async-start(), calls=%async_computation.56 | async-start | bytes 10616832 | tf_op jit(solution)/shard_map/reduce_scatter | solution.py:138
  1669.1 760.6 %reduce-scatter.65.cloned.1.call-start = ((), (), s32[]{:S(2)}) async-start(), calls=%async_computation.57 | async-start | bytes 10616832 | tf_op jit(solution)/shard_map/reduce_scatter | solution.py:139
  1685.8 816.6 %reduce-scatter.61.cloned.1.call-start = ((), (), s32[]{:S(2)}) async-start(), calls=%async_computation.55 | async-start | bytes 2654208 | tf_op jit(solution)/shard_map/reduce_scatter | solution.py:137
  1694.1 880.8 %reduce-scatter.59.cloned.1.call-start = ((), (), s32[]{:S(2)}) async-start(), calls=%async_computation.54 | async-start | bytes 2654208 | tf_op jit(solution)/shard_map/reduce_scatter | solution.py:135
  1701.9 945.6 %reduce-scatter.57.cloned.1.call-start = ((), (), s32[]{:S(2)}) async-start(), calls=%async_computation.53 | async-start | bytes 2654208 | tf_op jit(solution)/shard_map/reduce_scatter | solution.py:134
  (259 other events, 6206.5 us)
Sparse Core Ops, SparseCore 0:
  97.4 65.1 all-gather.27
  164.8 39.5 all-gather.29
  236.1 58.4 reduce-scatter.28
  297.1 58.3 reduce-scatter.34
  357.7 52.1 all-gather.31
  412.0 39.5 all-gather.35
  483.2 41.0 all-gather.37
  556.3 58.2 reduce-scatter.36
  617.2 58.3 reduce-scatter.30
  677.6 79.9 all-gather.41
  788.3 28.5 all-gather.61
  818.9 79.8 all-gather.43
  960.0 58.3 reduce-scatter.46
  1021.1 58.3 reduce-scatter.40
  1082.0 58.3 reduce-scatter.38
  1143.1 58.3 reduce-scatter.32
  1249.2 58.3 reduce-scatter.48
  1315.0 28.5 all-gather.51
  1345.7 28.5 all-gather.57
  1376.9 58.3 reduce-scatter.42
  1441.2 28.5 all-gather.53
  1484.5 58.5 reduce-scatter.50
  1557.6 58.3 reduce-scatter.44
  1664.5 169.6 all-reduce.3
  1837.4 61.5 reduce-scatter.68
  1902.5 61.4 reduce-scatter.70
  1967.6 127.9 reduce-scatter.66
  2100.2 162.4 reduce-scatter.62
  2267.1 162.5 reduce-scatter.64
  2434.2 68.0 reduce-scatter.60
  2506.8 68.0 reduce-scatter.58
  2579.4 68.1 reduce-scatter.56
  (10 shorter events, 257.8 us)
where the time goes:
time: 2660 us; the launch traced here: 2650 us
  waiting for transfers between devices  1980 us (74%)
  matrix products  400 us (15%)
  other arithmetic  95.3 us (4%)
  local copies, waits for them, and re-layouts  80 us (3%)
  blocking collectives  72.1 us (3%)
    unnamed x46, waiting for transfers between devices  373 us
    reduce_scatter x6, waiting for transfers between devices, sum_forward(): lax.psum_scatter(row_product(left_rows, weight, left_dims, right_dims), '...  315 us
    reduce_scatter x6, waiting for transfers between devices, sum_backward(): lax.psum_scatter(row_product(left_rows, weight, left_dims, right_dims), '...  173 us
    reduce_scatter x1, waiting for transfers between devices, reduce_grads(): lax.psum_scatter(parts[6], 'fsdp', scatter_dimension=1, tiled=True)  167 us
    reduce_scatter x1, waiting for transfers between devices, reduce_grads(): lax.psum_scatter(parts[5], 'fsdp', scatter_dimension=0, tiled=True)  165 us
    all_gather x6, waiting for transfers between devices, gather_rows(): return lax.all_gather(values, 'tp', axis=0, tiled=True)  128 us
    dot_general x14, matrix products, row_product(): lax.dot_general(left_rows, weight, ((left_dims, right_dims), ((), ())), p...  88.8 us
    all_gather x6, waiting for transfers between devices, gather_grads(): return lax.all_gather(values, 'tp', axis=0, tiled=True)  87 us
  transfers between devices with their start and end apart: 42, of which 38 were waited for; matrix products, arithmetic and copies ran while one was open for 19% of the time, Pallas kernels for 0%

commit v1 on v0

v1 whole, which is shorter than its diff:
```python
import functools
import math

import jax
import jax.numpy as jnp
from jax import lax
from jax.experimental import pallas as pl
from jax.experimental.pallas import tpu as pltpu
from jax.sharding import PartitionSpec as P

HEAD = 64
PAIR = 2 * HEAD
EPSILON = 1e-05
F32 = jnp.float32
BF16 = jnp.bfloat16
RATE = HEAD ** (-0.5) * math.log2(math.e)
TOKEN = (8, 128)
COST = 1000
VMEM = 44 * 2**20


def swap_chip(values):
    return lax.ppermute(values, "tp", [(t, t ^ 2) for t in range(4)])


def swap_core(values):
    return lax.ppermute(values, "tp", [(t, t ^ 1) for t in range(4)])


def place_of(share, t):
    apart = share ^ t
    return ((apart & 1) << 1) | (apart >> 1)


def gather_rows(values, swapped):
    pair = jnp.concatenate((values, swapped), axis=0)
    return pair, swap_core(pair)


def ring_of(n):
    return list(range(0, n, 2)) + list(range(n - 1, 0, -2))


def ring_place(n):
    i = lax.axis_index("fsdp")
    return jnp.where(i % 2 == 0, i // 2, n - (i + 1) // 2)


def ring_index(n, place):
    place = lax.rem(place + 2 * n, n)
    return jnp.where(place < n // 2, 2 * place, 2 * (n - place) - 1)


def send_next(values, n):
    ring = ring_of(n)
    return lax.ppermute(values, "fsdp", [(ring[k], ring[(k + 1) % n]) for k in range(n)])


def send_prev(values, n):
    ring = ring_of(n)
    return lax.ppermute(values, "fsdp", [(ring[(k + 1) % n], ring[k]) for k in range(n)])


def ring_table(n):
    return ring_index(n, ring_place(n) + jnp.arange(-(n // 2), n // 2 + 1)).astype(jnp.int32)


def place_pieces_body(n, rows, places, *refs):
    pieces, whole = refs[:-1], refs[-1]
    for piece, (step, offset) in zip(pieces, places):
        begin = ring_index(n, ring_place(n) + step) * rows + offset
        size = piece.shape[0]
        whole[pl.ds(pl.multiple_of(begin, math.gcd(rows, size)), size), :] = piece[...]


class RingGather:
    def __init__(self, shard, n):
        self.n, self.shard, self.got = n, shard, []
        self.direct = n > 16 or n % 2

    def step(self):
        if self.direct:
            return ()
        up, down = self.got[-1] if self.got else (self.shard, self.shard)
        if len(self.got) == self.n // 2 - 1:
            half = self.shard.shape[0] // 2
            up, down = up[:half], down[half:]
        self.got.append((send_next(up, self.n), send_prev(down, self.n)))
        return self.got[-1]

    def turn(self, values=(), *wait):
        if self.direct:
            return tick(list(values), *wait) if values else []
        pair = self.got[-1]
        passed = tick([*pair, *values], *wait)
        self.got[-1] = tuple(passed[:2])
        self.step()
        return passed[2:]

    def whole(self, wait=()):
        if self.direct:
            return lax.all_gather(self.shard, "fsdp", axis=0, tiled=True)
        rows, cols = self.shard.shape
        pieces, places = [self.shard], [(0, 0)]
        for k, pair in enumerate(self.got, 1):
            pieces += pair
            places += [(-k, 0), (k, 0 if k < self.n // 2 else rows // 2)]
        size = 768 if cols % 768 == 0 else cols
        return call(
            functools.partial(place_pieces_body, self.n, rows, places),
            (cols // size,),
            pieces,
            [pl.BlockSpec((v.shape[0], size), lambda i: (0, i)) for v in pieces],
            [((self.n * rows, cols), self.shard.dtype)],
            [pl.BlockSpec((self.n * rows, size), lambda i: (0, i))],
                wait=wait,
        )[0]


def ring_body(kind, rows, count, sides, *refs):
    table, wholes = refs[0], refs[1 : 1 + count]
    came = refs[1 + count : -len(sides) - count - 1]
    outs, own, sems = refs[-len(sides) - count - 1 : -count - 1], refs[-count - 1 : -1], refs[-1]
    copies = []
    for side, (entry, first, last) in enumerate(sides):
        begin = pl.multiple_of(table[entry] * rows + first, rows // 2)
        for k in range(count):
            source = wholes[k].at[pl.ds(begin, last - first), :]
            to = own[k].at[side, pl.ds(0, last - first), :]
            copies.append(pltpu.make_async_copy(source, to, sems.at[side, k]))
    for copy in copies:
        copy.start()
    for copy in copies:
        copy.wait()
    half = rows // 2
    for side, (_, first, last) in enumerate(sides):
        begin = 0
        for k in range(count):
            cols = slice(begin, begin + wholes[k].shape[1])
            begin = cols.stop
            mine = own[k][side, : last - first, :]
            if kind == "begin":
                outs[side][:, cols] = mine
            elif kind == "first":
                add = came[side][:, cols].astype(F32)
                here = slice(side * half, (side + 1) * half)
                there = slice((1 - side) * half, (2 - side) * half)
                outs[side][here, cols] = (mine[here].astype(F32) + add).astype(BF16)
                outs[side][there, cols] = mine[there]
            elif kind == "middle":
                add = came[side][:, cols].astype(F32)
                outs[side][:, cols] = (mine.astype(F32) + add).astype(BF16)
            else:
                add = came[0][:, cols].astype(F32) + came[1][:, cols].astype(F32)
                outs[side][:, cols] = mine.astype(F32) + add


class RingSum:
    def __init__(self, wholes, n, table):
        self.wholes, self.n, self.table = wholes, n, table
        self.direct = n > 16 or n % 2
        self.left = n // 2
        self.came = ()
        self.step()

    def run(self, kind, step, wait=()):
        rows = self.wholes[0].shape[0] // self.n
        half = rows // 2
        widths = [v.shape[1] for v in self.wholes]
        middle = self.n // 2
        if kind == "end":
            sides = [(middle, 0, rows)]
        elif kind == "begin":
            sides = [(middle + step, 0, half), (middle - step, half, rows)]
        else:
            sides = [(middle + step, 0, rows), (middle - step, 0, rows)]
        size = half if kind == "begin" else rows
        out = ((size, sum(widths)), F32 if kind == "end" else BF16)
        hbm = pl.BlockSpec(memory_space=pltpu.HBM)
        return call(
            functools.partial(ring_body, kind, rows, len(widths), sides),
            (1,),
            (self.table, *self.wholes, *self.came),
            [pl.BlockSpec(memory_space=pltpu.SMEM)]
            + [hbm] * len(widths)
            + [whole_spec(v.shape) for v in self.came],
            [out] * len(sides),
            [whole_spec(out[0])] * len(sides),
            [pltpu.VMEM((len(sides), rows, cols), BF16) for cols in widths]
            + [pltpu.SemaphoreType.DMA((len(sides), len(widths)))],
            wait=wait,
        )

    def step(self, wait=()):
        if self.direct or not self.left:
            return
        if self.left == self.n // 2:
            kind = "begin"
        else:
            kind = "first" if self.left == self.n // 2 - 1 else "middle"
        up, down = self.run(kind, self.left, wait)
        self.came = (send_next(up, self.n), send_prev(down, self.n))
        self.left -= 1

    def total(self):
        if self.direct:
            whole = jnp.concatenate(self.wholes, 1)
            return lax.psum_scatter(whole, "fsdp", scatter_dimension=0, tiled=True).astype(F32)
        while self.left:
            self.step()
        return self.run("end", 0)[0]


def swap_fsdp(values, n, bit):
    return lax.ppermute(values, "fsdp", [(i, i ^ bit) for i in range(n)])


def small_gather(shard, n):
    if n & (n - 1):
        return lax.all_gather(shard, "fsdp", axis=1, tiled=True)
    found = shard[None]
    bit = 1
    while bit < n:
        found = jnp.concatenate((found, swap_fsdp(found, n, bit)), axis=0)
        bit *= 2
    found = jnp.take(found, jnp.arange(n) ^ lax.axis_index("fsdp"), axis=0)
    return found.transpose(1, 0, 2).reshape(shard.shape[0], -1)


def times(rows, weight):
    return jnp.dot(rows, weight, preferred_element_type=F32)


def times_t(rows, weight):
    return lax.dot_general(rows, weight, (((1,), (1,)), ((), ())), preferred_element_type=F32)


def t_times(left, right):
    return lax.dot_general(left, right, (((0,), (0,)), ((), ())), preferred_element_type=F32)


def whole_spec(shape):
    return pl.BlockSpec(shape, lambda *_: (0,) * len(shape))


class Order:
    token = None


def call(body, grid, ins, in_specs, outs, out_specs, scratch=(), wait=(), alias=None):
    count = len(ins)
    extra = list(wait) + ([Order.token] if Order.token is not None else [])
    any_spec, hbm = (pl.BlockSpec(memory_space=space) for space in (pl.ANY, pltpu.HBM))

    def run(*refs):
        after = refs[count + len(extra) :]
        body(*refs[:count], *after[: len(outs)], *after[len(outs) + 1 :])
        after[len(outs)][...] = jnp.zeros(TOKEN, F32)

    results = pl.pallas_call(
        run,
        grid=grid,
        in_specs=list(in_specs) + [hbm] * len(wait) + [any_spec] * (len(extra) - len(wait)),
        out_specs=list(out_specs) + [whole_spec(TOKEN)],
        scratch_shapes=list(scratch),
        out_shape=[jax.ShapeDtypeStruct(s, d) for s, d in list(outs) + [(TOKEN, F32)]],
        input_output_aliases=alias or {},
        compiler_params=pltpu.CompilerParams(vmem_limit_bytes=VMEM),
        name=getattr(body, "func", body).__name__,
        cost_estimate=pl.CostEstimate(flops=COST, bytes_accessed=0, transcendentals=0),
    )(*ins, *extra)
    Order.token = results[-1]
    return results[:-1]


def head_masks(rows):
    low = lax.broadcasted_iota(jnp.int32, (rows, PAIR), 1) < HEAD
    return low, jnp.logical_not(low)


def split_heads(block, masks):
    zero = jnp.zeros_like(block)
    return [jnp.where(m, block, zero) for m in masks]


def rows_call(body, ins, outs, sums=(), wait=(), shifts=None):
    rows = outs[0][0][0]
    block = next((v for v in (128, 96) if rows % v == 0), rows)
    steps = rows // block
    shifts = shifts or [0] * len(ins)
    in_specs = []
    for v, shift in zip(ins, shifts):
        if shift is None:
            in_specs.append(whole_spec(v.shape))
        else:
            first = shift // block
            in_specs.append(
                pl.BlockSpec((block, v.shape[1]), functools.partial(lambda f, i: (i + f, 0), first))
            )
    out_specs = [pl.BlockSpec((block, shape[1]), lambda i: (i, 0)) for shape, _ in outs]
    out_specs += [whole_spec(shape) for shape, _ in sums]
    return call(
        body, (steps,), ins, in_specs, list(outs) + list(sums), out_specs, wait=wait
    )


def tick_body(*refs):
    pass


def tick(values, *wait):
    spec = pl.BlockSpec(memory_space=pl.ANY)
    count = len(values)
    return call(
        tick_body,
        (1,),
        values,
        [spec] * count,
        [(v.shape, v.dtype) for v in values],
        [spec] * count,
        wait=wait,
        alias={k: k for k in range(count)},
    )


def copy_body(from_ref, to_ref):
    to_ref[...] = from_ref[...]


def hold(values, wait=()):
    return rows_call(copy_body, (values,), [(values.shape, values.dtype)], wait=wait)[0]


def add_body(keep_ref, seen_ref, out_ref):
    out_ref[...] = (keep_ref[...] + seen_ref[...].astype(F32)).astype(BF16)


def sum_over_tp(keep, send, wait=()):
    seen = swap_core(send)
    half = keep.shape[0] // 2
    (passed,) = rows_call(
        add_body, (keep, seen), [((half, keep.shape[1]), BF16)], shifts=(half, half), wait=wait
    )
    return keep, seen, swap_chip(passed)


def total_of(refs):
    return sum(ref[...].astype(F32) for ref in refs)


def norm_forward_body(index, *refs):
    params, outs = refs[-3], refs[-2:]
    stream = total_of(refs[:-3])
    outs[0][...] = stream
    center = stream - jnp.mean(stream, axis=-1, keepdims=True)
    spread = jnp.mean(center * center, axis=-1, keepdims=True)
    gain, bias = params[index : index + 1, :], params[3 + index : 4 + index, :]
    outs[1][...] = (center * lax.rsqrt(spread + EPSILON) * gain + bias).astype(BF16)


def norm_forward(index, terms, params, rows, wait=()):
    shape = (rows, params.shape[1])
    return rows_call(
        functools.partial(norm_forward_body, index),
        (*terms, params),
        [(shape, F32), (shape, BF16)],
        shifts=[0] * len(terms) + [None],
        wait=wait,
    )


def norm_backward_body(index, count, *refs):
    stream_ref, base_ref, terms = refs[0], refs[1], refs[2 : 2 + count]
    params, outs, sums = refs[2 + count], refs[3 + count : -1], refs[-1]
    stream = stream_ref[...].astype(F32)
    center = stream - jnp.mean(stream, axis=-1, keepdims=True)
    scale = lax.rsqrt(jnp.mean(center * center, axis=-1, keepdims=True) + EPSILON)
    xhat = center * scale
    grad = total_of(terms)
    e = grad * params[index : index + 1, :]
    back = scale * (
        e - jnp.mean(e, axis=-1, keepdims=True) - xhat * jnp.mean(e * xhat, axis=-1, keepdims=True)
    )
    total = base_ref[...].astype(F32) + back
    for out in outs:
        out[...] = total.astype(out.dtype)

    @pl.when(pl.program_id(0) == 0)
    def _():
        sums[...] = jnp.zeros_like(sums)

    sums[0:1, :] += jnp.sum(grad * xhat, axis=0, keepdims=True)
    sums[1:2, :] += jnp.sum(grad, axis=0, keepdims=True)


def norm_backward(index, stream, base, terms, params, kinds):
    shape = stream.shape
    return rows_call(
        functools.partial(norm_backward_body, index, len(terms)),
        (stream, base, *terms, params),
        [(shape, kind) for kind in kinds],
        [((8, shape[1]), F32)],
        shifts=[0] * (2 + len(terms)) + [None],
    )


def sum_pair_body(left_ref, right_ref, out_ref):
    out_ref[...] = left_ref[...] + right_ref[...]


class SmallSum:
    def __init__(self, whole, n):
        self.whole, self.n = whole, n
        self.swaps = [swap_core, swap_chip]
        if n & (n - 1):
            self.whole = lax.psum(whole, "fsdp")
        else:
            bits = [2**k for k in range(n.bit_length() - 1)]
            self.swaps += [functools.partial(swap_fsdp, n=n, bit=bit) for bit in bits]
        self.came = self.swaps.pop(0)(self.whole)

    def step(self):
        if self.came is None:
            return
        shape = self.whole.shape
        (self.whole,) = call(
            sum_pair_body,
            (1,),
            (self.whole, self.came),
            [whole_spec(shape)] * 2,
            [(shape, F32)],
            [whole_spec(shape)],
        )
        self.came = self.swaps.pop(0)(self.whole) if self.swaps else None

    def total(self):
        while self.came is not None:
            self.step()
        cols = self.whole.shape[1] // self.n
        begin = lax.axis_index("fsdp") * cols
        return lax.dynamic_slice(self.whole, (0, begin), (self.whole.shape[0], cols))


def join_body(count, *refs):
    outs = refs[count]
    for k in range(count):
        outs[k] = refs[k][...]


def join(parts):
    shape, kind = parts[0].shape, parts[0].dtype
    block = 128 if shape[0] % 128 == 0 else shape[0]
    return call(
        functools.partial(join_body, len(parts)),
        (shape[0] // block,),
        parts,
        [pl.BlockSpec((block, shape[1]), lambda i: (i, 0))] * len(parts),
        [((len(parts), *shape), kind)],
        [pl.BlockSpec((len(parts), block, shape[1]), lambda i: (0, i, 0))],
    )[0]


def sum_terms_body(*refs):
    refs[-1][...] = total_of(refs[:-1]).astype(BF16)


def sum_terms(terms, shape):
    return rows_call(sum_terms_body, terms, [(shape, BF16)])[0]


def self_forward_body(
    a_ref, b_ref, w_ref, wo_ref, qkv_ref, attn_ref, lse_ref, keep_ref, send_ref, vt_ref
):
    step = pl.program_id(0)
    t = lax.axis_index("tp")
    half = a_ref.shape[0]
    share = half // 2
    qkv_ref[:half, :] = times(a_ref[...], w_ref[...]).astype(BF16)
    qkv_ref[half:, :] = times(b_ref[...], w_ref[...]).astype(BF16)
    vt_ref[...] = qkv_ref[:, 2 * PAIR :].T
    masks = head_masks(share)
    at = [pl.ds(pl.multiple_of(place_of(g, t) * share, share), share) for g in range(4)]
    seen = lax.broadcasted_iota(jnp.int32, (share, share), 0) <= lax.broadcasted_iota(
        jnp.int32, (share, share), 1
    )
    lanes = pl.ds(pl.multiple_of(step * PAIR, PAIR), PAIR)
    for g in range(4):
        queries = split_heads(qkv_ref[at[g], :PAIR], masks)
        found = []
        for e in range(2):
            scores = []
            for b in range(g + 1):
                s = times_t(qkv_ref[at[b], PAIR : 2 * PAIR], queries[e])
                scores.append(jnp.where(seen, s, -1e30) if b == g else s)
            peak = functools.reduce(
                jnp.maximum, [jnp.max(s, axis=0, keepdims=True) for s in scores]
            )
            peak = peak * RATE
            probs = [jnp.exp2(s * RATE - peak) for s in scores]
            total = sum(jnp.sum(p, axis=0, keepdims=True) for p in probs)
            rows = slice(e * HEAD, (e + 1) * HEAD)
            mixed = sum(times(vt_ref[rows, at[b]], probs[b].astype(BF16)) for b in range(g + 1))
            found.append(mixed / total)
            lse_ref[e : e + 1, at[g]] = peak + jnp.log2(total)
        attn_ref[at[g], lanes] = jnp.concatenate(found, 0).T.astype(BF16)

    @pl.when(step == pl.num_programs(0) - 1)
    def _():
        for k in range(2):
            rows = slice(k * share, (k + 1) * share)
            keep_ref[rows, :] = times_t(attn_ref[rows, :], wo_ref[...])
            late = slice(half + k * share, half + (k + 1) * share)
            send_ref[rows, :] = times_t(attn_ref[late, :], wo_ref[...]).astype(BF16)


def self_forward(a, b, weight, units):
    half, width = a.shape
    pairs = units // PAIR
    rows = 2 * half
    return call(
        self_forward_body,
        (pairs,),
        (a, b, weight, weight),
        [
            whole_spec((half, width)),
            whole_spec((half, width)),
            pl.BlockSpec((width, 3 * PAIR), lambda h: (0, h)),
            pl.BlockSpec((width, units), lambda h: (0, 3)),
        ],
        [
            ((rows, 3 * units), BF16),
            ((rows, units), BF16),
            ((8 * pairs, rows), F32),
            ((half, width), F32),
            ((half, width), BF16),
        ],
        [
            pl.BlockSpec((rows, 3 * PAIR), lambda h: (0, h)),
            whole_spec((rows, units)),
            pl.BlockSpec((8, rows), lambda h: (h, 0)),
            whole_spec((half, width)),
            whole_spec((half, width)),
        ],
        [pltpu.VMEM((PAIR, rows), BF16)],
    )


def self_backward_body(
    a_ref, b_ref, wo_ref, w_ref, qkv_ref, attn_ref, lse_ref,
    grads_ref, keep_ref, send_ref, hg_ref, kt_ref, dk_ref, dv_ref,
):
    step = pl.program_id(0)
    t = lax.axis_index("tp")
    half = a_ref.shape[0]
    share = half // 2
    hg_ref[:half, :] = times(a_ref[...], wo_ref[...]).astype(BF16)
    hg_ref[half:, :] = times(b_ref[...], wo_ref[...]).astype(BF16)
    kt_ref[...] = qkv_ref[:, PAIR : 2 * PAIR].T
    dk_ref[...] = jnp.zeros_like(dk_ref)
    dv_ref[...] = jnp.zeros_like(dv_ref)
    masks = head_masks(share)
    at = [pl.ds(pl.multiple_of(place_of(g, t) * share, share), share) for g in range(4)]
    seen = lax.broadcasted_iota(jnp.int32, (share, share), 0) <= lax.broadcasted_iota(
        jnp.int32, (share, share), 1
    )
    base = step * 3 * PAIR
    lanes = [pl.ds(pl.multiple_of(base + c * PAIR, PAIR), PAIR) for c in range(3)]
    for g in range(4):
        queries = split_heads(qkv_ref[at[g], :PAIR], masks)
        block = hg_ref[at[g], :]
        outer = split_heads(block, masks)
        inner = (block.astype(F32) * attn_ref[at[g], :].astype(F32)).T
        query_grad = []
        for e in range(2):
            rows = slice(e * HEAD, (e + 1) * HEAD)
            lse = lse_ref[e : e + 1, at[g]]
            delta = jnp.sum(inner[rows], axis=0, keepdims=True)
            total = jnp.zeros((HEAD, share), F32)
            for b in range(g + 1):
                s = times_t(qkv_ref[at[b], PAIR : 2 * PAIR], queries[e])
                probs = jnp.exp2(s * RATE - lse)
                if b == g:
                    probs = jnp.where(seen, probs, 0.0)
                grad = times_t(qkv_ref[at[b], 2 * PAIR :], outer[e])
                score_grad = (probs * (grad - delta)).astype(BF16)
                dv_ref[at[b], :] += times(probs.astype(BF16), outer[e])
                dk_ref[at[b], :] += times(score_grad, queries[e])
                total += times(kt_ref[rows, at[b]], score_grad)
            query_grad.append(total)
        query_grad = jnp.concatenate(query_grad, 0) * (HEAD ** (-0.5))
        grads_ref[at[g], lanes[0]] = query_grad.T.astype(BF16)
    grads_ref[:, lanes[1]] = (dk_ref[...] * (HEAD ** (-0.5))).astype(BF16)
    grads_ref[:, lanes[2]] = dv_ref[...].astype(BF16)

    @pl.when(step == pl.num_programs(0) - 1)
    def _():
        for k in range(2):
            rows = slice(k * share, (k + 1) * share)
            keep_ref[rows, :] = times_t(grads_ref[rows, :], w_ref[...])
            late = slice(half + k * share, half + (k + 1) * share)
            send_ref[rows, :] = times_t(grads_ref[late, :], w_ref[...]).astype(BF16)


def self_backward(a, b, weight, qkv, attn, lse):
    half, width = a.shape
    units = attn.shape[1]
    pairs = units // PAIR
    rows = 2 * half
    return call(
        self_backward_body,
        (pairs,),
        (a, b, weight, weight, qkv, attn, lse),
        [
            whole_spec((half, width)),
            whole_spec((half, width)),
            pl.BlockSpec((width, PAIR), lambda h: (0, 3 * pairs + h)),
            whole_spec((width, 3 * units)),
            pl.BlockSpec((rows, 3 * PAIR), lambda h: (0, h)),
            pl.BlockSpec((rows, PAIR), lambda h: (0, h)),
            pl.BlockSpec((8, rows), lambda h: (h, 0)),
        ],
        [
            ((rows, 3 * units), BF16),
            ((half, width), F32),
            ((half, width), BF16),
        ],
        [
            whole_spec((rows, 3 * units)),
            whole_spec((half, width)),
            whole_spec((half, width)),
        ],
        [
            pltpu.VMEM((rows, PAIR), BF16),
            pltpu.VMEM((PAIR, rows), BF16),
            pltpu.VMEM((rows, PAIR), F32),
            pltpu.VMEM((rows, PAIR), F32),
        ],
    )


def cross_weight_specs(width, units):
    return [pl.BlockSpec((width, units), functools.partial(lambda j, _: (0, j), j)) for j in (0, 2, 1, 3)]


def cross_probs(keys, queries):
    s = times_t(keys, queries)
    peak = jnp.max(s, axis=0, keepdims=True) * RATE
    probs = jnp.exp2(s * RATE - peak)
    return probs / jnp.sum(probs, axis=0, keepdims=True)


def cross_forward_body(
    a_ref, b_ref, wq0_ref, wq1_ref, wo0_ref, wo1_ref, kv0_ref, kv1_ref,
    q_ref, attn_ref, keep_ref, send_ref,
):
    share = a_ref.shape[0]
    units = wq0_ref.shape[1]
    masks = head_masks(kv0_ref.shape[0])
    keep = send = 0.0
    for j, (wq_ref, wo_ref, kv_ref) in enumerate(
        ((wq0_ref, wo0_ref, kv0_ref), (wq1_ref, wo1_ref, kv1_ref))
    ):
        cols = slice(j * units, (j + 1) * units)
        q_ref[:share, cols] = times(a_ref[...], wq_ref[...]).astype(BF16)
        q_ref[share:, cols] = times(b_ref[...], wq_ref[...]).astype(BF16)
        for begin in range(0, units, PAIR):
            lanes = slice(j * units + begin, j * units + begin + PAIR)
            queries = q_ref[:, lanes]
            keys = split_heads(kv_ref[:, begin : begin + PAIR], masks)
            values = kv_ref[:, units + begin : units + begin + PAIR].T
            mixed = [
                times(
                    values[e * HEAD : (e + 1) * HEAD],
                    cross_probs(keys[e], queries).astype(BF16),
                )
                for e in range(2)
            ]
            attn_ref[:, lanes] = jnp.concatenate(mixed, 0).T.astype(BF16)
        keep += times_t(attn_ref[:share, cols], wo_ref[...])
        send += times_t(attn_ref[share:, cols], wo_ref[...])
    keep_ref[...] = keep
    send_ref[...] = send.astype(BF16)


def cross_forward(a, b, weight, kvs):
    share, width = a.shape
    units = weight.shape[1] // 6
    ins = (a, b, *[weight] * 4, *kvs)
    outs = [
        ((2 * share, 2 * units), BF16),
        ((2 * share, 2 * units), BF16),
        ((share, width), F32),
        ((share, width), BF16),
    ]
    return call(
        cross_forward_body,
        (1,),
        ins,
        [whole_spec(v.shape) for v in ins[:2]]
        + cross_weight_specs(width, units)
        + [whole_spec(v.shape) for v in ins[6:]],
        outs,
        [whole_spec(s) for s, _ in outs],
    )


def cross_backward_body(
    a_ref, b_ref, wq0_ref, wq1_ref, wo0_ref, wo1_ref, kv0_ref, kv1_ref, q_ref,
    dq_ref, own_ref, other_ref, keep_ref, send_ref, hg_ref,
):
    share = a_ref.shape[0]
    units = wq0_ref.shape[1]
    text = kv0_ref.shape[0]
    masks = head_masks(text)
    keep = send = 0.0
    for j, (wq_ref, wo_ref, kv_ref, out_ref) in enumerate(
        ((wq0_ref, wo0_ref, kv0_ref, own_ref), (wq1_ref, wo1_ref, kv1_ref, other_ref))
    ):
        cols = slice(j * units, (j + 1) * units)
        hg_ref[:share, :] = times(a_ref[...], wo_ref[...]).astype(BF16)
        hg_ref[share:, :] = times(b_ref[...], wo_ref[...]).astype(BF16)
        for begin in range(0, units, PAIR):
            lanes = slice(j * units + begin, j * units + begin + PAIR)
            local = slice(begin, begin + PAIR)
            queries = q_ref[:, lanes]
            outer = hg_ref[:, local]
            pair_keys = kv_ref[:, local]
            keys = split_heads(pair_keys, masks)
            values = split_heads(kv_ref[:, units + begin : units + begin + PAIR], masks)
            keys_t = pair_keys.T
            query_grad, key_grad, value_grad = [], [], []
            for e in range(2):
                probs = cross_probs(keys[e], queries)
                grad = times_t(values[e], outer)
                inner = jnp.sum(probs * grad, axis=0, keepdims=True)
                score_grad = (probs * (grad - inner)).astype(BF16)
                query_grad.append(times(keys_t[e * HEAD : (e + 1) * HEAD], score_grad))
                key_grad.append(times(score_grad, queries))
                value_grad.append(times(probs.astype(BF16), outer))
            query_grad = jnp.concatenate(query_grad, 0) * (HEAD ** (-0.5))
            dq_ref[:, lanes] = query_grad.T.astype(BF16)
            key_grad = jnp.where(masks[0], *key_grad) * (HEAD ** (-0.5))
            value_grad = jnp.where(masks[0], *value_grad)
            out_ref[:, local] = key_grad.astype(out_ref.dtype)
            out_ref[:, units + begin : units + begin + PAIR] = value_grad.astype(out_ref.dtype)
        keep += times_t(dq_ref[:share, cols], wq_ref[...])
        send += times_t(dq_ref[share:, cols], wq_ref[...])
    keep_ref[...] = keep
    send_ref[...] = send.astype(BF16)


def cross_backward(a, b, weight, kvs, queries):
    share, width = a.shape
    units = weight.shape[1] // 6
    text = kvs[0].shape[0]
    ins = (a, b, *[weight] * 4, *kvs, queries)
    outs = [
        ((2 * share, 2 * units), BF16),
        ((text, 2 * units), F32),
        ((text, 2 * units), BF16),
        ((share, width), F32),
        ((share, width), BF16),
    ]
    return call(
        cross_backward_body,
        (1,),
        ins,
        [whole_spec(v.shape) for v in ins[:2]]
        + cross_weight_specs(width, units)
        + [whole_spec(v.shape) for v in ins[6:]],
        outs,
        [whole_spec(s) for s, _ in outs],
        [pltpu.VMEM((2 * share, units), BF16)],
    )


def gelu_pair(hidden):
    phi = 0.5 * (1.0 + lax.erf(hidden * (0.5**0.5)))
    density = jnp.exp(-0.5 * hidden * hidden) * 0.3989422804014327
    return hidden * phi, phi + hidden * density


def ffn_products(x, grad, up_ref, down_ref, active_ref, hidden_ref):
    units = up_ref.shape[1]
    size = units // 3 if units % (3 * 128) == 0 else units
    out = back = 0.0
    for begin in range(0, units, size):
        cols = slice(begin, begin + size)
        active, slope = gelu_pair(times(x, up_ref[:, cols]))
        active = active.astype(BF16)
        active_ref[:, cols] = active
        hidden_grad = (times(grad, down_ref[:, cols]) * slope).astype(BF16)
        hidden_ref[:, cols] = hidden_grad
        out += times_t(active, down_ref[:, cols])
        back += times_t(hidden_grad, up_ref[:, cols])
    return out, back


def ffn_first_body(
    xa_ref, xb_ref, ga_ref, gb_ref, up_ref, down_ref, active_ref, hidden_ref, out_ref, back_ref
):
    early = pl.program_id(0) < 2
    x = jnp.where(early, xa_ref[...], xb_ref[...])
    grad = jnp.where(early, ga_ref[...], gb_ref[...])
    out, back = ffn_products(x, grad, up_ref, down_ref, active_ref, hidden_ref)
    out_ref[...] = out
    back_ref[...] = back


def ffn_second_body(
    xa_ref, xb_ref, ga_ref, gb_ref, up_ref, down_ref, out_ref, back_ref,
    active_ref, hidden_ref, out_keep_ref, out_send_ref, keep_ref, send_ref,
):
    early = pl.program_id(0) < 2
    x = jnp.where(early, xa_ref[...], xb_ref[...])
    grad = jnp.where(early, ga_ref[...], gb_ref[...])
    out, back = ffn_products(x, grad, up_ref, down_ref, active_ref, hidden_ref)
    out += out_ref[...]
    back += back_ref[...]

    @pl.when(early)
    def _():
        out_keep_ref[...] = out
        keep_ref[...] = back

    @pl.when(jnp.logical_not(early))
    def _():
        out_send_ref[...] = out.astype(BF16)
        send_ref[...] = back.astype(BF16)


def ffn(x, grad, weight, partial=None):
    half, width = x[0].shape
    share = half // 2
    units = weight.shape[1] // 2
    rows = 2 * half

    def each(i):
        return (i, 0)

    def first(i):
        return (jnp.minimum(i, 1), 0)

    def second(i):
        return (jnp.maximum(i - 2, 0), 0)

    block = (share, width)
    in_specs = [
        pl.BlockSpec(block, first),
        pl.BlockSpec(block, second),
        pl.BlockSpec(block, first),
        pl.BlockSpec(block, second),
        pl.BlockSpec((width, units), lambda i: (0, 0)),
        pl.BlockSpec((width, units), lambda i: (0, 1)),
    ]
    outs = [((rows, units), BF16), ((rows, units), BF16)]
    out_specs = [pl.BlockSpec((share, units), each)] * 2
    if partial is None:
        outs += [((rows, width), F32)] * 2
        out_specs += [pl.BlockSpec(block, each)] * 2
    else:
        in_specs += [pl.BlockSpec(block, each)] * 2
        outs += [((half, width), F32), ((half, width), BF16)] * 2
        out_specs += [pl.BlockSpec(block, first), pl.BlockSpec(block, second)] * 2
    return call(
        ffn_first_body if partial is None else ffn_second_body,
        (4,),
        (*x, *grad, weight, weight, *(partial or ())),
        in_specs,
        outs,
        out_specs,
    )


def weight_grad_body(plan, lefts_count, *refs):
    lefts, rights, out = refs[:lefts_count], refs[lefts_count:-1], refs[-1]
    begin = 0
    for pairs in plan:
        cols = rights[pairs[0][1]].shape[1]
        total = 0.0
        for left, right, first in pairs:
            size = lefts[left].shape[0]
            total += t_times(lefts[left][...], rights[right][first : first + size, :])
        out[:, begin : begin + cols] = total.astype(BF16)
        begin += cols


def weight_grad(*parts):
    lefts, rights, plan = [], [], []
    for part_lefts, part_rights in parts:
        pairs = []
        right = first = 0
        for left in part_lefts:
            pairs.append((len(lefts), len(rights) + right, first))
            lefts.append(left)
            first += left.shape[0]
            if first == part_rights[right].shape[0]:
                right, first = right + 1, 0
        rights += part_rights
        plan.append(pairs)
    width = lefts[0].shape[1]
    cols = sum(part_rights[0].shape[1] for _, part_rights in parts)
    size = 256 if width % 256 == 0 else width
    return call(
        functools.partial(weight_grad_body, plan, len(lefts)),
        (width // size,),
        (*lefts, *rights),
        [pl.BlockSpec((v.shape[0], size), lambda i: (0, i)) for v in lefts]
        + [whole_spec(v.shape) for v in rights],
        [((width, cols), BF16)],
        [pl.BlockSpec((size, cols), lambda i: (i, 0))],
    )[0]


def text_project_body(text_ref, weight_ref, out_ref):
    out_ref[...] = times(text_ref[...], weight_ref[...]).astype(BF16)


def text_project(text, weight, block, cols):
    ins = (text, weight)
    specs = [whole_spec(text.shape), pl.BlockSpec((weight.shape[0], cols), lambda i: (0, block))]
    shape = (text.shape[0], cols)
    return call(text_project_body, (1,), ins, specs, [(shape, BF16)], [whole_spec(shape)])[0]


def text_back_body(half, grads_ref, weight_ref, keep_ref, send_ref):
    rows = times_t(grads_ref[...], weight_ref[...])
    for c in range(keep_ref.shape[0]):
        begin = 2 * c * half
        keep_ref[c] = rows[begin : begin + half]
        send_ref[c] = rows[begin + half : begin + 2 * half].astype(BF16)


def text_back(grads, weight, block, clips):
    width, cols = weight.shape[0], grads.shape[1]
    half = grads.shape[0] // clips // 2
    shape = (clips, half, width)
    return call(
        functools.partial(text_back_body, half),
        (1,),
        (grads, weight),
        [whole_spec(grads.shape), pl.BlockSpec((width, cols), lambda i: (0, block))],
        [(shape, F32), (shape, BF16)],
        [whole_spec(shape)] * 2,
    )


def local(
    n,
    audio_states,
    text_states,
    out_grad,
    self_qkv,
    self_out,
    cross_query,
    cross_kv,
    cross_out,
    mlp_up,
    mlp_down,
    norm_gain,
    norm_bias,
):
    clips, share, width = audio_states.shape
    units = self_out.shape[0]
    pairs = units // PAIR
    both = range(clips)

    Order.token = None
    table = ring_table(n)

    qkv_shard = self_qkv.reshape(3, -1, pairs, PAIR).transpose(1, 2, 0, 3).reshape(-1, 3 * units)
    self_ring = RingGather(jnp.concatenate((qkv_shard, self_out.T), 1), n)
    got = self_ring.step()
    params = small_gather(jnp.concatenate((norm_gain, norm_bias), 0), n).astype(F32)
    out_swapped = [swap_chip(out_grad[c]) for c in both]
    cross_own = jnp.concatenate((cross_query, cross_out.T), 1)
    cross_came = swap_chip(cross_own)
    part = mlp_up.shape[1] // 2
    ffn_shards = [
        jnp.concatenate([v[:, k * part : (k + 1) * part] for v in (mlp_up, mlp_down.T)], 1)
        for k in range(2)
    ]

    rows_in = audio_states.reshape(clips * share, width)
    cross_came, out_swapped[0] = self_ring.turn([cross_came, out_swapped[0]], params)
    cross_shard = jnp.concatenate((cross_own, cross_came, cross_kv[0], cross_kv[1]), axis=1)
    _, normed = norm_forward(0, (rows_in,), params, clips * share)
    normed = [normed[c * share : (c + 1) * share] for c in both]
    normed_swapped = [swap_chip(v) for v in normed]
    full_self = [gather_rows(normed[0], normed_swapped[0])]
    self_ring.step()
    cross_ring = RingGather(hold(cross_shard, self_ring.step()), n)
    got = cross_ring.step()
    self_w = self_ring.whole(wait=normed_swapped[1:])
    full_self += [gather_rows(normed[c], normed_swapped[c]) for c in range(1, clips)]
    seen_out = [gather_rows(out_grad[0], out_swapped[0])]
    text_pair = jnp.concatenate((text_states, swap_chip(text_states)), axis=1)
    text_full = jnp.concatenate((text_pair, swap_core(text_pair)), axis=1)
    qkv, self_attn, self_log, mid_terms = [], [], [], []
    for c in both:
        rows, attn, log, keep, send = self_forward(*full_self[c], self_w, units)
        if c == 0:
            (send,) = cross_ring.turn([send])
        else:
            keep_0, seen_0, other_0 = mid_terms[0][1:]
            send, other_0 = cross_ring.turn([send, other_0])
            mid_terms[0] = (audio_states[0], keep_0, seen_0, other_0)
        mid_terms.append((audio_states[c], *sum_over_tp(keep, send)))
        qkv.append(rows)
        self_attn.append(attn)
        self_log.append(log)
    stream_mid, cross_rows = [], []
    for c in both:
        stream, normed = norm_forward(1, mid_terms[c], params, share)
        stream_mid.append(stream)
        cross_rows.append((normed, swap_core(normed)))
    cross_ring.turn()
    early_gather = RingGather(hold(ffn_shards[0], cross_ring.got[-1] if cross_ring.got else ()), n)
    early_gather.step()
    cross_w = cross_ring.whole(wait=out_swapped[1:])
    seen_out += [gather_rows(out_grad[c], out_swapped[c]) for c in range(1, clips)]
    text_rows = text_full.reshape(-1, width)
    text_kv = text_project(text_rows, cross_w, 2, 2 * units).reshape(clips, -1, 2 * units)
    text_other = swap_chip(text_kv)
    early_gather.turn()
    cross_q, cross_attn, stream_late, full_ffn = [], [], [], []
    for c in both:
        queries, attn, keep, send = cross_forward(
            *cross_rows[c], cross_w, (text_kv[c], text_other[c])
        )
        if c:
            send, came = early_gather.turn([send, came])
            full_ffn.append(gather_rows(normed_late, came))
        cross_q.append(queries)
        cross_attn.append(attn)
        stream, normed = norm_forward(2, (stream_mid[c], keep, swap_core(send)), params, share)
        stream_late.append(stream)
        normed_late, came = normed, swap_chip(normed)
        if c == 0:
            early_gather.turn()
    late_gather = RingGather(hold(ffn_shards[1], early_gather.got[-1] if early_gather.got else ()), n)
    late_gather.step()
    early_w = early_gather.whole()

    actives, hiddens, partials = [[], []], [[], []], []
    for c in both:
        active, hidden, *partial = ffn(full_ffn[c], seen_out[c], early_w)
        if c == 0:
            active, came = late_gather.turn([active, came])
            full_ffn.append(gather_rows(normed_late, came))
        else:
            (active,) = late_gather.turn([active])
        actives[0].append(active)
        hiddens[0].append(hidden)
        partials.append(partial)
    grad = weight_grad((sum(full_ffn, ()), hiddens[0]), (sum(seen_out, ()), actives[0]))
    (grad,) = late_gather.turn([grad])
    late_w = late_gather.whole()

    def sum_clips(grad):
        return lax.psum_scatter(grad, "fsdp", scatter_dimension=0, tiled=True)

    ffn_totals = [sum_clips(grad)]
    back_terms, out_terms = [], []
    for c in both:
        active, hidden, out_keep, out_send, keep, send = ffn(
            full_ffn[c], seen_out[c], late_w, partials[c]
        )
        if c:
            (send,) = tick([send], back_terms[0][-1])
        back_terms.append(sum_over_tp(keep, send))
        out_terms.append((out_keep, out_send))
        actives[1].append(active)
        hiddens[1].append(hidden)

    norm_sums = [[], [], []]
    grad_mid, grad_in, seen_mid, seen_in = [], [], [], []
    cross_grads, own_kv, other_kv, terms, branches = [], [], [], [], []
    def late_back(c):
        grad, branch, sums = norm_backward(
            2, stream_late[c], out_grad[c], back_terms[c], params, (F32, BF16)
        )
        norm_sums[2].append(sums)
        grad_mid.append(grad)
        seen_mid.append((branch, swap_core(branch)))

    def cross_back(c):
        dq, own, other, keep, send = cross_backward(
            *seen_mid[c], cross_w, (text_kv[c], text_other[c]), cross_q[c]
        )
        cross_grads.append(dq)
        own_kv.append(own)
        other_kv.append(other)
        terms.append((keep, swap_core(send)))

    def mid_back(c):
        grad, branch, sums = norm_backward(
            1, stream_mid[c], grad_mid[c], terms[c], params, (F32, BF16)
        )
        norm_sums[1].append(sums)
        grad_in.append(grad)
        branches.append((branch, swap_chip(branch)))

    late_back(0)
    wide = weight_grad((sum(full_ffn, ()), hiddens[1]), (sum(seen_out, ()), actives[1]))
    wide, other = tick([wide, back_terms[1][-1]])
    back_terms[1] = (*back_terms[1][:-1], other)
    ffn_totals.append(sum_clips(wide))
    for c in both:
        cross_back(c)
        if c + 1 < clips:
            late_back(c + 1)
        mid_back(c)
    kv_came = swap_chip(jnp.stack(other_kv))
    wide = weight_grad((sum(cross_rows, ()), cross_grads), (sum(seen_mid, ()), cross_attn))
    wide, came = tick([wide, branches[0][1]])
    seen_in = [gather_rows(branches[0][0], came)]
    seen_in += [gather_rows(*branches[c]) for c in range(1, clips)]
    cross_shares = [
        jnp.concatenate([wide[:, k * units : (k + 1) * units] for k in (first, first + 2)], 1)
        for first in range(2)
    ]
    cross_came = swap_chip(cross_shares[1])

    self_grads, in_terms, out_sums = [], [], []
    for c in both:
        grads, keep, send = self_backward(
            *seen_in[c], self_w, qkv[c], self_attn[c], self_log[c]
        )
        if c == 0:
            send, kv_came = tick([send, kv_came])
        else:
            send, cross_came, text_came = tick([send, cross_came, text_came], *out_sum.came)
            out_sum.step()
        in_terms.append(sum_over_tp(keep, send))
        self_grads.append(grads)
        if c == 0:
            kv_grads = (jnp.stack(own_kv) + kv_came.astype(F32)).astype(BF16)
            kv_rows = kv_grads.reshape(-1, 2 * units)
            grad = weight_grad((sum(seen_in, ()), self_attn), ([text_rows], [kv_rows]))
            out_sum = RingSum([grad], n, table)
            text_keep, text_send = text_back(kv_rows, cross_w, 2, clips)
            quarter = text_keep.shape[1] // 2
            text_seen = text_keep + swap_core(text_send).astype(F32)
            text_came = swap_chip(text_seen[:, quarter:].astype(BF16))
        else:
            cross_total = sum_clips(
                (cross_shares[0].astype(F32) + cross_came.astype(F32)).astype(BF16)
            )
    text_grad = text_seen[:, :quarter] + text_came.astype(F32)
    grad = weight_grad((sum(full_self, ()), self_grads))
    qkv_sum = RingSum([grad], n, table)
    out_sum.step()
    late_terms = [sum_over_tp(*out_terms[c]) for c in both]
    audio_grad, layer_out = [], []
    for c in both:
        grad, sums = norm_backward(0, audio_states[c], grad_in[c], in_terms[c], params, (BF16,))
        norm_sums[0].append(sums)
        audio_grad.append(grad)
        if c == 0:
            qkv_sum.step()
            out_sum.step()
    norm_total = SmallSum(jnp.concatenate([sum(v) for v in norm_sums], 0), n)
    audio_grad = join(audio_grad)
    norm_total.step()
    norm_total.step()
    qkv_sum.step()
    out_total = out_sum.total()
    norm_total.step()
    layer_out.append(sum_terms((stream_late[0], *late_terms[0]), (share, width)))
    norm_total.step()
    qkv_sum.step()
    for c in range(1, clips):
        layer_out.append(sum_terms((stream_late[c], *late_terms[c]), (share, width)))
    layer_out = join(layer_out)
    norm_total = norm_total.total()
    qkv_total = qkv_sum.total()

    def cut(total, begin, count=1):
        return total[:, begin * units : (begin + count) * units]

    qkv_total = qkv_total.reshape(-1, pairs, 3, PAIR).transpose(2, 0, 1, 3)
    return (
        layer_out,
        audio_grad,
        text_grad.astype(BF16),
        qkv_total.reshape(3, -1, units),
        cut(out_total, 0).T,
        cut(cross_total, 0).astype(F32),
        jnp.stack((cut(out_total, 1), cut(out_total, 2))),
        cut(cross_total, 1).astype(F32).T,
        jnp.concatenate([v[:, :part] for v in ffn_totals], 1).astype(F32),
        jnp.concatenate([v[:, part:] for v in ffn_totals], 1).astype(F32).T,
        norm_total[0::8],
        norm_total[1::8],
    )


def solution(mesh):
    n = mesh.shape["fsdp"]

    def body(*args):
        return local(n, *args)

    return jax.shard_map(
        body,
        mesh=mesh,
        in_specs=(
            P("fsdp", "tp", None),
            P("fsdp", "tp", None),
            P("fsdp", "tp", None),
            P(None, "fsdp", "tp"),
            P("tp", "fsdp"),
            P("fsdp", "tp"),
            P(None, "fsdp", "tp"),
            P("tp", "fsdp"),
            P("fsdp", "tp"),
            P("tp", "fsdp"),
            P(None, "fsdp"),
            P(None, "fsdp"),
        ),
        out_specs=(
            P("fsdp", "tp", None),
            P("fsdp", "tp", None),
            P("fsdp", "tp", None),
            P(None, "fsdp", "tp"),
            P("tp", "fsdp"),
            P("fsdp", "tp"),
            P(None, "fsdp", "tp"),
            P("tp", "fsdp"),
            P("fsdp", "tp"),
            P("tp", "fsdp"),
            P(None, "fsdp"),
            P(None, "fsdp"),
        ),
        check_vma=False,
    )
```

time: 2660 us -> 782 us (0.29)
  waiting for transfers between devices: 1980 us -> 199 us
  matrix products: 400 us -> 0 us
  Pallas kernels: 0 us -> 333 us
  starting transfers between devices: 4.01 us -> 86.7 us
  other arithmetic: 95.3 us -> 17 us
  blocking collectives: 72.1 us -> 0 us
  local copies, waits for them, and re-layouts: 80 us -> 120 us
    reduce_scatter x19 -> x3, waiting for transfers between devices: 1040 us -> 0.01 us  [sum_clips(): return lax.psum_scatter(grad, 'fsdp', scatter_dimension=0, tiled=True)]
    all_gather x19 -> x0, waiting for transfers between devices: 574 us -> none  [the longest x6 128 us: gather_rows(): return lax.all_gather(values, 'tp', axis=0, tiled=True)]
    dot_general x90 -> x0, matrix products: 400 us -> none  [the longest x14 88.8 us: row_product(): lax.dot_general(left_rows, weight, ((left_dims, right_dims), ((), ())), p...]
    unnamed x46 -> x3, waiting for transfers between devices: 373 us -> 0.05 us
    pallas_call x0 -> x79, Pallas kernels: none -> 333 us  [call(): pl.pallas_call(run, grid=grid, in_specs=list(in_specs) + [hbm] * len(wait...]
    ppermute x0 -> x104, waiting for transfers between devices: none -> 199 us  [the longest x24 65.2 us: send_next(): lax.ppermute(values, 'fsdp', [(ring[k], ring[(k + 1) % n]) for k in range...]
    ppermute x0 -> x104, starting transfers between devices: none -> 86.2 us  [the longest x24 43.6 us: send_next(): lax.ppermute(values, 'fsdp', [(ring[k], ring[(k + 1) % n]) for k in range...]
    all_gather x4 -> x0, blocking collectives: 65.8 us -> none  [the longest x1 27.8 us: local(): lax.all_gather(norm_gain, 'fsdp', axis=1, tiled=True)]
  transfers between devices with their start and end apart: 42 -> 107, of which waited for: 38 -> 44; matrix products, arithmetic and copies ran while one was open for 19% -> 4% of each run, Pallas kernels for 0% -> 42%
where the time goes in v1:
time: 782 us; the launch traced here: 773 us
  Pallas kernels  333 us (43%)
  waiting for transfers between devices  199 us (25%)
  local copies, waits for them, and re-layouts  120 us (15%)
  starting transfers between devices  86.7 us (11%)
  other arithmetic  17 us (2%)
  between operations  16.5 us (2%)
    pallas_call x79, Pallas kernels, call(): pl.pallas_call(run, grid=grid, in_specs=list(in_specs) + [hbm] * len(wait...  333 us
    unnamed x486, local copies, waits for them, and re-layouts  101 us
    ppermute x24, waiting for transfers between devices, send_next(): lax.ppermute(values, 'fsdp', [(ring[k], ring[(k + 1) % n]) for k in range...  65.2 us
    ppermute x23, waiting for transfers between devices, swap_chip(): return lax.ppermute(values, 'tp', [(t, t ^ 2) for t in range(4)])  52.1 us
    ppermute x24, waiting for transfers between devices, send_prev(): lax.ppermute(values, 'fsdp', [(ring[(k + 1) % n], ring[k]) for k in range...  43.9 us
    ppermute x24, starting transfers between devices, send_next(): lax.ppermute(values, 'fsdp', [(ring[k], ring[(k + 1) % n]) for k in range...  43.6 us
    ppermute x6, waiting for transfers between devices, swap_fsdp(): return lax.ppermute(values, 'fsdp', [(i, i ^ bit) for i in range(n)])  25.4 us
    ppermute x23, starting transfers between devices, swap_chip(): return lax.ppermute(values, 'tp', [(t, t ^ 2) for t in range(4)])  19.6 us
  transfers between devices with their start and end apart: 107, of which 44 were waited for; matrix products, arithmetic and copies ran while one was open for 4% of the time, Pallas kernels for 42%

profile of v1, /device:TPU:0, one launch (start us, length us, event | category | flops | bytes accessed | tf_op | source)
XLA Modules:
  0.0 772.8 jit_solution(11505363932818487695)
XLA Ops:
  18.7 10.1 %collective-permute-done = bf16[1,6,192]{2,1,0:T(8,128)(2,1)S(1)} collective-permute-done((bf16[1,6,192]{2,1,0:T(8,128)(2,1)S(1)}, bf16[1,6,192]{2,1,0:T(8,128)(2,1)S(1)}, u32[]{:S(2)}, u32[]{:S(2)}) %collective-permute-start) | collective-permute-done | bytes 2336 | tf_op jit(solution)/shard_map/ppermute | solution.py:215
  47.8 11.6 %collective-permute-done.9.refs_3_ = bf16[192,1536]{1,0:T(8,128)(2,1)S(1)} collective-permute-done((bf16[192,1536]{1,0:T(8,128)(2,1)}, bf16[192,1536]{1,0:T(8,128)(2,1)S(1)}, u32[]{:S(2)}, u32[]{:S(2)}) %collective-permute-start.9) | collective-permute-done | bytes 589856 | tf_op jit(solution)/shard_map/ppermute | solution.py:56
  62.0 10.8 %collective-permute-done.11.refs_5_ = bf16[192,1536]{1,0:T(8,128)(2,1)S(1)} collective-permute-done((bf16[192,1536]{1,0:T(8,128)(2,1)S(1)}, bf16[192,1536]{1,0:T(8,128)(2,1)S(1)}, u32[]{:S(2)}, u32[]{:S(2)}) %collective-permute-start.11) | collective-permute-done | bytes 589856 | tf_op jit(solution)/shard_map/ppermute | solution.py:56
  86.4 11.5 %collective-permute-done.15.refs_9_ = bf16[256,1536]{1,0:T(8,128)(2,1)S(1)} collective-permute-done((bf16[256,1536]{1,0:T(8,128)(2,1)S(1)}, bf16[256,1536]{1,0:T(8,128)(2,1)S(1)}, u32[]{:S(2)}, u32[]{:S(2)}) %collective-permute-start.15) | collective-permute-done | bytes 786464 | tf_op jit(solution)/shard_map/ppermute | solution.py:23
  101.9 21.6 %self_forward_body.2 = (bf16[1024,1152]{1,0:T(8,128)(2,1)S(1)}, bf16[1024,384]{1,0:T(8,128)(2,1)S(1)}, f32[24,1024]{1,0:T(8,128)S(1)}, f32[512,1536]{1,0:T(8,128...) custom-call(bf16[512,1536]{1,0:T(8,128)(2,1)S(1)} %pad_maximum_fusion.1.refs_0_, ...), custom_call_target="tpu_custom_call" | custom-call | flops 1000 | tf_op jit(solution)/shard_map/self_forward_body/pallas_call | solution.py:260
  131.6 21.5 %self_forward_body.3 = (bf16[1024,1152]{1,0:T(8,128)(2,1)S(1)}, bf16[1024,384]{1,0:T(8,128)(2,1)S(1)}, f32[24,1024]{1,0:T(8,128)S(1)}, f32[512,1536]{1,0:T(8,128...) custom-call(bf16[512,1536]{1,0:T(8,128)(2,1)S(1)} %pad_maximum_fusion.2.refs_0_.refs_2_, ...), custom_call_target="tpu_custom_call" | custom-call | flops 1000 | tf_op jit(solution)/shard_map/self_forward_body/pallas_call | solution.py:260
  167.7 29.7 %collective-permute-done.27.refs_3_ = bf16[256,1536]{1,0:T(8,128)(2,1)S(1)} collective-permute-done((bf16[256,1536]{1,0:T(8,128)(2,1)}, bf16[256,1536]{1,0:T(8,128)(2,1)S(1)}, u32[]{:S(2)}, u32[]{:S(2)}) %collective-permute-start.27) | collective-permute-done | bytes 786464 | tf_op jit(solution)/shard_map/ppermute | solution.py:23
  201.1 8.0 %collective-permute-done.29.refs_2_.refs_8_ = bf16[96,2304]{1,0:T(8,128)(2,1)S(1)} collective-permute-done((bf16[96,2304]{1,0:T(8,128)(2,1)S(1)}, bf16[96,2304]{1,0:T(8,128)(2,1)S(1)}, u32[]{:S(2)}, u32[]{:S(2)}) %collective-permute-start.29) | collective-permute-done | bytes 442400 | tf_op jit(solution)/shard_map/ppermute | solution.py:61
  220.7 5.1 collective-permute-done.33
  226.0 9.5 %cross_forward_body.2 = (bf16[512,768]{1,0:T(8,128)(2,1)S(1)}, bf16[512,768]{1,0:T(8,128)(2,1)S(1)}, f32[256,1536]{1,0:T(8,128)S(1)}, bf16[256,1536]{1,0:T(8,128)(2,1)S(1)}, f32[8,128]{1,0:T(8,128)S(1)}) custom-call(bf16[256,1536]{1,0:T(8,128)(2,1)S(1)} %copy-done.113, bf16[256,1536]{1,0:T(8,128)(2,1)S(1)} %collective-permute-done.24.refs_1_, ...), custom_call_target="tpu_custom_call" | custom-call | flops 1000 | tf_op jit(solution)/shard_map/cross_forward_body/pallas_call | solution.py:260
  240.9 12.2 %collective-permute-done.37.refs_0_ = bf16[192,1536]{1,0:T(8,128)(2,1)S(1)} collective-permute-done((bf16[192,1536]{1,0:T(8,128)(2,1)S(1)}, bf16[192,1536]{1,0:T(8,128)(2,1)S(1)}, u32[]{:S(2)}, u32[]{:S(2)}) %collective-permute-start.37) | collective-permute-done | bytes 589856 | tf_op jit(solution)/shard_map/ppermute | solution.py:56
  257.9 9.5 %cross_forward_body.3 = (bf16[512,768]{1,0:T(8,128)(2,1)S(1)}, bf16[512,768]{1,0:T(8,128)(2,1)S(1)}, f32[256,1536]{1,0:T(8,128)S(1)}, bf16[256,1536]{1,0:T(8,128)(2,1)S(1)}, f32[8,128]{1,0:T(8,128)S(1)}) custom-call(bf16[256,1536]{1,0:T(8,128)(2,1)S(1)} %get-tuple-element.313.refs_0_.refs_2_, bf16[256,1536]{1,0:T(8,128)(2,1)S(1)} %collective-permute-done.41.refs_1_.refs_3_, ...), custom_call_target="tpu_custom_call" | custom-call | flops 1000 | tf_op jit(solution)/shard_map/cross_forward_body/pallas_call | solution.py:260
  290.4 16.5 %ffn_first_body.2 = (bf16[1024,768]{1,0:T(8,128)(2,1)S(1)}, bf16[1024,768]{1,0:T(8,128)(2,1)S(1)}, f32[1024,1536]{1,0:T(8,128)}, f32[1024,1536]{1,0:T(8,128)}, f32[8,128]{1,0:T(8,128)S(1)}) custom-call(bf16[512,1536]{1,0:T(8,128)(2,1)S(1)} %constant_dynamic-update-slice_fusion.3.refs_0_, bf16[512,1536]{1,0:T(8,128)(2,1)S(1)} %collective-permute-done.43.refs_1_, ...), custom_call_target="tpu_custom_call" | custom-call | flops 1000 | tf_op jit(solution)/shard_map/ffn_first_body/pallas_call | solution.py:260
  311.7 16.0 %ffn_first_body.3 = (bf16[1024,768]{1,0:T(8,128)(2,1)S(1)}, bf16[1024,768]{1,0:T(8,128)(2,1)S(1)}, f32[1024,1536]{1,0:T(8,128)}, f32[1024,1536]{1,0:T(8,128)}, f32[8,128]{1,0:T(8,128)S(1)}) custom-call(bf16[512,1536]{1,0:T(8,128)(2,1)S(1)} %constant_dynamic-update-slice_fusion.5.refs_0_.refs_2_, ...), custom_call_target="tpu_custom_call" | custom-call | flops 1000 | tf_op jit(solution)/shard_map/ffn_first_body/pallas_call | solution.py:260
  331.8 15.7 %weight_grad_body.5 = (bf16[1536,1536]{1,0:T(8,128)(2,1)}, f32[8,128]{1,0:T(8,128)S(1)}) custom-call(bf16[512,1536]{1,0:T(8,128)(2,1)S(1)} %constant_dynamic-update-slice_fusion.3.refs_0_, bf16[512,1536]{1,0:T(8,128)(2,1)S(1)} %collective-permute-done.43.refs_1_, bf16[512,1536]{1,0:T(8,128)(2,1)S(1)} %constant_dynamic-update-slice_fusion.5.refs_0_.refs_2_, ...), custom_call_target="tpu_custom_call" | custom-call | flops 1000 | tf_op jit(solution)/shard_map/weight_grad_body/pallas_call | solution.py:260
  354.3 8.7 %collective-permute-done.58.refs_8_ = bf16[96,1536]{1,0:T(8,128)(2,1)S(1)} collective-permute-done((bf16[96,1536]{1,0:T(8,128)(2,1)S(1)}, bf16[96,1536]{1,0:T(8,128)(2,1)S(1)}, u32[]{:S(2)}, u32[]{:S(2)}) %collective-permute-start.58) | collective-permute-done | bytes 294944 | tf_op jit(solution)/shard_map/ppermute | solution.py:61
  368.0 18.0 %ffn_second_body.2 = (bf16[1024,768]{1,0:T(8,128)(2,1)S(1)}, bf16[1024,768]{1,0:T(8,128)(2,1)S(1)}, f32[512,1536]{1,0:T(8,128)}, bf16[512,1536]{1,0:T(8,128)(2,1...) custom-call(bf16[512,1536]{1,0:T(8,128)(2,1)S(1)} %copy-done.16, ...), custom_call_target="tpu_custom_call" | custom-call | flops 1000 | tf_op jit(solution)/shard_map/ffn_second_body/pallas_call | solution.py:260
  397.3 18.2 %ffn_second_body.3 = (bf16[1024,768]{1,0:T(8,128)(2,1)S(1)}, bf16[1024,768]{1,0:T(8,128)(2,1)S(1)}, f32[512,1536]{1,0:T(8,128)}, bf16[512,1536]{1,0:T(8,128)(2,1...) custom-call(bf16[512,1536]{1,0:T(8,128)(2,1)S(1)} %copy-done.14, ...), custom_call_target="tpu_custom_call" | custom-call | flops 1000 | tf_op jit(solution)/shard_map/ffn_second_body/pallas_call | solution.py:260
  431.3 15.9 %weight_grad_body.6 = (bf16[1536,1536]{1,0:T(8,128)(2,1)}, f32[8,128]{1,0:T(8,128)S(1)}) custom-call(bf16[512,1536]{1,0:T(8,128)(2,1)S(1)} %copy-done.16, bf16[512,1536]{1,0:T(8,128)(2,1)S(1)} %copy-done.20, bf16[512,1536]{1,0:T(8,128)(2,1)S(1)} %copy-done.14, bf16[512,1536]{1,0:T(8,128)(2,1)S(1)} %copy-done.23, bf16[512,1536]{1,0:T(8,128)(2,1)S(1)} %copy-done.11, ...), custom_call_target="tpu_custom_call" | custom-call | flops 1000 | tf_op jit(solution)/shard_map/weight_grad_body/pallas_call | solution.py:260
  455.6 9.7 %cross_backward_body.2 = (bf16[512,768]{1,0:T(8,128)(2,1)S(1)}, f32[64,768]{1,0:T(8,128)S(1)}, bf16[64,768]{1,0:T(8,128)(2,1)S(1)}, f32[256,1536]{1,0:T(8,128)S(...) custom-call(bf16[256,1536]{1,0:T(8,128)(2,1)S(1)} %get-tuple-element.371.refs_0_.refs_4_, ...), custom_call_target="tpu_custom_call" | custom-call | flops 1000 | tf_op jit(solution)/shard_map/cross_backward_body/pallas_call | solution.py:260
  477.0 9.6 %cross_backward_body.3 = (bf16[512,768]{1,0:T(8,128)(2,1)S(1)}, f32[64,768]{1,0:T(8,128)S(1)}, bf16[64,768]{1,0:T(8,128)(2,1)S(1)}, f32[256,1536]{1,0:T(8,128)S(...) custom-call(bf16[256,1536]{1,0:T(8,128)(2,1)S(1)} %get-tuple-element.389.refs_0_.refs_6_, ...), custom_call_target="tpu_custom_call" | custom-call | flops 1000 | tf_op jit(solution)/shard_map/cross_backward_body/pallas_call | solution.py:260
  498.4 7.7 %weight_grad_body.7 = (bf16[1536,1536]{1,0:T(8,128)(2,1)}, f32[8,128]{1,0:T(8,128)S(1)}) custom-call(bf16[256,1536]{1,0:T(8,128)(2,1)S(1)} %copy-done.114, bf16[256,1536]{1,0:T(8,128)(2,1)S(1)} %copy-done.118, bf16[256,1536]{1,0:T(8,128)(2,1)S(1)} %copy-done.116, bf16[256,1536]{1,0:T(8,128)(2,1)S(1)} %copy-done.120, ...), custom_call_target="tpu_custom_call" | custom-call | flops 1000 | tf_op jit(solution)/shard_map/weight_grad_body/pallas_call | solution.py:260
  517.5 27.0 %self_backward_body.2 = (bf16[1024,1152]{1,0:T(8,128)(2,1)S(1)}, f32[512,1536]{1,0:T(8,128)}, bf16[512,1536]{1,0:T(8,128)(2,1)}, f32[8,128]{1,0:T(8,128)S(1)}) custom-call(bf16[512,1536]{1,0:T(8,128)(2,1)S(1)} %constant_dynamic-update-slice_fusion.7.refs_0_, bf16[512,1536]{1,0:T(8,128)(2,1)S(1)} %collective-permute-done.69.refs_1_, ...), custom_call_target="tpu_custom_call" | custom-call | flops 1000 | tf_op jit(solution)/shard_map/self_backward_body/pallas_call | solution.py:260
  554.9 8.1 %weight_grad_body.8 = (bf16[1536,1152]{1,0:T(8,128)(2,1)}, f32[8,128]{1,0:T(8,128)S(1)}) custom-call(bf16[512,1536]{1,0:T(8,128)(2,1)S(1)} %copy-done.48, bf16[512,1536]{1,0:T(8,128)(2,1)S(1)} %copy-done.82, bf16[512,1536]{1,0:T(8,128)(2,1)} %constant_dynamic-update-slice_fusion.9.refs_2_.refs_0_, bf16[512,1536]{1,0:T(8,128)(2,1)} %collective-permute-done.71.refs_3_.refs_1_, ...), custom_call_target="tpu_custom_call" | custom-call | flops 1000 | tf_op jit(solution)/shard_map/weight_grad_body/pallas_call | solution.py:260
  567.4 5.3 collective-permute-start.74
  574.0 27.7 %self_backward_body.3 = (bf16[1024,1152]{1,0:T(8,128)(2,1)S(1)}, f32[512,1536]{1,0:T(8,128)}, bf16[512,1536]{1,0:T(8,128)(2,1)}, f32[8,128]{1,0:T(8,128)S(1)}) custom-call(bf16[512,1536]{1,0:T(8,128)(2,1)} %constant_dynamic-update-slice_fusion.9.refs_2_.refs_0_, bf16[512,1536]{1,0:T(8,128)(2,1)} %collective-permute-done.71.refs_3_.refs_1_, ...), custom_call_target="tpu_custom_call" | custom-call | flops 1000 | tf_op jit(solution)/shard_map/self_backward_body/pallas_call | solution.py:260
  619.0 16.0 %collective-permute-done.79.refs_2_ = bf16[192,1152]{1,0:T(8,128)(2,1)S(1)} collective-permute-done((bf16[192,1152]{1,0:T(8,128)(2,1)S(1)}, bf16[192,1152]{1,0:T(8,128)(2,1)S(1)}, u32[]{:S(2)}, u32[]{:S(2)}) %collective-permute-start.79) | collective-permute-done | bytes 442400 | tf_op jit(solution)/shard_map/ppermute | solution.py:56
  638.4 12.2 %weight_grad_body.9 = (bf16[1536,1152]{1,0:T(8,128)(2,1)}, f32[8,128]{1,0:T(8,128)S(1)}) custom-call(bf16[512,1536]{1,0:T(8,128)(2,1)S(1)} %copy-done.30, bf16[512,1536]{1,0:T(8,128)(2,1)S(1)} %copy-done.76, bf16[512,1536]{1,0:T(8,128)(2,1)S(1)} %copy-done.32, bf16[512,1536]{1,0:T(8,128)(2,1)S(1)} %copy-done.78, bf16[1024,1152]{1,0:T(8,128)(2,1)S(1)} %copy-done.122, ...), custom_call_target="tpu_custom_call" | custom-call | flops 1000 | tf_op jit(solution)/shard_map/weight_grad_body/pallas_call | solution.py:260
  657.4 4.8 collective-permute-start.86
  675.2 6.1 collective-permute-done.88.refs_2_
  681.3 6.4 collective-permute-done.89.refs_3_
  731.4 7.2 collective-permute-done.100.refs_1_
  (820 shorter events, 338.4 us)
Async XLA Ops:
  7.2 703.7 %reduce-scatter.6.cloned.1.call-start = ((), (), s32[]{:S(2)}) async-start(), calls=%async_computation.4 | async-start | bytes 5308416 | tf_op jit(solution)/shard_map/reduce_scatter | solution.py:1061
  10.6 28.7 %collective-permute-start.4 = (bf16[192,1536]{1,0:T(8,128)(2,1)}, bf16[192,1536]{1,0:T(8,128)(2,1)}, u32[]{:S(2)}, u32[]{:S(2)}) collective-permute-start(bf16[192,1536]{1,0:T(8,128)(2,1)} %pad_maximum_fusion.5.refs_0_), channel_id=1, source_target_pairs={{8,0},{16,8},{24,16},{28,24},{20,28},{12,20},{4,12},{0,4},{9,1},{1... | collective-permute-start | bytes 1769480 | tf_op jit(solution)/shard_map/ppermute | solution.py:61
  13.6 25.7 %collective-permute-start.3 = (bf16[192,1536]{1,0:T(8,128)(2,1)}, bf16[192,1536]{1,0:T(8,128)(2,1)}, u32[]{:S(2)}, u32[]{:S(2)}) collective-permute-start(bf16[192,1536]{1,0:T(8,128)(2,1)} %pad_maximum_fusion.5.refs_0_), channel_id=1, source_target_pairs={{0,8},{8,16},{16,24},{24,28},{28,20},{20,12},{12,4},{4,0},{1,9},{9... | collective-permute-start | bytes 1769480 | tf_op jit(solution)/shard_map/ppermute | solution.py:56
  61.9 40.0 %collective-permute-start.8 = (bf16[512,1536]{1,0:T(8,128)(2,1)S(1)}, bf16[512,1536]{1,0:T(8,128)(2,1)S(1)}, u32[]{:S(2)}, u32[]{:S(2)}) collective-permute-start(bf16[512,1536]{1,0:T(8,128)(2,1)S(1)} %pad_maximum_fusion.1.refs_0_), channel_id=1, source_target_pairs={{0,1},{1,0},{2,3},{3,2},{4,5},{5,4},{6,7},{7,6},{8,9},{9,8},{10,11... | collective-permute-start | bytes 4718600 | tf_op jit(solution)/shard_map/ppermute | solution.py:27
  83.9 41.1 %collective-permute-start.17 = (bf16[192,2304]{1,0:T(8,128)(2,1)}, bf16[192,2304]{1,0:T(8,128)(2,1)S(1)}, u32[]{:S(2)}, u32[]{:S(2)}) collective-permute-start(bf16[192,2304]{1,0:T(8,128)(2,1)} %get-tuple-element.270.refs_0_), channel_id=1, source_target_pairs={{8,0},{16,8},{24,16},{28,24},{20,28},{12,20},{4,12},{0,4},{9,1},{1... | collective-permute-start | bytes 2654216 | tf_op jit(solution)/shard_map/ppermute | solution.py:61
  84.3 40.7 %collective-permute-start.16 = (bf16[192,2304]{1,0:T(8,128)(2,1)}, bf16[192,2304]{1,0:T(8,128)(2,1)S(1)}, u32[]{:S(2)}, u32[]{:S(2)}) collective-permute-start(bf16[192,2304]{1,0:T(8,128)(2,1)} %get-tuple-element.270.refs_0_), channel_id=1, source_target_pairs={{0,8},{8,16},{16,24},{24,28},{28,20},{20,12},{12,4},{4,0},{1,9},{9... | collective-permute-start | bytes 2654216 | tf_op jit(solution)/shard_map/ppermute | solution.py:56
  126.8 27.8 %collective-permute-start.19 = (bf16[192,2304]{1,0:T(8,128)(2,1)S(1)}, bf16[192,2304]{1,0:T(8,128)(2,1)S(1)}, u32[]{:S(2)}, u32[]{:S(2)}) collective-permute-start(bf16[192,2304]{1,0:T(8,128)(2,1)S(1)} %get-tuple-element.274.refs_1_), channel_id=1, source_target_pairs={{0,8},{8,16},{16,24},{24,28},{28,20},{20,12},{12,4},{4,0},{1,9},{9... | collective-permute-start | bytes 2654216 | tf_op jit(solution)/shard_map/ppermute | solution.py:56
  128.4 26.2 %collective-permute-start.20 = (bf16[192,2304]{1,0:T(8,128)(2,1)S(1)}, bf16[192,2304]{1,0:T(8,128)(2,1)S(1)}, u32[]{:S(2)}, u32[]{:S(2)}) collective-permute-start(bf16[192,2304]{1,0:T(8,128)(2,1)S(1)} %get-tuple-element.275.refs_2_), channel_id=1, source_target_pairs={{8,0},{16,8},{24,16},{28,24},{20,28},{12,20},{4,12},{0,4},{9,1},{1... | collective-permute-start | bytes 2654216 | tf_op jit(solution)/shard_map/ppermute | solution.py:61
  157.3 40.9 %collective-permute-start.25 = (bf16[192,2304]{1,0:T(8,128)(2,1)}, bf16[192,2304]{1,0:T(8,128)(2,1)S(1)}, u32[]{:S(2)}, u32[]{:S(2)}) collective-permute-start(bf16[192,2304]{1,0:T(8,128)(2,1)} %copy-done.95), channel_id=1, source_target_pairs={{0,8},{8,16},{16,24},{24,28},{28,20},{20,12},{12,4},{4,0},{1,9},{9... | collective-permute-start | bytes 2654216 | tf_op jit(solution)/shard_map/ppermute | solution.py:56
  158.9 39.3 %collective-permute-start.26 = (bf16[192,2304]{1,0:T(8,128)(2,1)}, bf16[192,2304]{1,0:T(8,128)(2,1)S(1)}, u32[]{:S(2)}, u32[]{:S(2)}) collective-permute-start(bf16[192,2304]{1,0:T(8,128)(2,1)} %copy-done.97), channel_id=1, source_target_pairs={{8,0},{16,8},{24,16},{28,24},{20,28},{12,20},{4,12},{0,4},{9,1},{1... | collective-permute-start | bytes 2654216 | tf_op jit(solution)/shard_map/ppermute | solution.py:61
  159.4 41.1 %collective-permute-start.31 = (bf16[2,16,1536]{2,1,0:T(8,128)(2,1)S(1)}, bf16[2,16,1536]{2,1,0:T(8,128)(2,1)S(1)}, u32[]{:S(2)}, u32[]{:S(2)}) collective-permute-start(bf16[2,16,1536]{2,1,0:T(8,128)(2,1)S(1)} %copy-done.230), channel_id=1, source_target_pairs={{0,2},{1,3},{2,0},{3,1},{4,6},{5,7},{6,4},{7,5},{8,10},{9,11},{10,... | collective-permute-start | bytes 294920 | tf_op jit(solution)/shard_map/ppermute | solution.py:23
  160.3 51.7 %collective-permute-start.30 = (bf16[256,1536]{1,0:T(8,128)(2,1)S(1)}, bf16[256,1536]{1,0:T(8,128)(2,1)S(1)}, u32[]{:S(2)}, u32[]{:S(2)}) collective-permute-start(bf16[256,1536]{1,0:T(8,128)(2,1)S(1)} %get-tuple-element.512.refs_1_), channel_id=1, source_target_pairs={{0,2},{1,3},{2,0},{3,1},{4,6},{5,7},{6,4},{7,5},{8,10},{9,11},{10,... | collective-permute-start | bytes 2359304 | tf_op jit(solution)/shard_map/ppermute | solution.py:23
  162.4 35.0 %collective-permute-start.27 = (bf16[256,1536]{1,0:T(8,128)(2,1)}, bf16[256,1536]{1,0:T(8,128)(2,1)S(1)}, u32[]{:S(2)}, u32[]{:S(2)}) collective-permute-start(bf16[256,1536]{1,0:T(8,128)(2,1)} %get-tuple-element.290), channel_id=1, source_target_pairs={{0,2},{1,3},{2,0},{3,1},{4,6},{5,7},{6,4},{7,5},{8,10},{9,11},{10,... | collective-permute-start | bytes 2359304 | tf_op jit(solution)/shard_map/ppermute | solution.py:23
  240.3 30.2 %collective-permute-start.42 = (bf16[256,1536]{1,0:T(8,128)(2,1)S(1)}, bf16[256,1536]{1,0:T(8,128)(2,1)S(1)}, u32[]{:S(2)}, u32[]{:S(2)}) collective-permute-start(bf16[256,1536]{1,0:T(8,128)(2,1)S(1)} %get-tuple-element.307), channel_id=1, source_target_pairs={{0,2},{1,3},{2,0},{3,1},{4,6},{5,7},{6,4},{7,5},{8,10},{9,11},{10,... | collective-permute-start | bytes 2359304 | tf_op jit(solution)/shard_map/ppermute | solution.py:23
  257.8 32.5 %collective-permute-start.44 = (bf16[512,1536]{1,0:T(8,128)(2,1)S(1)}, bf16[512,1536]{1,0:T(8,128)(2,1)S(1)}, u32[]{:S(2)}, u32[]{:S(2)}) collective-permute-start(bf16[512,1536]{1,0:T(8,128)(2,1)S(1)} %pad_maximum_fusion.3.refs_2_.refs_4_), channel_id=1, source_target_pairs={{0,1},{1,0},{2,3},{3,2},{4,5},{5,4},{6,7},{7,6},{8,9},{9,8},{10,11... | collective-permute-start | bytes 4718600 | tf_op jit(solution)/shard_map/ppermute | solution.py:27
  274.8 32.1 %collective-permute-start.50 = (bf16[256,1536]{1,0:T(8,128)(2,1)}, bf16[256,1536]{1,0:T(8,128)(2,1)S(1)}, u32[]{:S(2)}, u32[]{:S(2)}) collective-permute-start(bf16[256,1536]{1,0:T(8,128)(2,1)} %get-tuple-element.331), channel_id=1, source_target_pairs={{0,2},{1,3},{2,0},{3,1},{4,6},{5,7},{6,4},{7,5},{8,10},{9,11},{10,... | collective-permute-start | bytes 2359304 | tf_op jit(solution)/shard_map/ppermute | solution.py:23
  352.1 408.7 %reduce-scatter.8.cloned.1.call-start = ((), (), s32[]{:S(2)}) async-start(), calls=%async_computation.5 | async-start | bytes 5308416 | tf_op jit(solution)/shard_map/reduce_scatter | solution.py:1061
  451.7 312.6 %reduce-scatter.4.cloned.1.call-start = ((), (), s32[]{:S(2)}) async-start(), calls=%async_computation.3 | async-start | bytes 2654208 | tf_op jit(solution)/shard_map/reduce_scatter | solution.py:1061
  510.4 34.1 %collective-permute-start.72 = (bf16[2,64,768]{2,1,0:T(8,128)(2,1)S(1)}, bf16[2,64,768]{2,1,0:T(8,128)(2,1)S(1)}, u32[]{:S(2)}, u32[]{:S(2)}) collective-permute-start(bf16[2,64,768]{2,1,0:T(8,128)(2,1)S(1)} %pad_maximum_fusion.12), channel_id=1, source_target_pairs={{0,2},{1,3},{2,0},{3,1},{4,6},{5,7},{6,4},{7,5},{8,10},{9,11},{10,... | collective-permute-start | bytes 589832 | tf_op jit(solution)/shard_map/ppermute | solution.py:23
  511.1 34.1 %collective-permute-start.70 = (bf16[256,1536]{1,0:T(8,128)(2,1)S(1)}, bf16[256,1536]{1,0:T(8,128)(2,1)S(1)}, u32[]{:S(2)}, u32[]{:S(2)}) collective-permute-start(bf16[256,1536]{1,0:T(8,128)(2,1)S(1)} %get-tuple-element.404), channel_id=1, source_target_pairs={{0,2},{1,3},{2,0},{3,1},{4,6},{5,7},{6,4},{7,5},{8,10},{9,11},{10,... | collective-permute-start | bytes 2359304 | tf_op jit(solution)/shard_map/ppermute | solution.py:23
  515.9 87.2 %collective-permute-start.76 = (bf16[1536,768]{1,0:T(8,128)(2,1)}, bf16[1536,768]{1,0:T(8,128)(2,1)}, u32[]{:S(2)}, u32[]{:S(2)}) collective-permute-start(bf16[1536,768]{1,0:T(8,128)(2,1)} %pad_maximum_fusion), channel_id=1, source_target_pairs={{0,2},{1,3},{2,0},{3,1},{4,6},{5,7},{6,4},{7,5},{8,10},{9,11},{10,... | collective-permute-start | bytes 7077896 | tf_op jit(solution)/shard_map/ppermute | solution.py:23
  567.4 35.7 %collective-permute-start.74 = (bf16[96,1152]{1,0:T(8,128)(2,1)S(1)}, bf16[96,1152]{1,0:T(8,128)(2,1)S(1)}, u32[]{:S(2)}, u32[]{:S(2)}) collective-permute-start(bf16[96,1152]{1,0:T(8,128)(2,1)S(1)} %get-tuple-element.423), channel_id=1, source_target_pairs={{0,8},{8,16},{16,24},{24,28},{28,20},{20,12},{12,4},{4,0},{1,9},{9... | collective-permute-start | bytes 663560 | tf_op jit(solution)/shard_map/ppermute | solution.py:56
  572.7 30.4 %collective-permute-start.75 = (bf16[96,1152]{1,0:T(8,128)(2,1)S(1)}, bf16[96,1152]{1,0:T(8,128)(2,1)S(1)}, u32[]{:S(2)}, u32[]{:S(2)}) collective-permute-start(bf16[96,1152]{1,0:T(8,128)(2,1)S(1)} %get-tuple-element.424), channel_id=1, source_target_pairs={{8,0},{16,8},{24,16},{28,24},{20,28},{12,20},{4,12},{0,4},{9,1},{1... | collective-permute-start | bytes 663560 | tf_op jit(solution)/shard_map/ppermute | solution.py:61
  572.8 30.4 %collective-permute-start.78 = (bf16[2,16,1536]{2,1,0:T(8,128)(2,1)S(1)}, bf16[2,16,1536]{2,1,0:T(8,128)(2,1)S(1)}, u32[]{:S(2)}, u32[]{:S(2)}) collective-permute-start(bf16[2,16,1536]{2,1,0:T(8,128)(2,1)S(1)} %slice.210), channel_id=1, source_target_pairs={{0,2},{1,3},{2,0},{3,1},{4,6},{5,7},{6,4},{7,5},{8,10},{9,11},{10,... | collective-permute-start | bytes 294920 | tf_op jit(solution)/shard_map/ppermute | solution.py:23
  608.8 53.5 %collective-permute-start.59 = (bf16[512,1536]{1,0:T(8,128)(2,1)}, bf16[512,1536]{1,0:T(8,128)(2,1)}, u32[]{:S(2)}, u32[]{:S(2)}) collective-permute-start(bf16[512,1536]{1,0:T(8,128)(2,1)} %copy-done.210), channel_id=1, source_target_pairs={{0,1},{1,0},{2,3},{3,2},{4,5},{5,4},{6,7},{7,6},{8,9},{9,8},{10,11... | collective-permute-start | bytes 4718600 | tf_op jit(solution)/shard_map/ppermute | solution.py:27
  608.9 53.3 %collective-permute-start.84 = (bf16[512,1536]{1,0:T(8,128)(2,1)}, bf16[512,1536]{1,0:T(8,128)(2,1)S(1)}, u32[]{:S(2)}, u32[]{:S(2)}) collective-permute-start(bf16[512,1536]{1,0:T(8,128)(2,1)} %copy-done.211), channel_id=1, source_target_pairs={{0,1},{1,0},{2,3},{3,2},{4,5},{5,4},{6,7},{7,6},{8,9},{9,8},{10,11... | collective-permute-start | bytes 4718600 | tf_op jit(solution)/shard_map/ppermute | solution.py:27
  615.9 48.9 %collective-permute-start.83 = (bf16[256,1536]{1,0:T(8,128)(2,1)}, bf16[256,1536]{1,0:T(8,128)(2,1)}, u32[]{:S(2)}, u32[]{:S(2)}) collective-permute-start(bf16[256,1536]{1,0:T(8,128)(2,1)} %get-tuple-element.449), channel_id=1, source_target_pairs={{0,2},{1,3},{2,0},{3,1},{4,6},{5,7},{6,4},{7,5},{8,10},{9,11},{10,... | collective-permute-start | bytes 2359304 | tf_op jit(solution)/shard_map/ppermute | solution.py:23
  616.8 37.8 %collective-permute-start.80 = (bf16[192,1152]{1,0:T(8,128)(2,1)}, bf16[192,1152]{1,0:T(8,128)(2,1)}, u32[]{:S(2)}, u32[]{:S(2)}) collective-permute-start(bf16[192,1152]{1,0:T(8,128)(2,1)} %get-tuple-element.436), channel_id=1, source_target_pairs={{8,0},{16,8},{24,16},{28,24},{20,28},{12,20},{4,12},{0,4},{9,1},{1... | collective-permute-start | bytes 1327112 | tf_op jit(solution)/shard_map/ppermute | solution.py:61
  635.0 60.3 %collective-permute-start.85 = (bf16[256,1536]{1,0:T(8,128)(2,1)}, bf16[256,1536]{1,0:T(8,128)(2,1)}, u32[]{:S(2)}, u32[]{:S(2)}) collective-permute-start(bf16[256,1536]{1,0:T(8,128)(2,1)} %get-tuple-element.456), channel_id=1, source_target_pairs={{0,2},{1,3},{2,0},{3,1},{4,6},{5,7},{6,4},{7,5},{8,10},{9,11},{10,... | collective-permute-start | bytes 2359304 | tf_op jit(solution)/shard_map/ppermute | solution.py:23
  657.4 35.0 %collective-permute-start.86 = (bf16[192,1152]{1,0:T(8,128)(2,1)}, bf16[192,1152]{1,0:T(8,128)(2,1)}, u32[]{:S(2)}, u32[]{:S(2)}) collective-permute-start(bf16[192,1152]{1,0:T(8,128)(2,1)} %get-tuple-element.457), channel_id=1, source_target_pairs={{0,8},{8,16},{16,24},{24,28},{28,20},{20,12},{12,4},{4,0},{1,9},{9... | collective-permute-start | bytes 1327112 | tf_op jit(solution)/shard_map/ppermute | solution.py:56
  662.2 30.2 %collective-permute-start.87 = (bf16[192,1152]{1,0:T(8,128)(2,1)}, bf16[192,1152]{1,0:T(8,128)(2,1)}, u32[]{:S(2)}, u32[]{:S(2)}) collective-permute-start(bf16[192,1152]{1,0:T(8,128)(2,1)} %get-tuple-element.458), channel_id=1, source_target_pairs={{8,0},{16,8},{24,16},{28,24},{20,28},{12,20},{4,12},{0,4},{9,1},{1... | collective-permute-start | bytes 1327112 | tf_op jit(solution)/shard_map/ppermute | solution.py:61
  715.6 29.0 %collective-permute-start.97 = (bf16[256,1536]{1,0:T(8,128)(2,1)}, bf16[256,1536]{1,0:T(8,128)(2,1)S(1)}, u32[]{:S(2)}, u32[]{:S(2)}) collective-permute-start(bf16[256,1536]{1,0:T(8,128)(2,1)} %copy-done.212), channel_id=1, source_target_pairs={{0,2},{1,3},{2,0},{3,1},{4,6},{5,7},{6,4},{7,5},{8,10},{9,11},{10,... | collective-permute-start | bytes 2359304 | tf_op jit(solution)/shard_map/ppermute | solution.py:23
  (314 other events, 3440.1 us)
Sparse Core Ops, SparseCore 0:
  352.2 94.7 reduce-scatter.5
  451.8 99.1 reduce-scatter.7
  608.9 80.6 reduce-scatter.3

commit v2 on v1

--- a/solution.py
+++ b/solution.py
@@ -16,7 +16,7 @@
 RATE = HEAD ** (-0.5) * math.log2(math.e)
 TOKEN = (8, 128)
 COST = 1000
-VMEM = 44 * 2**20
+VMEM = 52 * 2**20
 
 
 def swap_chip(values):
@@ -117,7 +117,7 @@
         )[0]
 
 
-def ring_body(kind, rows, count, sides, *refs):
+def ring_body(kind, rows, count, sides, split, *refs):
     table, wholes = refs[0], refs[1 : 1 + count]
     came = refs[1 + count : -len(sides) - count - 1]
     outs, own, sems = refs[-len(sides) - count - 1 : -count - 1], refs[-count - 1 : -1], refs[-1]
@@ -151,8 +151,16 @@
                 add = came[side][:, cols].astype(F32)
                 outs[side][:, cols] = (mine.astype(F32) + add).astype(BF16)
             else:
-                add = came[0][:, cols].astype(F32) + came[1][:, cols].astype(F32)
-                outs[side][:, cols] = mine.astype(F32) + add
+                total = came[0][:, cols].astype(F32) + came[1][:, cols].astype(F32)
+                total += mine.astype(F32)
+                if split is None:
+                    outs[side][:, cols] = total
+                else:
+                    outer, inner = split
+                    size = total.shape[1] // (outer * inner)
+                    for at in range(outer * inner):
+                        to = pl.ds(at // inner * size, size)
+                        outs[side][at % inner, :, to] = total[:, at * size : (at + 1) * size]
 
 
 class RingSum:
@@ -163,7 +171,7 @@
         self.came = ()
         self.step()
 
-    def run(self, kind, step, wait=()):
+    def run(self, kind, step, wait=(), split=None):
         rows = self.wholes[0].shape[0] // self.n
         half = rows // 2
         widths = [v.shape[1] for v in self.wholes]
@@ -175,10 +183,13 @@
         else:
             sides = [(middle + step, 0, rows), (middle - step, 0, rows)]
         size = half if kind == "begin" else rows
-        out = ((size, sum(widths)), F32 if kind == "end" else BF16)
+        shape = (size, sum(widths))
+        if split is not None:
+            shape = (split[1], size, shape[1] // split[1])
+        out = (shape, F32 if kind == "end" else BF16)
         hbm = pl.BlockSpec(memory_space=pltpu.HBM)
         return call(
-            functools.partial(ring_body, kind, rows, len(widths), sides),
+            functools.partial(ring_body, kind, rows, len(widths), sides, split),
             (1,),
             (self.table, *self.wholes, *self.came),
             [pl.BlockSpec(memory_space=pltpu.SMEM)]
@@ -202,13 +213,17 @@
         self.came = (send_next(up, self.n), send_prev(down, self.n))
         self.left -= 1
 
-    def total(self):
+    def total(self, split=None):
         if self.direct:
             whole = jnp.concatenate(self.wholes, 1)
-            return lax.psum_scatter(whole, "fsdp", scatter_dimension=0, tiled=True).astype(F32)
+            total = lax.psum_scatter(whole, "fsdp", scatter_dimension=0, tiled=True).astype(F32)
+            if split is not None:
+                total = total.reshape(total.shape[0], *split, -1).transpose(2, 0, 1, 3)
+                total = total.reshape(*total.shape[:2], -1)
+            return total
         while self.left:
             self.step()
-        return self.run("end", 0)[0]
+        return self.run("end", 0, split=split)[0]
 
 
 def swap_fsdp(values, n, bit):
@@ -366,6 +381,26 @@
         [(shape, F32), (shape, BF16)],
         shifts=[0] * len(terms) + [None],
         wait=wait,
+    )
+
+
+def norm_pair_body(index, left_ref, right_ref, params, *outs):
+    gain, bias = params[index : index + 1, :], params[3 + index : 4 + index, :]
+    for ref, out in zip((left_ref, right_ref), outs):
+        stream = ref[...].astype(F32)
+        center = stream - jnp.mean(stream, axis=-1, keepdims=True)
+        spread = jnp.mean(center * center, axis=-1, keepdims=True)
+        out[...] = (center * lax.rsqrt(spread + EPSILON) * gain + bias).astype(BF16)
+
+
+def norm_pair(index, pair, params):
+    return tuple(
+        rows_call(
+            functools.partial(norm_pair_body, index),
+            (*pair, params),
+            [(v.shape, BF16) for v in pair],
+            shifts=[0, 0, None],
+        )
     )
 
 
@@ -872,20 +907,22 @@
     )
 
 
-def weight_grad_body(plan, lefts_count, *refs):
-    lefts, rights, out = refs[:lefts_count], refs[lefts_count:-1], refs[-1]
+def weight_grad_body(plan, lefts_count, rights_count, *refs):
+    lefts, rights = refs[:lefts_count], refs[lefts_count : lefts_count + rights_count]
+    outs = refs[lefts_count + rights_count :]
     begin = 0
     for pairs in plan:
-        cols = rights[pairs[0][1]].shape[1]
         total = 0.0
         for left, right, first in pairs:
             size = lefts[left].shape[0]
             total += t_times(lefts[left][...], rights[right][first : first + size, :])
-        out[:, begin : begin + cols] = total.astype(BF16)
+        cols = total.shape[1] // len(outs)
+        for k, out in enumerate(outs):
+            out[:, begin : begin + cols] = total[:, k * cols : (k + 1) * cols].astype(BF16)
         begin += cols
 
 
-def weight_grad(*parts):
+def weight_grad(*parts, split=1):
     lefts, rights, plan = [], [], []
     for part_lefts, part_rights in parts:
         pairs = []
@@ -899,17 +936,18 @@
         rights += part_rights
         plan.append(pairs)
     width = lefts[0].shape[1]
-    cols = sum(part_rights[0].shape[1] for _, part_rights in parts)
+    cols = sum(part_rights[0].shape[1] for _, part_rights in parts) // split
     size = 256 if width % 256 == 0 else width
-    return call(
-        functools.partial(weight_grad_body, plan, len(lefts)),
+    outs = call(
+        functools.partial(weight_grad_body, plan, len(lefts), len(rights)),
         (width // size,),
         (*lefts, *rights),
         [pl.BlockSpec((v.shape[0], size), lambda i: (0, i)) for v in lefts]
         + [whole_spec(v.shape) for v in rights],
-        [((width, cols), BF16)],
-        [pl.BlockSpec((size, cols), lambda i: (i, 0))],
-    )[0]
+        [((width, cols), BF16)] * split,
+        [pl.BlockSpec((size, cols), lambda i: (i, 0))] * split,
+    )
+    return outs[0] if split == 1 else outs
 
 
 def text_project_body(text_ref, weight_ref, out_ref):
@@ -981,26 +1019,26 @@
         for k in range(2)
     ]
 
-    rows_in = audio_states.reshape(clips * share, width)
-    cross_came, out_swapped[0] = self_ring.turn([cross_came, out_swapped[0]], params)
+    raw_swapped = [swap_chip(audio_states[c]) for c in both]
+    cross_came, raw_swapped[0] = self_ring.turn([cross_came, raw_swapped[0]], params)
     cross_shard = jnp.concatenate((cross_own, cross_came, cross_kv[0], cross_kv[1]), axis=1)
-    _, normed = norm_forward(0, (rows_in,), params, clips * share)
-    normed = [normed[c * share : (c + 1) * share] for c in both]
-    normed_swapped = [swap_chip(v) for v in normed]
-    full_self = [gather_rows(normed[0], normed_swapped[0])]
-    self_ring.step()
-    cross_ring = RingGather(hold(cross_shard, self_ring.step()), n)
-    got = cross_ring.step()
-    self_w = self_ring.whole(wait=normed_swapped[1:])
-    full_self += [gather_rows(normed[c], normed_swapped[c]) for c in range(1, clips)]
-    seen_out = [gather_rows(out_grad[0], out_swapped[0])]
+    raw = gather_rows(audio_states[0], raw_swapped[0])
+    full_self = [norm_pair(0, raw, params)]
+    self_ring.turn()
+    raw_swapped[1:] = self_ring.turn(raw_swapped[1:])
+    raw = [gather_rows(audio_states[c], raw_swapped[c]) for c in range(1, clips)]
+    full_self += [norm_pair(0, v, params) for v in raw]
+    cross_ring = RingGather(hold(cross_shard, self_ring.got[-1] if self_ring.got else ()), n)
+    cross_ring.step()
+    self_w = self_ring.whole()
     text_pair = jnp.concatenate((text_states, swap_chip(text_states)), axis=1)
     text_full = jnp.concatenate((text_pair, swap_core(text_pair)), axis=1)
     qkv, self_attn, self_log, mid_terms = [], [], [], []
     for c in both:
         rows, attn, log, keep, send = self_forward(*full_self[c], self_w, units)
         if c == 0:
-            (send,) = cross_ring.turn([send])
+            send, *out_swapped = cross_ring.turn([send, *out_swapped])
+            seen_out = [gather_rows(out_grad[k], out_swapped[k]) for k in both]
         else:
             keep_0, seen_0, other_0 = mid_terms[0][1:]
             send, other_0 = cross_ring.turn([send, other_0])
@@ -1014,15 +1052,14 @@
         stream, normed = norm_forward(1, mid_terms[c], params, share)
         stream_mid.append(stream)
         cross_rows.append((normed, swap_core(normed)))
-    cross_ring.turn()
+        if c == 0:
+            cross_ring.turn()
     early_gather = RingGather(hold(ffn_shards[0], cross_ring.got[-1] if cross_ring.got else ()), n)
     early_gather.step()
-    cross_w = cross_ring.whole(wait=out_swapped[1:])
-    seen_out += [gather_rows(out_grad[c], out_swapped[c]) for c in range(1, clips)]
+    cross_w = cross_ring.whole()
     text_rows = text_full.reshape(-1, width)
     text_kv = text_project(text_rows, cross_w, 2, 2 * units).reshape(clips, -1, 2 * units)
-    text_other = swap_chip(text_kv)
-    early_gather.turn()
+    (text_other,) = early_gather.turn([swap_chip(text_kv)])
     cross_q, cross_attn, stream_late, full_ffn = [], [], [], []
     for c in both:
         queries, attn, keep, send = cross_forward(
@@ -1031,13 +1068,13 @@
         if c:
             send, came = early_gather.turn([send, came])
             full_ffn.append(gather_rows(normed_late, came))
+        else:
+            (send,) = early_gather.turn([send])
         cross_q.append(queries)
         cross_attn.append(attn)
         stream, normed = norm_forward(2, (stream_mid[c], keep, swap_core(send)), params, share)
         stream_late.append(stream)
         normed_late, came = normed, swap_chip(normed)
-        if c == 0:
-            early_gather.turn()
     late_gather = RingGather(hold(ffn_shards[1], early_gather.got[-1] if early_gather.got else ()), n)
     late_gather.step()
     early_w = early_gather.whole()
@@ -1046,20 +1083,21 @@
     for c in both:
         active, hidden, *partial = ffn(full_ffn[c], seen_out[c], early_w)
         if c == 0:
-            active, came = late_gather.turn([active, came])
+            (came,) = late_gather.turn([came])
             full_ffn.append(gather_rows(normed_late, came))
         else:
-            (active,) = late_gather.turn([active])
+            late_gather.turn()
         actives[0].append(active)
         hiddens[0].append(hidden)
         partials.append(partial)
     grad = weight_grad((sum(full_ffn, ()), hiddens[0]), (sum(seen_out, ()), actives[0]))
-    (grad,) = late_gather.turn([grad])
+    late_gather.turn()
     late_w = late_gather.whole()
 
     def sum_clips(grad):
         return lax.psum_scatter(grad, "fsdp", scatter_dimension=0, tiled=True)
 
+    (grad,) = tick([grad])
     ffn_totals = [sum_clips(grad)]
     back_terms, out_terms = [], []
     for c in both:
@@ -1112,14 +1150,12 @@
             late_back(c + 1)
         mid_back(c)
     kv_came = swap_chip(jnp.stack(other_kv))
-    wide = weight_grad((sum(cross_rows, ()), cross_grads), (sum(seen_mid, ()), cross_attn))
-    wide, came = tick([wide, branches[0][1]])
+    cross_shares = weight_grad(
+        (sum(cross_rows, ()), cross_grads), (sum(seen_mid, ()), cross_attn), split=2
+    )
+    (came,) = tick([branches[0][1]])
     seen_in = [gather_rows(branches[0][0], came)]
     seen_in += [gather_rows(*branches[c]) for c in range(1, clips)]
-    cross_shares = [
-        jnp.concatenate([wide[:, k * units : (k + 1) * units] for k in (first, first + 2)], 1)
-        for first in range(2)
-    ]
     cross_came = swap_chip(cross_shares[1])
 
     self_grads, in_terms, out_sums = [], [], []
@@ -1130,27 +1166,23 @@
         if c == 0:
             send, kv_came = tick([send, kv_came])
         else:
-            send, cross_came, text_came = tick([send, cross_came, text_came], *out_sum.came)
-            out_sum.step()
+            send, cross_came, text_came = tick([send, cross_came, text_came])
         in_terms.append(sum_over_tp(keep, send))
         self_grads.append(grads)
         if c == 0:
             kv_grads = (jnp.stack(own_kv) + kv_came.astype(F32)).astype(BF16)
             kv_rows = kv_grads.reshape(-1, 2 * units)
             grad = weight_grad((sum(seen_in, ()), self_attn), ([text_rows], [kv_rows]))
-            out_sum = RingSum([grad], n, table)
+            out_total = sum_clips(grad)
             text_keep, text_send = text_back(kv_rows, cross_w, 2, clips)
             quarter = text_keep.shape[1] // 2
             text_seen = text_keep + swap_core(text_send).astype(F32)
             text_came = swap_chip(text_seen[:, quarter:].astype(BF16))
         else:
-            cross_total = sum_clips(
-                (cross_shares[0].astype(F32) + cross_came.astype(F32)).astype(BF16)
-            )
+            cross_total = sum_clips(sum_terms((cross_shares[0], cross_came), cross_came.shape))
     text_grad = text_seen[:, :quarter] + text_came.astype(F32)
     grad = weight_grad((sum(full_self, ()), self_grads))
     qkv_sum = RingSum([grad], n, table)
-    out_sum.step()
     late_terms = [sum_over_tp(*out_terms[c]) for c in both]
     audio_grad, layer_out = [], []
     for c in both:
@@ -1159,40 +1191,37 @@
         audio_grad.append(grad)
         if c == 0:
             qkv_sum.step()
-            out_sum.step()
-    norm_total = SmallSum(jnp.concatenate([sum(v) for v in norm_sums], 0), n)
+    norm_total = SmallSum(jnp.concatenate([sum(v)[:2] for v in norm_sums], 0), n)
     audio_grad = join(audio_grad)
+    qkv_sum.step()
     norm_total.step()
     norm_total.step()
-    qkv_sum.step()
-    out_total = out_sum.total()
+    layer_out.append(sum_terms((stream_late[0], *late_terms[0]), (share, width)))
+    qkv_sum.step([out_total])
     norm_total.step()
-    layer_out.append(sum_terms((stream_late[0], *late_terms[0]), (share, width)))
     norm_total.step()
-    qkv_sum.step()
     for c in range(1, clips):
         layer_out.append(sum_terms((stream_late[c], *late_terms[c]), (share, width)))
     layer_out = join(layer_out)
+    qkv_total = qkv_sum.total(split=(pairs, 3))
     norm_total = norm_total.total()
-    qkv_total = qkv_sum.total()
 
     def cut(total, begin, count=1):
         return total[:, begin * units : (begin + count) * units]
 
-    qkv_total = qkv_total.reshape(-1, pairs, 3, PAIR).transpose(2, 0, 1, 3)
     return (
         layer_out,
         audio_grad,
         text_grad.astype(BF16),
-        qkv_total.reshape(3, -1, units),
-        cut(out_total, 0).T,
+        qkv_total,
+        cut(out_total, 0).astype(F32).T,
         cut(cross_total, 0).astype(F32),
-        jnp.stack((cut(out_total, 1), cut(out_total, 2))),
+        jnp.stack((cut(out_total, 1), cut(out_total, 2))).astype(F32),
         cut(cross_total, 1).astype(F32).T,
         jnp.concatenate([v[:, :part] for v in ffn_totals], 1).astype(F32),
         jnp.concatenate([v[:, part:] for v in ffn_totals], 1).astype(F32).T,
-        norm_total[0::8],
-        norm_total[1::8],
+        norm_total[0::2],
+        norm_total[1::2],
     )
 
 

time: 782 us -> 742 us (0.949)
  local copies, waits for them, and re-layouts: 120 us -> 55.7 us
  Pallas kernels: 333 us -> 394 us
  waiting for transfers between devices: 199 us -> 176 us
  starting transfers between devices: 86.7 us -> 74.3 us
    pallas_call x79, Pallas kernels: 333 us -> 394 us  [call(): pl.pallas_call(run, grid=grid, in_specs=list(in_specs) + [hbm] * len(wait...]
    unnamed x486 -> x240, local copies, waits for them, and re-layouts: 101 us -> 42.7 us
    ppermute x24 -> x20, waiting for transfers between devices: 65.2 us -> 40.2 us  [send_next(): lax.ppermute(values, 'fsdp', [(ring[k], ring[(k + 1) % n]) for k in range...]
    ppermute x24 -> x20, waiting for transfers between devices: 43.9 us -> 21.6 us  [send_prev(): lax.ppermute(values, 'fsdp', [(ring[(k + 1) % n], ring[k]) for k in range...]
    reduce_scatter x3 -> x4, waiting for transfers between devices: 0.01 us -> 19.4 us  [sum_clips(): return lax.psum_scatter(grad, 'fsdp', scatter_dimension=0, tiled=True)]
    ppermute x24 -> x20, starting transfers between devices: 43.6 us -> 28.2 us  [send_next(): lax.ppermute(values, 'fsdp', [(ring[k], ring[(k + 1) % n]) for k in range...]
    ppermute x27, waiting for transfers between devices: 12.6 us -> 25 us  [swap_core(): return lax.ppermute(values, 'tp', [(t, t ^ 1) for t in range(4)])]
  transfers between devices with their start and end apart: 107 -> 100, of which waited for: 44 -> 45; matrix products, arithmetic and copies ran while one was open for 4% -> 3% of each run, Pallas kernels for 42% -> 53%
where the time goes in v2:
time: 742 us; the launch traced here: 732 us
  Pallas kernels  394 us (53%)
  waiting for transfers between devices  176 us (24%)
  starting transfers between devices  74.3 us (10%)
  local copies, waits for them, and re-layouts  55.7 us (8%)
  other arithmetic  15.9 us (2%)
  between operations  15.7 us (2%)
    pallas_call x79, Pallas kernels, call(): pl.pallas_call(run, grid=grid, in_specs=list(in_specs) + [hbm] * len(wait...  394 us
    ppermute x23, waiting for transfers between devices, swap_chip(): return lax.ppermute(values, 'tp', [(t, t ^ 2) for t in range(4)])  50.5 us
    unnamed x240, local copies, waits for them, and re-layouts  42.7 us
    ppermute x20, waiting for transfers between devices, send_next(): lax.ppermute(values, 'fsdp', [(ring[k], ring[(k + 1) % n]) for k in range...  40.2 us
    ppermute x20, starting transfers between devices, send_next(): lax.ppermute(values, 'fsdp', [(ring[k], ring[(k + 1) % n]) for k in range...  28.2 us
    ppermute x27, waiting for transfers between devices, swap_core(): return lax.ppermute(values, 'tp', [(t, t ^ 1) for t in range(4)])  25 us
    ppermute x23, starting transfers between devices, swap_chip(): return lax.ppermute(values, 'tp', [(t, t ^ 2) for t in range(4)])  22.3 us
    ppermute x20, waiting for transfers between devices, send_prev(): lax.ppermute(values, 'fsdp', [(ring[(k + 1) % n], ring[k]) for k in range...  21.6 us
  transfers between devices with their start and end apart: 100, of which 45 were waited for; matrix products, arithmetic and copies ran while one was open for 3% of the time, Pallas kernels for 53%

profile of v2, /device:TPU:0, one launch (start us, length us, event | category | flops | bytes accessed | tf_op | source)
XLA Modules:
  0.0 731.9 jit_solution(11889692493930830094)
XLA Ops:
  18.7 10.0 %collective-permute-done.4 = bf16[1,6,192]{2,1,0:T(8,128)(2,1)S(1)} collective-permute-done((bf16[1,6,192]{2,1,0:T(8,128)(2,1)S(1)}, bf16[1,6,192]{2,1,0:T(8,128)(2,1)S(1)}, u32[]{:S(2)}, u32[]{:S(2)}) %collective-permute-start.4) | collective-permute-done | bytes 2336 | tf_op jit(solution)/shard_map/ppermute | solution.py:230
  47.8 4.7 norm_pair_body.2
  53.7 5.1 collective-permute-done.8.refs_0_
  64.5 10.2 %collective-permute-done.10.refs_0_ = bf16[192,1536]{1,0:T(8,128)(2,1)S(1)} collective-permute-done((bf16[192,1536]{1,0:T(8,128)(2,1)S(1)}, bf16[192,1536]{1,0:T(8,128)(2,1)S(1)}, u32[]{:S(2)}, u32[]{:S(2)}) %collective-permute-start.10) | collective-permute-done | bytes 589856 | tf_op jit(solution)/shard_map/ppermute | solution.py:56
  80.8 4.7 norm_pair_body.3
  97.4 22.6 %self_forward_body.2 = (bf16[1024,1152]{1,0:T(8,128)(2,1)}, bf16[1024,384]{1,0:T(8,128)(2,1)S(1)}, f32[24,1024]{1,0:T(8,128)S(1)}, f32[512,1536]{1,0:T(8,128)}, ...) custom-call(bf16[512,1536]{1,0:T(8,128)(2,1)} %copy-done.7, bf16[512,1536]{1,0:T(8,128)(2,1)} %get-tuple-element.265.refs_1_, ...), custom_call_target="tpu_custom_call" | custom-call | flops 1000 | tf_op jit(solution)/shard_map/self_forward_body/pallas_call | solution.py:275
  120.9 6.5 collective-permute-done.18.refs_3_
  136.7 22.4 %self_forward_body.3 = (bf16[1024,1152]{1,0:T(8,128)(2,1)}, bf16[1024,384]{1,0:T(8,128)(2,1)S(1)}, f32[24,1024]{1,0:T(8,128)S(1)}, f32[512,1536]{1,0:T(8,128)}, ...) custom-call(bf16[512,1536]{1,0:T(8,128)(2,1)} %copy-done.9, bf16[512,1536]{1,0:T(8,128)(2,1)} %get-tuple-element.289.refs_1_.refs_3_, ...), custom_call_target="tpu_custom_call" | custom-call | flops 1000 | tf_op jit(solution)/shard_map/self_forward_body/pallas_call | solution.py:275
  172.6 9.5 %collective-permute-done.26.refs_0_ = bf16[192,2304]{1,0:T(8,128)(2,1)S(1)} collective-permute-done((bf16[192,2304]{1,0:T(8,128)(2,1)S(1)}, bf16[192,2304]{1,0:T(8,128)(2,1)S(1)}, u32[]{:S(2)}, u32[]{:S(2)}) %collective-permute-start.26) | collective-permute-done | bytes 884768 | tf_op jit(solution)/shard_map/ppermute | solution.py:56
  199.5 6.3 place_pieces_body.5
  208.6 5.1 collective-permute-done.35.refs_2_
  217.5 10.3 %cross_forward_body.2 = (bf16[512,768]{1,0:T(8,128)(2,1)S(1)}, bf16[512,768]{1,0:T(8,128)(2,1)S(1)}, f32[256,1536]{1,0:T(8,128)}, bf16[256,1536]{1,0:T(8,128)(2,1)}, f32[8,128]{1,0:T(8,128)S(1)}) custom-call(bf16[256,1536]{1,0:T(8,128)(2,1)} %copy-done.28, bf16[256,1536]{1,0:T(8,128)(2,1)} %copy-done.31, ...), custom_call_target="tpu_custom_call" | custom-call | flops 1000 | tf_op jit(solution)/shard_map/cross_forward_body/pallas_call | solution.py:275
  239.9 10.3 %cross_forward_body.3 = (bf16[512,768]{1,0:T(8,128)(2,1)S(1)}, bf16[512,768]{1,0:T(8,128)(2,1)S(1)}, f32[256,1536]{1,0:T(8,128)}, bf16[256,1536]{1,0:T(8,128)(2,1)}, f32[8,128]{1,0:T(8,128)S(1)}) custom-call(bf16[256,1536]{1,0:T(8,128)(2,1)} %copy-done.30, bf16[256,1536]{1,0:T(8,128)(2,1)} %copy-done.92, ...), custom_call_target="tpu_custom_call" | custom-call | flops 1000 | tf_op jit(solution)/shard_map/cross_forward_body/pallas_call | solution.py:275
  277.2 16.5 %ffn_first_body.2 = (bf16[1024,768]{1,0:T(8,128)(2,1)S(1)}, bf16[1024,768]{1,0:T(8,128)(2,1)}, f32[1024,1536]{1,0:T(8,128)}, f32[1024,1536]{1,0:T(8,128)}, f32[8,128]{1,0:T(8,128)S(1)}) custom-call(bf16[512,1536]{1,0:T(8,128)(2,1)} %copy-done, bf16[512,1536]{1,0:T(8,128)(2,1)} %collective-permute-done.43.refs_1_, bf16[512,1536]{1,0:T(8,128)(2,1)} %copy-done.71, ...), custom_call_target="tpu_custom_call" | custom-call | flops 1000 | tf_op jit(solution)/shard_map/ffn_first_body/pallas_call | solution.py:275
  300.8 16.6 %ffn_first_body.3 = (bf16[1024,768]{1,0:T(8,128)(2,1)S(1)}, bf16[1024,768]{1,0:T(8,128)(2,1)}, f32[1024,1536]{1,0:T(8,128)}, f32[1024,1536]{1,0:T(8,128)}, f32[8,128]{1,0:T(8,128)S(1)}) custom-call(bf16[512,1536]{1,0:T(8,128)(2,1)} %copy-done.74, bf16[512,1536]{1,0:T(8,128)(2,1)} %copy-done.75, bf16[512,1536]{1,0:T(8,128)(2,1)} %pad_maximum_fusion.3.refs_2_.refs_6_, ...), custom_call_target="tpu_custom_call" | custom-call | flops 1000 | tf_op jit(solution)/shard_map/ffn_first_body/pallas_call | solution.py:275
  320.8 15.7 %weight_grad_body.5 = (bf16[1536,1536]{1,0:T(8,128)(2,1)}, f32[8,128]{1,0:T(8,128)S(1)}) custom-call(bf16[512,1536]{1,0:T(8,128)(2,1)S(1)} %copy-done.1, bf16[512,1536]{1,0:T(8,128)(2,1)} %collective-permute-done.43.refs_1_, bf16[512,1536]{1,0:T(8,128)(2,1)} %copy-done.74, bf16[512,1536]{1,0:T(8,128)(2,1)} %copy-done.75, bf16[512,1536]{1,0:T(8,128)(2,1)} %copy-done.71, ...), custom_call_target="tpu_custom_call" | custom-call | flops 1000 | tf_op jit(solution)/shard_map/weight_grad_body/pallas_call | solution.py:275
  338.7 6.7 collective-permute-done.58.refs_8_
  349.4 19.1 %ffn_second_body.2 = (bf16[1024,768]{1,0:T(8,128)(2,1)S(1)}, bf16[1024,768]{1,0:T(8,128)(2,1)}, f32[512,1536]{1,0:T(8,128)}, bf16[512,1536]{1,0:T(8,128)(2,1)}, ...) custom-call(bf16[512,1536]{1,0:T(8,128)(2,1)} %copy-done, ...), custom_call_target="tpu_custom_call" | custom-call | flops 1000 | tf_op jit(solution)/shard_map/ffn_second_body/pallas_call | solution.py:275
  376.7 19.4 %ffn_second_body.3 = (bf16[1024,768]{1,0:T(8,128)(2,1)S(1)}, bf16[1024,768]{1,0:T(8,128)(2,1)}, f32[512,1536]{1,0:T(8,128)}, bf16[512,1536]{1,0:T(8,128)(2,1)}, ...) custom-call(bf16[512,1536]{1,0:T(8,128)(2,1)} %copy-done.74, bf16[512,1536]{1,0:T(8,128)(2,1)} %copy-done.75, ...), custom_call_target="tpu_custom_call" | custom-call | flops 1000 | tf_op jit(solution)/shard_map/ffn_second_body/pallas_call | solution.py:275
  409.7 16.0 %weight_grad_body.6 = (bf16[1536,1536]{1,0:T(8,128)(2,1)}, f32[8,128]{1,0:T(8,128)S(1)}) custom-call(bf16[512,1536]{1,0:T(8,128)(2,1)S(1)} %copy-done.2, bf16[512,1536]{1,0:T(8,128)(2,1)} %collective-permute-done.43.refs_1_, bf16[512,1536]{1,0:T(8,128)(2,1)} %copy-done.74, bf16[512,1536]{1,0:T(8,128)(2,1)} %copy-done.75, bf16[512,1536]{1,0:T(8,128)(2,1)} %copy-done.71, ...), custom_call_target="tpu_custom_call" | custom-call | flops 1000 | tf_op jit(solution)/shard_map/weight_grad_body/pallas_call | solution.py:275
  431.2 11.4 %cross_backward_body.2 = (bf16[512,768]{1,0:T(8,128)(2,1)S(1)}, f32[64,768]{1,0:T(8,128)S(1)}, bf16[64,768]{1,0:T(8,128)(2,1)S(1)}, f32[256,1536]{1,0:T(8,128)},...) custom-call(bf16[256,1536]{1,0:T(8,128)(2,1)} %copy-done.33, bf16[256,1536]{1,0:T(8,128)(2,1)} %copy-done.93, ...), custom_call_target="tpu_custom_call" | custom-call | flops 1000 | tf_op jit(solution)/shard_map/cross_backward_body/pallas_call | solution.py:275
  452.1 11.5 %cross_backward_body.3 = (bf16[512,768]{1,0:T(8,128)(2,1)S(1)}, f32[64,768]{1,0:T(8,128)S(1)}, bf16[64,768]{1,0:T(8,128)(2,1)S(1)}, f32[256,1536]{1,0:T(8,128)},...) custom-call(bf16[256,1536]{1,0:T(8,128)(2,1)} %copy-done.34, bf16[256,1536]{1,0:T(8,128)(2,1)} %copy-done.94, ...), custom_call_target="tpu_custom_call" | custom-call | flops 1000 | tf_op jit(solution)/shard_map/cross_backward_body/pallas_call | solution.py:275
  470.1 10.1 %weight_grad_body.7 = (bf16[1536,768]{1,0:T(8,128)(2,1)}, bf16[1536,768]{1,0:T(8,128)(2,1)}, f32[8,128]{1,0:T(8,128)S(1)}) custom-call(bf16[256,1536]{1,0:T(8,128)(2,1)S(1)} %copy-done.29, bf16[256,1536]{1,0:T(8,128)(2,1)S(1)} %copy-done.32, bf16[256,1536]{1,0:T(8,128)(2,1)} %copy-done.30, bf16[256,1536]{1,0:T(8,128)(2,1)} %copy-done.92, ...), custom_call_target="tpu_custom_call" | custom-call | flops 1000 | tf_op jit(solution)/shard_map/weight_grad_body/pallas_call | solution.py:275
  488.3 28.5 %self_backward_body.2 = (bf16[1024,1152]{1,0:T(8,128)(2,1)}, f32[512,1536]{1,0:T(8,128)}, bf16[512,1536]{1,0:T(8,128)(2,1)}, f32[8,128]{1,0:T(8,128)S(1)}) custom-call(bf16[512,1536]{1,0:T(8,128)(2,1)} %copy-done.76, bf16[512,1536]{1,0:T(8,128)(2,1)} %copy-done.88, bf16[1536,1536]{1,0:T(8,128)(2,1)} %get-tuple-element.279.refs_2_.refs_3_, ...), custom_call_target="tpu_custom_call" | custom-call | flops 1000 | tf_op jit(solution)/shard_map/self_backward_body/pallas_call | solution.py:275
  525.7 8.8 %weight_grad_body.8 = (bf16[1536,1152]{1,0:T(8,128)(2,1)}, f32[8,128]{1,0:T(8,128)S(1)}) custom-call(bf16[512,1536]{1,0:T(8,128)(2,1)} %copy-done.76, bf16[512,1536]{1,0:T(8,128)(2,1)} %copy-done.88, bf16[512,1536]{1,0:T(8,128)(2,1)} %copy-done.77, bf16[512,1536]{1,0:T(8,128)(2,1)} %copy-done.87, bf16[128,1536]{1,0:T(8,128)(2,1)S(1)} %bitcast.45, ...), custom_call_target="tpu_custom_call" | custom-call | flops 1000 | tf_op jit(solution)/shard_map/weight_grad_body/pallas_call | solution.py:275
  541.0 28.6 %self_backward_body.3 = (bf16[1024,1152]{1,0:T(8,128)(2,1)}, f32[512,1536]{1,0:T(8,128)}, bf16[512,1536]{1,0:T(8,128)(2,1)}, f32[8,128]{1,0:T(8,128)S(1)}) custom-call(bf16[512,1536]{1,0:T(8,128)(2,1)} %copy-done.77, bf16[512,1536]{1,0:T(8,128)(2,1)} %copy-done.87, bf16[1536,1536]{1,0:T(8,128)(2,1)} %get-tuple-element.279.refs_2_.refs_3_, ...), custom_call_target="tpu_custom_call" | custom-call | flops 1000 | tf_op jit(solution)/shard_map/self_backward_body/pallas_call | solution.py:275
  569.5 19.4 %collective-permute-done.74.refs_1_ = bf16[1536,768]{1,0:T(8,128)(2,1)S(1)} collective-permute-done((bf16[1536,768]{1,0:T(8,128)(2,1)}, bf16[1536,768]{1,0:T(8,128)(2,1)S(1)}, u32[]{:S(2)}, u32[]{:S(2)}) %collective-permute-start.74) | collective-permute-done | bytes 2359328 | tf_op jit(solution)/shard_map/ppermute | solution.py:23
  598.1 8.7 %sum_terms_body.3 = (bf16[1536,768]{1,0:T(8,128)(2,1)}, f32[8,128]{1,0:T(8,128)S(1)}) custom-call(bf16[1536,768]{1,0:T(8,128)(2,1)} %get-tuple-element.442.refs_0_, bf16[1536,768]{1,0:T(8,128)(2,1)} %get-tuple-element.448.refs_1_, f32[8,128]{1,0:T(8,128)S(1)} %get-tuple-element.452.refs_2_), custom_call_target="tpu_custom_call" | custom-call | flops 1000 | tf_op jit(solution)/shard_map/sum_terms_body/pallas_call | solution.py:275
  609.4 13.1 %weight_grad_body.9 = (bf16[1536,1152]{1,0:T(8,128)(2,1)}, f32[8,128]{1,0:T(8,128)S(1)}) custom-call(bf16[512,1536]{1,0:T(8,128)(2,1)S(1)} %copy-done.8, bf16[512,1536]{1,0:T(8,128)(2,1)} %get-tuple-element.265.refs_1_, bf16[512,1536]{1,0:T(8,128)(2,1)} %copy-done.9, bf16[512,1536]{1,0:T(8,128)(2,1)} %get-tuple-element.289.refs_1_.refs_3_, ...), custom_call_target="tpu_custom_call" | custom-call | flops 1000 | tf_op jit(solution)/shard_map/weight_grad_body/pallas_call | solution.py:275
  652.5 7.6 %collective-permute-done.85.refs_2_ = bf16[192,1152]{1,0:T(8,128)(2,1)} collective-permute-done((bf16[192,1152]{1,0:T(8,128)(2,1)}, bf16[192,1152]{1,0:T(8,128)(2,1)}, u32[]{:S(2)}, u32[]{:S(2)}) %collective-permute-start.85) | collective-permute-done | bytes 442400 | tf_op jit(solution)/shard_map/ppermute | solution.py:56
  678.9 5.8 collective-permute-done.90.refs_2_
  689.6 19.3 %reduce-scatter.7.cloned.1.call-done = bf16[192,768]{1,0:T(8,128)(2,1)} async-done(((bf16[1536,768]{1,0:T(8,128)(2,1)}), bf16[192,768]{1,0:T(8,128)(2,1)}) %reduce-scatter.7.cloned.1.call-update) | async-done | bytes 294928 | tf_op jit(solution)/shard_map/reduce_scatter | solution.py:1098
  (553 shorter events, 305.5 us)
Async XLA Ops:
  7.2 642.2 %reduce-scatter.9.cloned.1.call-start = ((), (), s32[]{:S(2)}) async-start(), calls=%async_computation.6 | async-start | bytes 5308416 | tf_op jit(solution)/shard_map/reduce_scatter | solution.py:1098
  10.6 27.2 %collective-permute-start.1 = (bf16[192,1536]{1,0:T(8,128)(2,1)}, bf16[192,1536]{1,0:T(8,128)(2,1)S(1)}, u32[]{:S(2)}, u32[]{:S(2)}) collective-permute-start(bf16[192,1536]{1,0:T(8,128)(2,1)} %pad_maximum_fusion.4.refs_0_), channel_id=1, source_target_pairs={{8,0},{16,8},{24,16},{28,24},{20,28},{12,20},{4,12},{0,4},{9,1},{1... | collective-permute-start | bytes 1769480 | tf_op jit(solution)/shard_map/ppermute | solution.py:61
  13.6 24.2 %collective-permute-start = (bf16[192,1536]{1,0:T(8,128)(2,1)}, bf16[192,1536]{1,0:T(8,128)(2,1)S(1)}, u32[]{:S(2)}, u32[]{:S(2)}) collective-permute-start(bf16[192,1536]{1,0:T(8,128)(2,1)} %pad_maximum_fusion.4.refs_0_), channel_id=1, source_target_pairs={{0,8},{8,16},{16,24},{24,28},{28,20},{20,12},{12,4},{4,0},{1,9},{9... | collective-permute-start | bytes 1769480 | tf_op jit(solution)/shard_map/ppermute | solution.py:56
  18.1 23.5 %collective-permute-start.3 = (bf16[256,1536]{1,0:T(8,128)(2,1)S(1)}, bf16[256,1536]{1,0:T(8,128)(2,1)}, u32[]{:S(2)}, u32[]{:S(2)}) collective-permute-start(bf16[256,1536]{1,0:T(8,128)(2,1)S(1)} %get-tuple-element.515.refs_0_), channel_id=1, source_target_pairs={{0,2},{1,3},{2,0},{3,1},{4,6},{5,7},{6,4},{7,5},{8,10},{9,11},{10,... | collective-permute-start | bytes 2359304 | tf_op jit(solution)/shard_map/ppermute | solution.py:23
  87.9 39.5 %collective-permute-start.17 = (bf16[192,2304]{1,0:T(8,128)(2,1)S(1)}, bf16[192,2304]{1,0:T(8,128)(2,1)S(1)}, u32[]{:S(2)}, u32[]{:S(2)}) collective-permute-start(bf16[192,2304]{1,0:T(8,128)(2,1)S(1)} %get-tuple-element.282.refs_0_), channel_id=1, source_target_pairs={{8,0},{16,8},{24,16},{28,24},{20,28},{12,20},{4,12},{0,4},{9,1},{1... | collective-permute-start | bytes 2654216 | tf_op jit(solution)/shard_map/ppermute | solution.py:61
  88.4 39.0 %collective-permute-start.16 = (bf16[192,2304]{1,0:T(8,128)(2,1)S(1)}, bf16[192,2304]{1,0:T(8,128)(2,1)S(1)}, u32[]{:S(2)}, u32[]{:S(2)}) collective-permute-start(bf16[192,2304]{1,0:T(8,128)(2,1)S(1)} %get-tuple-element.282.refs_0_), channel_id=1, source_target_pairs={{0,8},{8,16},{16,24},{24,28},{28,20},{20,12},{12,4},{4,0},{1,9},{9... | collective-permute-start | bytes 2654216 | tf_op jit(solution)/shard_map/ppermute | solution.py:56
  91.5 29.4 %collective-permute-start.19 = (bf16[256,1536]{1,0:T(8,128)(2,1)S(1)}, bf16[256,1536]{1,0:T(8,128)(2,1)S(1)}, u32[]{:S(2)}, u32[]{:S(2)}) collective-permute-start(bf16[256,1536]{1,0:T(8,128)(2,1)S(1)} %get-tuple-element.512.refs_1_), channel_id=1, source_target_pairs={{0,2},{1,3},{2,0},{3,1},{4,6},{5,7},{6,4},{7,5},{8,10},{9,11},{10,... | collective-permute-start | bytes 2359304 | tf_op jit(solution)/shard_map/ppermute | solution.py:23
  93.1 34.4 %collective-permute-start.18 = (bf16[256,1536]{1,0:T(8,128)(2,1)S(1)}, bf16[256,1536]{1,0:T(8,128)(2,1)S(1)}, u32[]{:S(2)}, u32[]{:S(2)}) collective-permute-start(bf16[256,1536]{1,0:T(8,128)(2,1)S(1)} %get-tuple-element.513.refs_1_), channel_id=1, source_target_pairs={{0,2},{1,3},{2,0},{3,1},{4,6},{5,7},{6,4},{7,5},{8,10},{9,11},{10,... | collective-permute-start | bytes 2359304 | tf_op jit(solution)/shard_map/ppermute | solution.py:23
  128.7 30.4 %collective-permute-start.21 = (bf16[192,2304]{1,0:T(8,128)(2,1)}, bf16[192,2304]{1,0:T(8,128)(2,1)S(1)}, u32[]{:S(2)}, u32[]{:S(2)}) collective-permute-start(bf16[192,2304]{1,0:T(8,128)(2,1)} %get-tuple-element.286.refs_1_), channel_id=1, source_target_pairs={{0,8},{8,16},{16,24},{24,28},{28,20},{20,12},{12,4},{4,0},{1,9},{9... | collective-permute-start | bytes 2654216 | tf_op jit(solution)/shard_map/ppermute | solution.py:56
  130.3 28.8 %collective-permute-start.22 = (bf16[192,2304]{1,0:T(8,128)(2,1)}, bf16[192,2304]{1,0:T(8,128)(2,1)}, u32[]{:S(2)}, u32[]{:S(2)}) collective-permute-start(bf16[192,2304]{1,0:T(8,128)(2,1)} %get-tuple-element.287.refs_2_), channel_id=1, source_target_pairs={{8,0},{16,8},{24,16},{28,24},{20,28},{12,20},{4,12},{0,4},{9,1},{1... | collective-permute-start | bytes 2654216 | tf_op jit(solution)/shard_map/ppermute | solution.py:61
  135.1 24.0 %collective-permute-start.23 = (bf16[256,1536]{1,0:T(8,128)(2,1)S(1)}, bf16[256,1536]{1,0:T(8,128)(2,1)S(1)}, u32[]{:S(2)}, u32[]{:S(2)}) collective-permute-start(bf16[256,1536]{1,0:T(8,128)(2,1)S(1)} %get-tuple-element.293), channel_id=1, source_target_pairs={{0,2},{1,3},{2,0},{3,1},{4,6},{5,7},{6,4},{7,5},{8,10},{9,11},{10,... | collective-permute-start | bytes 2359304 | tf_op jit(solution)/shard_map/ppermute | solution.py:23
  166.6 22.7 %collective-permute-start.30 = (bf16[256,1536]{1,0:T(8,128)(2,1)S(1)}, bf16[256,1536]{1,0:T(8,128)(2,1)S(1)}, u32[]{:S(2)}, u32[]{:S(2)}) collective-permute-start(bf16[256,1536]{1,0:T(8,128)(2,1)S(1)} %get-tuple-element.307), channel_id=1, source_target_pairs={{0,2},{1,3},{2,0},{3,1},{4,6},{5,7},{6,4},{7,5},{8,10},{9,11},{10,... | collective-permute-start | bytes 2359304 | tf_op jit(solution)/shard_map/ppermute | solution.py:23
  238.8 37.7 %collective-permute-start.44 = (bf16[512,1536]{1,0:T(8,128)(2,1)S(1)}, bf16[512,1536]{1,0:T(8,128)(2,1)}, u32[]{:S(2)}, u32[]{:S(2)}) collective-permute-start(bf16[512,1536]{1,0:T(8,128)(2,1)S(1)} %pad_maximum_fusion.2.refs_2_.refs_4_), channel_id=1, source_target_pairs={{0,1},{1,0},{2,3},{3,2},{4,5},{5,4},{6,7},{7,6},{8,9},{9,8},{10,11... | collective-permute-start | bytes 4718600 | tf_op jit(solution)/shard_map/ppermute | solution.py:27
  263.4 30.4 %collective-permute-start.50 = (bf16[256,1536]{1,0:T(8,128)(2,1)S(1)}, bf16[256,1536]{1,0:T(8,128)(2,1)S(1)}, u32[]{:S(2)}, u32[]{:S(2)}) collective-permute-start(bf16[256,1536]{1,0:T(8,128)(2,1)S(1)} %get-tuple-element.343), channel_id=1, source_target_pairs={{0,2},{1,3},{2,0},{3,1},{4,6},{5,7},{6,4},{7,5},{8,10},{9,11},{10,... | collective-permute-start | bytes 2359304 | tf_op jit(solution)/shard_map/ppermute | solution.py:23
  267.9 25.9 %collective-permute-start.49 = (bf16[192,1536]{1,0:T(8,128)(2,1)S(1)}, bf16[192,1536]{1,0:T(8,128)(2,1)S(1)}, u32[]{:S(2)}, u32[]{:S(2)}) collective-permute-start(bf16[192,1536]{1,0:T(8,128)(2,1)S(1)} %get-tuple-element.342.refs_0_), channel_id=1, source_target_pairs={{8,0},{16,8},{24,16},{28,24},{20,28},{12,20},{4,12},{0,4},{9,1},{1... | collective-permute-start | bytes 1769480 | tf_op jit(solution)/shard_map/ppermute | solution.py:61
  268.4 25.4 %collective-permute-start.48 = (bf16[192,1536]{1,0:T(8,128)(2,1)S(1)}, bf16[192,1536]{1,0:T(8,128)(2,1)S(1)}, u32[]{:S(2)}, u32[]{:S(2)}) collective-permute-start(bf16[192,1536]{1,0:T(8,128)(2,1)S(1)} %get-tuple-element.342.refs_0_), channel_id=1, source_target_pairs={{0,8},{8,16},{16,24},{24,28},{28,20},{20,12},{12,4},{4,0},{1,9},{9... | collective-permute-start | bytes 1769480 | tf_op jit(solution)/shard_map/ppermute | solution.py:56
  349.3 325.2 %reduce-scatter.11.cloned.1.call-start = ((), (), s32[]{:S(2)}) async-start(), calls=%async_computation.7 | async-start | bytes 5308416 | tf_op jit(solution)/shard_map/reduce_scatter | solution.py:1098
  426.6 258.2 %reduce-scatter.5.cloned.1.call-start = ((), (), s32[]{:S(2)}) async-start(), calls=%async_computation.4 | async-start | bytes 3981312 | tf_op jit(solution)/shard_map/reduce_scatter | solution.py:1098
  483.7 34.6 %collective-permute-start.70 = (bf16[256,1536]{1,0:T(8,128)(2,1)S(1)}, bf16[256,1536]{1,0:T(8,128)(2,1)}, u32[]{:S(2)}, u32[]{:S(2)}) collective-permute-start(bf16[256,1536]{1,0:T(8,128)(2,1)S(1)} %get-tuple-element.424), channel_id=1, source_target_pairs={{0,2},{1,3},{2,0},{3,1},{4,6},{5,7},{6,4},{7,5},{8,10},{9,11},{10,... | collective-permute-start | bytes 2359304 | tf_op jit(solution)/shard_map/ppermute | solution.py:23
  484.1 32.6 %collective-permute-start.72 = (bf16[2,64,768]{2,1,0:T(8,128)(2,1)S(1)}, bf16[2,64,768]{2,1,0:T(8,128)(2,1)S(1)}, u32[]{:S(2)}, u32[]{:S(2)}) collective-permute-start(bf16[2,64,768]{2,1,0:T(8,128)(2,1)S(1)} %pad_maximum_fusion.10), channel_id=1, source_target_pairs={{0,2},{1,3},{2,0},{3,1},{4,6},{5,7},{6,4},{7,5},{8,10},{9,11},{10,... | collective-permute-start | bytes 589832 | tf_op jit(solution)/shard_map/ppermute | solution.py:23
  534.5 174.4 %reduce-scatter.7.cloned.1.call-start = ((), (), s32[]{:S(2)}) async-start(), calls=%async_computation.5 | async-start | bytes 2654208 | tf_op jit(solution)/shard_map/reduce_scatter | solution.py:1098
  534.6 54.4 %collective-permute-start.74 = (bf16[1536,768]{1,0:T(8,128)(2,1)}, bf16[1536,768]{1,0:T(8,128)(2,1)S(1)}, u32[]{:S(2)}, u32[]{:S(2)}) collective-permute-start(bf16[1536,768]{1,0:T(8,128)(2,1)} %get-tuple-element.444), channel_id=1, source_target_pairs={{0,2},{1,3},{2,0},{3,1},{4,6},{5,7},{6,4},{7,5},{8,10},{9,11},{10,... | collective-permute-start | bytes 7077896 | tf_op jit(solution)/shard_map/ppermute | solution.py:23
  539.2 51.1 %collective-permute-start.76 = (bf16[2,16,1536]{2,1,0:T(8,128)(2,1)S(1)}, bf16[2,16,1536]{2,1,0:T(8,128)(2,1)S(1)}, u32[]{:S(2)}, u32[]{:S(2)}) collective-permute-start(bf16[2,16,1536]{2,1,0:T(8,128)(2,1)S(1)} %slice.213), channel_id=1, source_target_pairs={{0,2},{1,3},{2,0},{3,1},{4,6},{5,7},{6,4},{7,5},{8,10},{9,11},{10,... | collective-permute-start | bytes 294920 | tf_op jit(solution)/shard_map/ppermute | solution.py:23
  606.9 22.6 %collective-permute-start.80 = (bf16[512,1536]{1,0:T(8,128)(2,1)}, bf16[512,1536]{1,0:T(8,128)(2,1)}, u32[]{:S(2)}, u32[]{:S(2)}) collective-permute-start(bf16[512,1536]{1,0:T(8,128)(2,1)} %get-tuple-element.461), channel_id=1, source_target_pairs={{0,1},{1,0},{2,3},{3,2},{4,5},{5,4},{6,7},{7,6},{8,9},{9,8},{10,11... | collective-permute-start | bytes 4718600 | tf_op jit(solution)/shard_map/ppermute | solution.py:27
  607.3 24.9 %collective-permute-start.79 = (bf16[256,1536]{1,0:T(8,128)(2,1)}, bf16[256,1536]{1,0:T(8,128)(2,1)S(1)}, u32[]{:S(2)}, u32[]{:S(2)}) collective-permute-start(bf16[256,1536]{1,0:T(8,128)(2,1)} %copy-done.69), channel_id=1, source_target_pairs={{0,2},{1,3},{2,0},{3,1},{4,6},{5,7},{6,4},{7,5},{8,10},{9,11},{10,... | collective-permute-start | bytes 2359304 | tf_op jit(solution)/shard_map/ppermute | solution.py:23
  607.7 37.2 %collective-permute-start.81 = (bf16[256,1536]{1,0:T(8,128)(2,1)}, bf16[256,1536]{1,0:T(8,128)(2,1)S(1)}, u32[]{:S(2)}, u32[]{:S(2)}) collective-permute-start(bf16[256,1536]{1,0:T(8,128)(2,1)} %copy-done.70), channel_id=1, source_target_pairs={{0,2},{1,3},{2,0},{3,1},{4,6},{5,7},{6,4},{7,5},{8,10},{9,11},{10,... | collective-permute-start | bytes 2359304 | tf_op jit(solution)/shard_map/ppermute | solution.py:23
  629.5 42.7 %collective-permute-start.78 = (bf16[256,1536]{1,0:T(8,128)(2,1)}, bf16[256,1536]{1,0:T(8,128)(2,1)S(1)}, u32[]{:S(2)}, u32[]{:S(2)}) collective-permute-start(bf16[256,1536]{1,0:T(8,128)(2,1)} %get-tuple-element.457), channel_id=1, source_target_pairs={{0,2},{1,3},{2,0},{3,1},{4,6},{5,7},{6,4},{7,5},{8,10},{9,11},{10,... | collective-permute-start | bytes 2359304 | tf_op jit(solution)/shard_map/ppermute | solution.py:23
  640.6 23.2 %collective-permute-start.86 = (bf16[192,1152]{1,0:T(8,128)(2,1)}, bf16[192,1152]{1,0:T(8,128)(2,1)}, u32[]{:S(2)}, u32[]{:S(2)}) collective-permute-start(bf16[192,1152]{1,0:T(8,128)(2,1)} %get-tuple-element.477), channel_id=1, source_target_pairs={{8,0},{16,8},{24,16},{28,24},{20,28},{12,20},{4,12},{0,4},{9,1},{1... | collective-permute-start | bytes 1327112 | tf_op jit(solution)/shard_map/ppermute | solution.py:61
  669.9 47.0 %collective-permute-start.88 = (bf16[256,1536]{1,0:T(8,128)(2,1)}, bf16[256,1536]{1,0:T(8,128)(2,1)S(1)}, u32[]{:S(2)}, u32[]{:S(2)}) collective-permute-start(bf16[256,1536]{1,0:T(8,128)(2,1)} %get-tuple-element.487), channel_id=1, source_target_pairs={{0,2},{1,3},{2,0},{3,1},{4,6},{5,7},{6,4},{7,5},{8,10},{9,11},{10,... | collective-permute-start | bytes 2359304 | tf_op jit(solution)/shard_map/ppermute | solution.py:23
  672.1 38.7 %collective-permute-start.89 = (f32[6,1536]{1,0:T(8,128)S(1)}, f32[6,1536]{1,0:T(8,128)S(1)}, u32[]{:S(2)}, u32[]{:S(2)}) collective-permute-start(f32[6,1536]{1,0:T(8,128)S(1)} %get-tuple-element.488.refs_0_), channel_id=1, source_target_pairs={{0,4},{4,0},{8,12},{12,8},{16,20},{20,16},{24,28},{28,24},{1,5},{5... | collective-permute-start | bytes 110600 | tf_op jit(solution)/shard_map/ppermute | solution.py:230
  687.5 32.9 %collective-permute-start.93 = (bf16[192,1152]{1,0:T(8,128)(2,1)}, bf16[192,1152]{1,0:T(8,128)(2,1)S(1)}, u32[]{:S(2)}, u32[]{:S(2)}) collective-permute-start(bf16[192,1152]{1,0:T(8,128)(2,1)} %get-tuple-element.502), channel_id=1, source_target_pairs={{0,8},{8,16},{16,24},{24,28},{28,20},{20,12},{12,4},{4,0},{1,9},{9... | collective-permute-start | bytes 1327112 | tf_op jit(solution)/shard_map/ppermute | solution.py:56
  687.6 32.8 %collective-permute-start.94 = (bf16[192,1152]{1,0:T(8,128)(2,1)}, bf16[192,1152]{1,0:T(8,128)(2,1)S(1)}, u32[]{:S(2)}, u32[]{:S(2)}) collective-permute-start(bf16[192,1152]{1,0:T(8,128)(2,1)} %get-tuple-element.503), channel_id=1, source_target_pairs={{8,0},{16,8},{24,16},{28,24},{20,28},{12,20},{4,12},{0,4},{9,1},{1... | collective-permute-start | bytes 1327112 | tf_op jit(solution)/shard_map/ppermute | solution.py:61
  (184 other events, 1725.0 us)
Sparse Core Ops, SparseCore 0:
  349.4 94.7 reduce-scatter.8
  447.9 94.9 reduce-scatter.10
  546.6 78.9 reduce-scatter.4
  628.9 79.9 reduce-scatter.6

commit v3 on v2

--- a/solution.py
+++ b/solution.py
@@ -298,9 +298,9 @@
     return [jnp.where(m, block, zero) for m in masks]
 
 
-def rows_call(body, ins, outs, sums=(), wait=(), shifts=None):
+def rows_call(body, ins, outs, sums=(), wait=(), shifts=None, most=128):
     rows = outs[0][0][0]
-    block = next((v for v in (128, 96) if rows % v == 0), rows)
+    block = next((v for v in (most, 96) if rows % v == 0), rows)
     steps = rows // block
     shifts = shifts or [0] * len(ins)
     in_specs = []
@@ -493,6 +493,21 @@
         [((len(parts), *shape), kind)],
         [pl.BlockSpec((len(parts), block, shape[1]), lambda i: (0, i, 0))],
     )[0]
+
+
+def sum_beside_body(own_ref, *refs):
+    came, last, out = refs[:-2], refs[-2], refs[-1]
+    begin = 0
+    for ref in came:
+        cols = slice(begin, begin + ref.shape[1])
+        begin = cols.stop
+        out[:, cols] = (own_ref[:, cols].astype(F32) + ref[...].astype(F32)).astype(BF16)
+    out[:, begin:] = last[...]
+
+
+def sum_beside(own, came, last):
+    shape = (own.shape[0], own.shape[1] + last.shape[1])
+    return rows_call(sum_beside_body, (own, *came, last), [(shape, BF16)], most=256)[0]
 
 
 def sum_terms_body(*refs):
@@ -1020,11 +1035,11 @@
     ]
 
     raw_swapped = [swap_chip(audio_states[c]) for c in both]
-    cross_came, raw_swapped[0] = self_ring.turn([cross_came, raw_swapped[0]], params)
-    cross_shard = jnp.concatenate((cross_own, cross_came, cross_kv[0], cross_kv[1]), axis=1)
+    (raw_swapped[0],) = self_ring.turn(raw_swapped[:1])
     raw = gather_rows(audio_states[0], raw_swapped[0])
     full_self = [norm_pair(0, raw, params)]
-    self_ring.turn()
+    (cross_came,) = self_ring.turn([cross_came])
+    cross_shard = jnp.concatenate((cross_own, cross_came, cross_kv[0], cross_kv[1]), axis=1)
     raw_swapped[1:] = self_ring.turn(raw_swapped[1:])
     raw = [gather_rows(audio_states[c], raw_swapped[c]) for c in range(1, clips)]
     full_self += [norm_pair(0, v, params) for v in raw]
@@ -1037,16 +1052,16 @@
     for c in both:
         rows, attn, log, keep, send = self_forward(*full_self[c], self_w, units)
         if c == 0:
-            send, *out_swapped = cross_ring.turn([send, *out_swapped])
-            seen_out = [gather_rows(out_grad[k], out_swapped[k]) for k in both]
+            send, out_swapped[0] = cross_ring.turn([send, out_swapped[0]])
         else:
             keep_0, seen_0, other_0 = mid_terms[0][1:]
-            send, other_0 = cross_ring.turn([send, other_0])
+            send, other_0, *out_swapped[1:] = cross_ring.turn([send, other_0, *out_swapped[1:]])
             mid_terms[0] = (audio_states[0], keep_0, seen_0, other_0)
         mid_terms.append((audio_states[c], *sum_over_tp(keep, send)))
         qkv.append(rows)
         self_attn.append(attn)
         self_log.append(log)
+    seen_out = [gather_rows(out_grad[c], out_swapped[c]) for c in both]
     stream_mid, cross_rows = [], []
     for c in both:
         stream, normed = norm_forward(1, mid_terms[c], params, share)
@@ -1156,7 +1171,8 @@
     (came,) = tick([branches[0][1]])
     seen_in = [gather_rows(branches[0][0], came)]
     seen_in += [gather_rows(*branches[c]) for c in range(1, clips)]
-    cross_came = swap_chip(cross_shares[1])
+    first = 2 * units // 3 if units % 192 == 0 else units
+    cross_came = [swap_chip(cross_shares[1][:, :first]), swap_chip(cross_shares[1][:, first:])]
 
     self_grads, in_terms, out_sums = [], [], []
     for c in both:
@@ -1164,22 +1180,22 @@
             *seen_in[c], self_w, qkv[c], self_attn[c], self_log[c]
         )
         if c == 0:
-            send, kv_came = tick([send, kv_came])
+            send, kv_came, cross_came[0] = tick([send, kv_came, cross_came[0]])
         else:
-            send, cross_came, text_came = tick([send, cross_came, text_came])
+            send, cross_came[1], text_came = tick([send, cross_came[1], text_came])
         in_terms.append(sum_over_tp(keep, send))
         self_grads.append(grads)
         if c == 0:
             kv_grads = (jnp.stack(own_kv) + kv_came.astype(F32)).astype(BF16)
             kv_rows = kv_grads.reshape(-1, 2 * units)
             grad = weight_grad((sum(seen_in, ()), self_attn), ([text_rows], [kv_rows]))
-            out_total = sum_clips(grad)
+            out_wide = grad
             text_keep, text_send = text_back(kv_rows, cross_w, 2, clips)
             quarter = text_keep.shape[1] // 2
             text_seen = text_keep + swap_core(text_send).astype(F32)
             text_came = swap_chip(text_seen[:, quarter:].astype(BF16))
         else:
-            cross_total = sum_clips(sum_terms((cross_shares[0], cross_came), cross_came.shape))
+            mid_total = sum_clips(sum_beside(cross_shares[0], cross_came, out_wide))
     text_grad = text_seen[:, :quarter] + text_came.astype(F32)
     grad = weight_grad((sum(full_self, ()), self_grads))
     qkv_sum = RingSum([grad], n, table)
@@ -1197,7 +1213,7 @@
     norm_total.step()
     norm_total.step()
     layer_out.append(sum_terms((stream_late[0], *late_terms[0]), (share, width)))
-    qkv_sum.step([out_total])
+    qkv_sum.step()
     norm_total.step()
     norm_total.step()
     for c in range(1, clips):
@@ -1214,10 +1230,10 @@
         audio_grad,
         text_grad.astype(BF16),
         qkv_total,
-        cut(out_total, 0).astype(F32).T,
-        cut(cross_total, 0).astype(F32),
-        jnp.stack((cut(out_total, 1), cut(out_total, 2))).astype(F32),
-        cut(cross_total, 1).astype(F32).T,
+        cut(mid_total, 2).astype(F32).T,
+        cut(mid_total, 0).astype(F32),
+        jnp.stack((cut(mid_total, 3), cut(mid_total, 4))).astype(F32),
+        cut(mid_total, 1).astype(F32).T,
         jnp.concatenate([v[:, :part] for v in ffn_totals], 1).astype(F32),
         jnp.concatenate([v[:, part:] for v in ffn_totals], 1).astype(F32).T,
         norm_total[0::2],

time: 742 us -> 762 us (1.027)
  local copies, waits for them, and re-layouts: 55.7 us -> 66.3 us
    ppermute x20, waiting for transfers between devices: 21.6 us -> 54.2 us  [send_prev(): lax.ppermute(values, 'fsdp', [(ring[(k + 1) % n], ring[k]) for k in range...]
    reduce_scatter x4 -> x3, waiting for transfers between devices: 19.4 us -> 0.02 us  [sum_clips(): return lax.psum_scatter(grad, 'fsdp', scatter_dimension=0, tiled=True)]
    ppermute x23 -> x24, starting transfers between devices: 22.3 us -> 29.9 us  [swap_chip(): return lax.ppermute(values, 'tp', [(t, t ^ 2) for t in range(4)])]
    ppermute x23 -> x24, waiting for transfers between devices: 50.5 us -> 52.3 us  [swap_chip(): return lax.ppermute(values, 'tp', [(t, t ^ 2) for t in range(4)])]
  transfers between devices with their start and end apart: 100 -> 100, of which waited for: 45 -> 41; matrix products, arithmetic and copies ran while one was open for 3% -> 4% of each run, Pallas kernels for 53% -> 51%
where the time goes in v3:
time: 762 us; the launch traced here: 752 us
  Pallas kernels  391 us (51%)
  waiting for transfers between devices  183 us (24%)
  starting transfers between devices  81.4 us (11%)
  local copies, waits for them, and re-layouts  66.3 us (9%)
  between operations  15.6 us (2%)
  other arithmetic  15.2 us (2%)
    pallas_call x79, Pallas kernels, call(): pl.pallas_call(run, grid=grid, in_specs=list(in_specs) + [hbm] * len(wait...  391 us
    ppermute x20, waiting for transfers between devices, send_prev(): lax.ppermute(values, 'fsdp', [(ring[(k + 1) % n], ring[k]) for k in range...  54.2 us
    ppermute x24, waiting for transfers between devices, swap_chip(): return lax.ppermute(values, 'tp', [(t, t ^ 2) for t in range(4)])  52.3 us
    unnamed x240, local copies, waits for them, and re-layouts  46.2 us
    ppermute x20, waiting for transfers between devices, send_next(): lax.ppermute(values, 'fsdp', [(ring[k], ring[(k + 1) % n]) for k in range...  39.1 us
    ppermute x24, starting transfers between devices, swap_chip(): return lax.ppermute(values, 'tp', [(t, t ^ 2) for t in range(4)])  29.9 us
    ppermute x20, starting transfers between devices, send_next(): lax.ppermute(values, 'fsdp', [(ring[k], ring[(k + 1) % n]) for k in range...  24.4 us
    ppermute x27, waiting for transfers between devices, swap_core(): return lax.ppermute(values, 'tp', [(t, t ^ 1) for t in range(4)])  19.8 us
  transfers between devices with their start and end apart: 100, of which 41 were waited for; matrix products, arithmetic and copies ran while one was open for 4% of the time, Pallas kernels for 51%

profile of v3, /device:TPU:0, one launch (start us, length us, event | category | flops | bytes accessed | tf_op | source)
XLA Modules:
  0.0 752.3 jit_solution(1842641084895574116)
XLA Ops:
  18.7 12.8 %collective-permute-done.1.refs_1_ = bf16[192,1536]{1,0:T(8,128)(2,1)S(1)} collective-permute-done((bf16[192,1536]{1,0:T(8,128)(2,1)S(1)}, bf16[192,1536]{1,0:T(8,128)(2,1)S(1)}, u32[]{:S(2)}, u32[]{:S(2)}) %collective-permute-start.1) | collective-permute-done | bytes 589856 | tf_op jit(solution)/shard_map/ppermute | solution.py:61
  43.8 12.0 %collective-permute-done.6 = bf16[4,6,192]{2,1,0:T(8,128)(2,1)S(1)} collective-permute-done((bf16[4,6,192]{2,1,0:T(8,128)(2,1)S(1)}, bf16[4,6,192]{2,1,0:T(8,128)(2,1)S(1)}, u32[]{:S(2)}, u32[]{:S(2)}) %collective-permute-start.6) | collective-permute-done | bytes 9248 | tf_op jit(solution)/shard_map/ppermute | solution.py:230
  65.9 7.0 collective-permute-done.12.refs_2_
  96.8 22.5 %self_forward_body.2 = (bf16[1024,1152]{1,0:T(8,128)(2,1)}, bf16[1024,384]{1,0:T(8,128)(2,1)S(1)}, f32[24,1024]{1,0:T(8,128)S(1)}, f32[512,1536]{1,0:T(8,128)}, ...) custom-call(bf16[512,1536]{1,0:T(8,128)(2,1)} %copy-done.7, bf16[512,1536]{1,0:T(8,128)(2,1)} %get-tuple-element.266.refs_1_, ...), custom_call_target="tpu_custom_call" | custom-call | flops 1000 | tf_op jit(solution)/shard_map/self_forward_body/pallas_call | solution.py:275
  129.2 22.5 %self_forward_body.3 = (bf16[1024,1152]{1,0:T(8,128)(2,1)}, bf16[1024,384]{1,0:T(8,128)(2,1)S(1)}, f32[24,1024]{1,0:T(8,128)S(1)}, f32[512,1536]{1,0:T(8,128)}, ...) custom-call(bf16[512,1536]{1,0:T(8,128)(2,1)} %copy-done.9, bf16[512,1536]{1,0:T(8,128)(2,1)} %get-tuple-element.290.refs_1_.refs_3_, ...), custom_call_target="tpu_custom_call" | custom-call | flops 1000 | tf_op jit(solution)/shard_map/self_forward_body/pallas_call | solution.py:275
  152.7 7.0 collective-permute-done.22.refs_3_
  173.3 8.7 %collective-permute-done.26.refs_0_ = bf16[192,2304]{1,0:T(8,128)(2,1)S(1)} collective-permute-done((bf16[192,2304]{1,0:T(8,128)(2,1)}, bf16[192,2304]{1,0:T(8,128)(2,1)S(1)}, u32[]{:S(2)}, u32[]{:S(2)}) %collective-permute-start.26) | collective-permute-done | bytes 884768 | tf_op jit(solution)/shard_map/ppermute | solution.py:56
  199.2 6.3 place_pieces_body.5
  217.3 10.3 %cross_forward_body.2 = (bf16[512,768]{1,0:T(8,128)(2,1)S(1)}, bf16[512,768]{1,0:T(8,128)(2,1)S(1)}, f32[256,1536]{1,0:T(8,128)}, bf16[256,1536]{1,0:T(8,128)(2,1)}, f32[8,128]{1,0:T(8,128)S(1)}) custom-call(bf16[256,1536]{1,0:T(8,128)(2,1)} %copy-done.27, bf16[256,1536]{1,0:T(8,128)(2,1)} %copy-done.30, ...), custom_call_target="tpu_custom_call" | custom-call | flops 1000 | tf_op jit(solution)/shard_map/cross_forward_body/pallas_call | solution.py:275
  240.7 10.3 %cross_forward_body.3 = (bf16[512,768]{1,0:T(8,128)(2,1)S(1)}, bf16[512,768]{1,0:T(8,128)(2,1)S(1)}, f32[256,1536]{1,0:T(8,128)}, bf16[256,1536]{1,0:T(8,128)(2,1)}, f32[8,128]{1,0:T(8,128)S(1)}) custom-call(bf16[256,1536]{1,0:T(8,128)(2,1)} %copy-done.29, bf16[256,1536]{1,0:T(8,128)(2,1)} %copy-done.90, ...), custom_call_target="tpu_custom_call" | custom-call | flops 1000 | tf_op jit(solution)/shard_map/cross_forward_body/pallas_call | solution.py:275
  277.5 16.6 %ffn_first_body.2 = (bf16[1024,768]{1,0:T(8,128)(2,1)S(1)}, bf16[1024,768]{1,0:T(8,128)(2,1)}, f32[1024,1536]{1,0:T(8,128)}, f32[1024,1536]{1,0:T(8,128)}, f32[8,128]{1,0:T(8,128)S(1)}) custom-call(bf16[512,1536]{1,0:T(8,128)(2,1)} %copy-done, bf16[512,1536]{1,0:T(8,128)(2,1)} %collective-permute-done.43.refs_1_, bf16[512,1536]{1,0:T(8,128)(2,1)} %copy-done.71, ...), custom_call_target="tpu_custom_call" | custom-call | flops 1000 | tf_op jit(solution)/shard_map/ffn_first_body/pallas_call | solution.py:275
  301.6 16.6 %ffn_first_body.3 = (bf16[1024,768]{1,0:T(8,128)(2,1)S(1)}, bf16[1024,768]{1,0:T(8,128)(2,1)}, f32[1024,1536]{1,0:T(8,128)}, f32[1024,1536]{1,0:T(8,128)}, f32[8,128]{1,0:T(8,128)S(1)}) custom-call(bf16[512,1536]{1,0:T(8,128)(2,1)} %copy-done.73, bf16[512,1536]{1,0:T(8,128)(2,1)} %copy-done.74, bf16[512,1536]{1,0:T(8,128)(2,1)} %pad_maximum_fusion.3.refs_2_.refs_6_, ...), custom_call_target="tpu_custom_call" | custom-call | flops 1000 | tf_op jit(solution)/shard_map/ffn_first_body/pallas_call | solution.py:275
  321.6 15.7 %weight_grad_body.5 = (bf16[1536,1536]{1,0:T(8,128)(2,1)}, f32[8,128]{1,0:T(8,128)S(1)}) custom-call(bf16[512,1536]{1,0:T(8,128)(2,1)S(1)} %copy-done.1, bf16[512,1536]{1,0:T(8,128)(2,1)} %collective-permute-done.43.refs_1_, bf16[512,1536]{1,0:T(8,128)(2,1)} %copy-done.73, bf16[512,1536]{1,0:T(8,128)(2,1)} %copy-done.74, bf16[512,1536]{1,0:T(8,128)(2,1)} %copy-done.71, ...), custom_call_target="tpu_custom_call" | custom-call | flops 1000 | tf_op jit(solution)/shard_map/weight_grad_body/pallas_call | solution.py:275
  339.5 6.7 collective-permute-done.58.refs_8_
  350.4 19.1 %ffn_second_body.2 = (bf16[1024,768]{1,0:T(8,128)(2,1)S(1)}, bf16[1024,768]{1,0:T(8,128)(2,1)}, f32[512,1536]{1,0:T(8,128)}, bf16[512,1536]{1,0:T(8,128)(2,1)}, ...) custom-call(bf16[512,1536]{1,0:T(8,128)(2,1)} %copy-done, ...), custom_call_target="tpu_custom_call" | custom-call | flops 1000 | tf_op jit(solution)/shard_map/ffn_second_body/pallas_call | solution.py:275
  378.5 19.3 %ffn_second_body.3 = (bf16[1024,768]{1,0:T(8,128)(2,1)S(1)}, bf16[1024,768]{1,0:T(8,128)(2,1)}, f32[512,1536]{1,0:T(8,128)}, bf16[512,1536]{1,0:T(8,128)(2,1)}, ...) custom-call(bf16[512,1536]{1,0:T(8,128)(2,1)} %copy-done.73, bf16[512,1536]{1,0:T(8,128)(2,1)} %copy-done.74, ...), custom_call_target="tpu_custom_call" | custom-call | flops 1000 | tf_op jit(solution)/shard_map/ffn_second_body/pallas_call | solution.py:275
  410.7 16.0 %weight_grad_body.6 = (bf16[1536,1536]{1,0:T(8,128)(2,1)}, f32[8,128]{1,0:T(8,128)S(1)}) custom-call(bf16[512,1536]{1,0:T(8,128)(2,1)S(1)} %copy-done.2, bf16[512,1536]{1,0:T(8,128)(2,1)} %collective-permute-done.43.refs_1_, bf16[512,1536]{1,0:T(8,128)(2,1)} %copy-done.73, bf16[512,1536]{1,0:T(8,128)(2,1)} %copy-done.74, bf16[512,1536]{1,0:T(8,128)(2,1)} %copy-done.71, ...), custom_call_target="tpu_custom_call" | custom-call | flops 1000 | tf_op jit(solution)/shard_map/weight_grad_body/pallas_call | solution.py:275
  432.1 11.4 %cross_backward_body.2 = (bf16[512,768]{1,0:T(8,128)(2,1)S(1)}, f32[64,768]{1,0:T(8,128)S(1)}, bf16[64,768]{1,0:T(8,128)(2,1)S(1)}, f32[256,1536]{1,0:T(8,128)},...) custom-call(bf16[256,1536]{1,0:T(8,128)(2,1)} %copy-done.32, bf16[256,1536]{1,0:T(8,128)(2,1)} %copy-done.91, ...), custom_call_target="tpu_custom_call" | custom-call | flops 1000 | tf_op jit(solution)/shard_map/cross_backward_body/pallas_call | solution.py:275
  453.9 11.6 %cross_backward_body.3 = (bf16[512,768]{1,0:T(8,128)(2,1)S(1)}, f32[64,768]{1,0:T(8,128)S(1)}, bf16[64,768]{1,0:T(8,128)(2,1)S(1)}, f32[256,1536]{1,0:T(8,128)},...) custom-call(bf16[256,1536]{1,0:T(8,128)(2,1)} %copy-done.33, bf16[256,1536]{1,0:T(8,128)(2,1)} %copy-done.92, ...), custom_call_target="tpu_custom_call" | custom-call | flops 1000 | tf_op jit(solution)/shard_map/cross_backward_body/pallas_call | solution.py:275
  472.8 10.3 %weight_grad_body.7 = (bf16[1536,768]{1,0:T(8,128)(2,1)}, bf16[1536,768]{1,0:T(8,128)(2,1)}, f32[8,128]{1,0:T(8,128)S(1)}) custom-call(bf16[256,1536]{1,0:T(8,128)(2,1)S(1)} %copy-done.28, bf16[256,1536]{1,0:T(8,128)(2,1)S(1)} %copy-done.31, bf16[256,1536]{1,0:T(8,128)(2,1)} %copy-done.29, bf16[256,1536]{1,0:T(8,128)(2,1)} %copy-done.90, ...), custom_call_target="tpu_custom_call" | custom-call | flops 1000 | tf_op jit(solution)/shard_map/weight_grad_body/pallas_call | solution.py:275
  492.8 28.6 %self_backward_body.2 = (bf16[1024,1152]{1,0:T(8,128)(2,1)}, f32[512,1536]{1,0:T(8,128)}, bf16[512,1536]{1,0:T(8,128)(2,1)}, f32[8,128]{1,0:T(8,128)S(1)}) custom-call(bf16[512,1536]{1,0:T(8,128)(2,1)} %copy-done.75, bf16[512,1536]{1,0:T(8,128)(2,1)} %copy-done.84, bf16[1536,1536]{1,0:T(8,128)(2,1)} %get-tuple-element.280.refs_2_.refs_3_, ...), custom_call_target="tpu_custom_call" | custom-call | flops 1000 | tf_op jit(solution)/shard_map/self_backward_body/pallas_call | solution.py:275
  521.3 7.5 collective-permute-done.72.refs_1_
  537.5 8.8 %weight_grad_body.8 = (bf16[1536,1152]{1,0:T(8,128)(2,1)}, f32[8,128]{1,0:T(8,128)S(1)}) custom-call(bf16[512,1536]{1,0:T(8,128)(2,1)} %copy-done.75, bf16[512,1536]{1,0:T(8,128)(2,1)} %copy-done.84, bf16[512,1536]{1,0:T(8,128)(2,1)} %copy-done.76, bf16[512,1536]{1,0:T(8,128)(2,1)} %copy-done.86, bf16[128,1536]{1,0:T(8,128)(2,1)S(1)} %bitcast.45, ...), custom_call_target="tpu_custom_call" | custom-call | flops 1000 | tf_op jit(solution)/shard_map/weight_grad_body/pallas_call | solution.py:275
  551.4 28.6 %self_backward_body.3 = (bf16[1024,1152]{1,0:T(8,128)(2,1)}, f32[512,1536]{1,0:T(8,128)}, bf16[512,1536]{1,0:T(8,128)(2,1)}, f32[8,128]{1,0:T(8,128)S(1)}) custom-call(bf16[512,1536]{1,0:T(8,128)(2,1)} %copy-done.76, bf16[512,1536]{1,0:T(8,128)(2,1)} %copy-done.86, bf16[1536,1536]{1,0:T(8,128)(2,1)} %get-tuple-element.280.refs_2_.refs_3_, ...), custom_call_target="tpu_custom_call" | custom-call | flops 1000 | tf_op jit(solution)/shard_map/self_backward_body/pallas_call | solution.py:275
  588.9 7.3 sum_beside_body.1
  598.0 13.0 %weight_grad_body.9 = (bf16[1536,1152]{1,0:T(8,128)(2,1)}, f32[8,128]{1,0:T(8,128)S(1)}) custom-call(bf16[512,1536]{1,0:T(8,128)(2,1)S(1)} %copy-done.8, bf16[512,1536]{1,0:T(8,128)(2,1)} %get-tuple-element.266.refs_1_, bf16[512,1536]{1,0:T(8,128)(2,1)} %copy-done.9, bf16[512,1536]{1,0:T(8,128)(2,1)} %get-tuple-element.290.refs_1_.refs_3_, ...), custom_call_target="tpu_custom_call" | custom-call | flops 1000 | tf_op jit(solution)/shard_map/weight_grad_body/pallas_call | solution.py:275
  624.9 7.3 collective-permute-done.84.refs_3_
  642.8 11.9 %collective-permute-done.86.refs_2_ = bf16[192,1152]{1,0:T(8,128)(2,1)S(1)} collective-permute-done((bf16[192,1152]{1,0:T(8,128)(2,1)S(1)}, bf16[192,1152]{1,0:T(8,128)(2,1)S(1)}, u32[]{:S(2)}, u32[]{:S(2)}) %collective-permute-start.86) | collective-permute-done | bytes 442400 | tf_op jit(solution)/shard_map/ppermute | solution.py:56
  654.7 10.8 %collective-permute-done.87.refs_3_ = bf16[192,1152]{1,0:T(8,128)(2,1)S(1)} collective-permute-done((bf16[192,1152]{1,0:T(8,128)(2,1)S(1)}, bf16[192,1152]{1,0:T(8,128)(2,1)S(1)}, u32[]{:S(2)}, u32[]{:S(2)}) %collective-permute-start.87) | collective-permute-done | bytes 442400 | tf_op jit(solution)/shard_map/ppermute | solution.py:61
  673.2 18.2 %collective-permute-done.88.refs_1_ = f32[6,1536]{1,0:T(8,128)S(1)} collective-permute-done((f32[6,1536]{1,0:T(8,128)S(1)}, f32[6,1536]{1,0:T(8,128)S(1)}, u32[]{:S(2)}, u32[]{:S(2)}) %collective-permute-start.88) | collective-permute-done | bytes 36896 | tf_op jit(solution)/shard_map/ppermute | solution.py:23
  712.6 10.4 %collective-permute-done.94.refs_2_ = bf16[192,1152]{1,0:T(8,128)(2,1)S(1)} collective-permute-done((bf16[192,1152]{1,0:T(8,128)(2,1)S(1)}, bf16[192,1152]{1,0:T(8,128)(2,1)S(1)}, u32[]{:S(2)}, u32[]{:S(2)}) %collective-permute-start.94) | collective-permute-done | bytes 442400 | tf_op jit(solution)/shard_map/ppermute | solution.py:56
  723.0 11.4 %collective-permute-done.95.refs_3_ = bf16[192,1152]{1,0:T(8,128)(2,1)S(1)} collective-permute-done((bf16[192,1152]{1,0:T(8,128)(2,1)S(1)}, bf16[192,1152]{1,0:T(8,128)(2,1)S(1)}, u32[]{:S(2)}, u32[]{:S(2)}) %collective-permute-start.95) | collective-permute-done | bytes 442400 | tf_op jit(solution)/shard_map/ppermute | solution.py:61
  (553 shorter events, 310.2 us)
Async XLA Ops:
  7.2 692.0 %reduce-scatter.6.cloned.1.call-start = ((), (), s32[]{:S(2)}) async-start(), calls=%async_computation.4 | async-start | bytes 5308416 | tf_op jit(solution)/shard_map/reduce_scatter | solution.py:1113
  8.8 23.9 %collective-permute-start.2 = (bf16[256,1536]{1,0:T(8,128)(2,1)S(1)}, bf16[256,1536]{1,0:T(8,128)(2,1)S(1)}, u32[]{:S(2)}, u32[]{:S(2)}) collective-permute-start(bf16[256,1536]{1,0:T(8,128)(2,1)S(1)} %get-tuple-element.517.refs_0_), channel_id=1, source_target_pairs={{0,2},{1,3},{2,0},{3,1},{4,6},{5,7},{6,4},{7,5},{8,10},{9,11},{10,... | collective-permute-start | bytes 2359304 | tf_op jit(solution)/shard_map/ppermute | solution.py:23
  34.2 23.7 %collective-permute-start.3 = (bf16[512,1536]{1,0:T(8,128)(2,1)}, bf16[512,1536]{1,0:T(8,128)(2,1)}, u32[]{:S(2)}, u32[]{:S(2)}) collective-permute-start(bf16[512,1536]{1,0:T(8,128)(2,1)} %pad_maximum_fusion.refs_0_), channel_id=1, source_target_pairs={{0,1},{1,0},{2,3},{3,2},{4,5},{5,4},{6,7},{7,6},{8,9},{9,8},{10,11... | collective-permute-start | bytes 4718600 | tf_op jit(solution)/shard_map/ppermute | solution.py:27
  36.6 27.2 %collective-permute-start.9 = (bf16[192,768]{1,0:T(8,128)(2,1)}, bf16[192,768]{1,0:T(8,128)(2,1)S(1)}, u32[]{:S(2)}, u32[]{:S(2)}) collective-permute-start(bf16[192,768]{1,0:T(8,128)(2,1)} %pad_maximum_fusion.8), channel_id=1, source_target_pairs={{0,2},{1,3},{2,0},{3,1},{4,6},{5,7},{6,4},{7,5},{8,10},{9,11},{10,... | collective-permute-start | bytes 884744 | tf_op jit(solution)/shard_map/ppermute | solution.py:23
  39.0 24.8 %collective-permute-start.7 = (bf16[192,1536]{1,0:T(8,128)(2,1)}, bf16[192,1536]{1,0:T(8,128)(2,1)}, u32[]{:S(2)}, u32[]{:S(2)}) collective-permute-start(bf16[192,1536]{1,0:T(8,128)(2,1)} %copy-done.42), channel_id=1, source_target_pairs={{0,8},{8,16},{16,24},{24,28},{28,20},{20,12},{12,4},{4,0},{1,9},{9... | collective-permute-start | bytes 1769480 | tf_op jit(solution)/shard_map/ppermute | solution.py:56
  39.9 23.9 %collective-permute-start.8 = (bf16[192,1536]{1,0:T(8,128)(2,1)}, bf16[192,1536]{1,0:T(8,128)(2,1)}, u32[]{:S(2)}, u32[]{:S(2)}) collective-permute-start(bf16[192,1536]{1,0:T(8,128)(2,1)} %copy-done.41), channel_id=1, source_target_pairs={{8,0},{16,8},{24,16},{28,24},{20,28},{12,20},{4,12},{0,4},{9,1},{1... | collective-permute-start | bytes 1769480 | tf_op jit(solution)/shard_map/ppermute | solution.py:61
  90.3 29.6 %collective-permute-start.17 = (bf16[192,2304]{1,0:T(8,128)(2,1)S(1)}, bf16[192,2304]{1,0:T(8,128)(2,1)S(1)}, u32[]{:S(2)}, u32[]{:S(2)}) collective-permute-start(bf16[192,2304]{1,0:T(8,128)(2,1)S(1)} %get-tuple-element.283.refs_0_), channel_id=1, source_target_pairs={{8,0},{16,8},{24,16},{28,24},{20,28},{12,20},{4,12},{0,4},{9,1},{1... | collective-permute-start | bytes 2654216 | tf_op jit(solution)/shard_map/ppermute | solution.py:61
  90.8 29.1 %collective-permute-start.16 = (bf16[192,2304]{1,0:T(8,128)(2,1)S(1)}, bf16[192,2304]{1,0:T(8,128)(2,1)S(1)}, u32[]{:S(2)}, u32[]{:S(2)}) collective-permute-start(bf16[192,2304]{1,0:T(8,128)(2,1)S(1)} %get-tuple-element.283.refs_0_), channel_id=1, source_target_pairs={{0,8},{8,16},{16,24},{24,28},{28,20},{20,12},{12,4},{4,0},{1,9},{9... | collective-permute-start | bytes 2654216 | tf_op jit(solution)/shard_map/ppermute | solution.py:56
  92.5 27.4 %collective-permute-start.18 = (bf16[256,1536]{1,0:T(8,128)(2,1)S(1)}, bf16[256,1536]{1,0:T(8,128)(2,1)S(1)}, u32[]{:S(2)}, u32[]{:S(2)}) collective-permute-start(bf16[256,1536]{1,0:T(8,128)(2,1)S(1)} %get-tuple-element.515.refs_1_), channel_id=1, source_target_pairs={{0,2},{1,3},{2,0},{3,1},{4,6},{5,7},{6,4},{7,5},{8,10},{9,11},{10,... | collective-permute-start | bytes 2359304 | tf_op jit(solution)/shard_map/ppermute | solution.py:23
  121.1 31.6 %collective-permute-start.20 = (bf16[192,2304]{1,0:T(8,128)(2,1)S(1)}, bf16[192,2304]{1,0:T(8,128)(2,1)S(1)}, u32[]{:S(2)}, u32[]{:S(2)}) collective-permute-start(bf16[192,2304]{1,0:T(8,128)(2,1)S(1)} %get-tuple-element.287.refs_1_), channel_id=1, source_target_pairs={{0,8},{8,16},{16,24},{24,28},{28,20},{20,12},{12,4},{4,0},{1,9},{9... | collective-permute-start | bytes 2654216 | tf_op jit(solution)/shard_map/ppermute | solution.py:56
  121.9 30.8 %collective-permute-start.21 = (bf16[192,2304]{1,0:T(8,128)(2,1)}, bf16[192,2304]{1,0:T(8,128)(2,1)}, u32[]{:S(2)}, u32[]{:S(2)}) collective-permute-start(bf16[192,2304]{1,0:T(8,128)(2,1)} %get-tuple-element.288.refs_2_), channel_id=1, source_target_pairs={{8,0},{16,8},{24,16},{28,24},{20,28},{12,20},{4,12},{0,4},{9,1},{1... | collective-permute-start | bytes 2654216 | tf_op jit(solution)/shard_map/ppermute | solution.py:61
  123.4 29.2 %collective-permute-start.23 = (bf16[256,1536]{1,0:T(8,128)(2,1)S(1)}, bf16[256,1536]{1,0:T(8,128)(2,1)S(1)}, u32[]{:S(2)}, u32[]{:S(2)}) collective-permute-start(bf16[256,1536]{1,0:T(8,128)(2,1)S(1)} %get-tuple-element.514.refs_1_), channel_id=1, source_target_pairs={{0,2},{1,3},{2,0},{3,1},{4,6},{5,7},{6,4},{7,5},{8,10},{9,11},{10,... | collective-permute-start | bytes 2359304 | tf_op jit(solution)/shard_map/ppermute | solution.py:23
  127.9 31.8 %collective-permute-start.22 = (bf16[256,1536]{1,0:T(8,128)(2,1)S(1)}, bf16[256,1536]{1,0:T(8,128)(2,1)S(1)}, u32[]{:S(2)}, u32[]{:S(2)}) collective-permute-start(bf16[256,1536]{1,0:T(8,128)(2,1)S(1)} %get-tuple-element.294), channel_id=1, source_target_pairs={{0,2},{1,3},{2,0},{3,1},{4,6},{5,7},{6,4},{7,5},{8,10},{9,11},{10,... | collective-permute-start | bytes 2359304 | tf_op jit(solution)/shard_map/ppermute | solution.py:23
  239.6 37.8 %collective-permute-start.44 = (bf16[512,1536]{1,0:T(8,128)(2,1)S(1)}, bf16[512,1536]{1,0:T(8,128)(2,1)}, u32[]{:S(2)}, u32[]{:S(2)}) collective-permute-start(bf16[512,1536]{1,0:T(8,128)(2,1)S(1)} %pad_maximum_fusion.2.refs_2_.refs_4_), channel_id=1, source_target_pairs={{0,1},{1,0},{2,3},{3,2},{4,5},{5,4},{6,7},{7,6},{8,9},{9,8},{10,11... | collective-permute-start | bytes 4718600 | tf_op jit(solution)/shard_map/ppermute | solution.py:27
  264.7 30.5 %collective-permute-start.50 = (bf16[256,1536]{1,0:T(8,128)(2,1)S(1)}, bf16[256,1536]{1,0:T(8,128)(2,1)S(1)}, u32[]{:S(2)}, u32[]{:S(2)}) collective-permute-start(bf16[256,1536]{1,0:T(8,128)(2,1)S(1)} %get-tuple-element.344), channel_id=1, source_target_pairs={{0,2},{1,3},{2,0},{3,1},{4,6},{5,7},{6,4},{7,5},{8,10},{9,11},{10,... | collective-permute-start | bytes 2359304 | tf_op jit(solution)/shard_map/ppermute | solution.py:23
  269.4 25.8 %collective-permute-start.49 = (bf16[192,1536]{1,0:T(8,128)(2,1)S(1)}, bf16[192,1536]{1,0:T(8,128)(2,1)S(1)}, u32[]{:S(2)}, u32[]{:S(2)}) collective-permute-start(bf16[192,1536]{1,0:T(8,128)(2,1)S(1)} %get-tuple-element.343.refs_0_), channel_id=1, source_target_pairs={{8,0},{16,8},{24,16},{28,24},{20,28},{12,20},{4,12},{0,4},{9,1},{1... | collective-permute-start | bytes 1769480 | tf_op jit(solution)/shard_map/ppermute | solution.py:61
  270.1 25.1 %collective-permute-start.48 = (bf16[192,1536]{1,0:T(8,128)(2,1)S(1)}, bf16[192,1536]{1,0:T(8,128)(2,1)S(1)}, u32[]{:S(2)}, u32[]{:S(2)}) collective-permute-start(bf16[192,1536]{1,0:T(8,128)(2,1)S(1)} %get-tuple-element.343.refs_0_), channel_id=1, source_target_pairs={{0,8},{8,16},{16,24},{24,28},{28,20},{20,12},{12,4},{4,0},{1,9},{9... | collective-permute-start | bytes 1769480 | tf_op jit(solution)/shard_map/ppermute | solution.py:56
  350.4 388.6 %reduce-scatter.8.cloned.1.call-start = ((), (), s32[]{:S(2)}) async-start(), calls=%async_computation.5 | async-start | bytes 5308416 | tf_op jit(solution)/shard_map/reduce_scatter | solution.py:1113
  427.5 314.8 %reduce-scatter.4.cloned.1.call-start = ((), (), s32[]{:S(2)}) async-start(), calls=%async_computation.3 | async-start | bytes 6635520 | tf_op jit(solution)/shard_map/reduce_scatter | solution.py:1113
  488.2 40.6 %collective-permute-start.73 = (bf16[1536,256]{1,0:T(8,128)(2,1)S(1)}, bf16[1536,256]{1,0:T(8,128)(2,1)S(1)}, u32[]{:S(2)}, u32[]{:S(2)}) collective-permute-start(bf16[1536,256]{1,0:T(8,128)(2,1)S(1)} %slice.159), channel_id=1, source_target_pairs={{0,2},{1,3},{2,0},{3,1},{4,6},{5,7},{6,4},{7,5},{8,10},{9,11},{10,... | collective-permute-start | bytes 2359304 | tf_op jit(solution)/shard_map/ppermute | solution.py:23
  489.4 39.5 %collective-permute-start.70 = (bf16[256,1536]{1,0:T(8,128)(2,1)S(1)}, bf16[256,1536]{1,0:T(8,128)(2,1)}, u32[]{:S(2)}, u32[]{:S(2)}) collective-permute-start(bf16[256,1536]{1,0:T(8,128)(2,1)S(1)} %get-tuple-element.425), channel_id=1, source_target_pairs={{0,2},{1,3},{2,0},{3,1},{4,6},{5,7},{6,4},{7,5},{8,10},{9,11},{10,... | collective-permute-start | bytes 2359304 | tf_op jit(solution)/shard_map/ppermute | solution.py:23
  490.3 38.5 %collective-permute-start.72 = (bf16[2,64,768]{2,1,0:T(8,128)(2,1)S(1)}, bf16[2,64,768]{2,1,0:T(8,128)(2,1)S(1)}, u32[]{:S(2)}, u32[]{:S(2)}) collective-permute-start(bf16[2,64,768]{2,1,0:T(8,128)(2,1)S(1)} %pad_maximum_fusion.10), channel_id=1, source_target_pairs={{0,2},{1,3},{2,0},{3,1},{4,6},{5,7},{6,4},{7,5},{8,10},{9,11},{10,... | collective-permute-start | bytes 589832 | tf_op jit(solution)/shard_map/ppermute | solution.py:23
  532.1 47.9 %collective-permute-start.75 = (bf16[1536,512]{1,0:T(8,128)(2,1)}, bf16[1536,512]{1,0:T(8,128)(2,1)S(1)}, u32[]{:S(2)}, u32[]{:S(2)}) collective-permute-start(bf16[1536,512]{1,0:T(8,128)(2,1)} %slice.160), channel_id=1, source_target_pairs={{0,2},{1,3},{2,0},{3,1},{4,6},{5,7},{6,4},{7,5},{8,10},{9,11},{10,... | collective-permute-start | bytes 4718600 | tf_op jit(solution)/shard_map/ppermute | solution.py:23
  550.5 29.5 %collective-permute-start.77 = (bf16[2,16,1536]{2,1,0:T(8,128)(2,1)S(1)}, bf16[2,16,1536]{2,1,0:T(8,128)(2,1)S(1)}, u32[]{:S(2)}, u32[]{:S(2)}) collective-permute-start(bf16[2,16,1536]{2,1,0:T(8,128)(2,1)S(1)} %slice.221), channel_id=1, source_target_pairs={{0,2},{1,3},{2,0},{3,1},{4,6},{5,7},{6,4},{7,5},{8,10},{9,11},{10,... | collective-permute-start | bytes 294920 | tf_op jit(solution)/shard_map/ppermute | solution.py:23
  596.8 23.8 %collective-permute-start.80 = (bf16[256,1536]{1,0:T(8,128)(2,1)}, bf16[256,1536]{1,0:T(8,128)(2,1)}, u32[]{:S(2)}, u32[]{:S(2)}) collective-permute-start(bf16[256,1536]{1,0:T(8,128)(2,1)} %copy-done.68), channel_id=1, source_target_pairs={{0,2},{1,3},{2,0},{3,1},{4,6},{5,7},{6,4},{7,5},{8,10},{9,11},{10,... | collective-permute-start | bytes 2359304 | tf_op jit(solution)/shard_map/ppermute | solution.py:23
  635.7 29.9 %collective-permute-start.87 = (bf16[192,1152]{1,0:T(8,128)(2,1)S(1)}, bf16[192,1152]{1,0:T(8,128)(2,1)S(1)}, u32[]{:S(2)}, u32[]{:S(2)}) collective-permute-start(bf16[192,1152]{1,0:T(8,128)(2,1)S(1)} %get-tuple-element.480), channel_id=1, source_target_pairs={{8,0},{16,8},{24,16},{28,24},{20,28},{12,20},{4,12},{0,4},{9,1},{1... | collective-permute-start | bytes 1327112 | tf_op jit(solution)/shard_map/ppermute | solution.py:61
  636.1 55.3 %collective-permute-start.79 = (bf16[256,1536]{1,0:T(8,128)(2,1)}, bf16[256,1536]{1,0:T(8,128)(2,1)S(1)}, u32[]{:S(2)}, u32[]{:S(2)}) collective-permute-start(bf16[256,1536]{1,0:T(8,128)(2,1)} %get-tuple-element.460), channel_id=1, source_target_pairs={{0,2},{1,3},{2,0},{3,1},{4,6},{5,7},{6,4},{7,5},{8,10},{9,11},{10,... | collective-permute-start | bytes 2359304 | tf_op jit(solution)/shard_map/ppermute | solution.py:23
  668.2 26.5 %collective-permute-start.91 = (bf16[192,1152]{1,0:T(8,128)(2,1)}, bf16[192,1152]{1,0:T(8,128)(2,1)S(1)}, u32[]{:S(2)}, u32[]{:S(2)}) collective-permute-start(bf16[192,1152]{1,0:T(8,128)(2,1)} %get-tuple-element.492), channel_id=1, source_target_pairs={{0,8},{8,16},{16,24},{24,28},{28,20},{20,12},{12,4},{4,0},{1,9},{9... | collective-permute-start | bytes 1327112 | tf_op jit(solution)/shard_map/ppermute | solution.py:56
  668.3 27.2 %collective-permute-start.92 = (bf16[192,1152]{1,0:T(8,128)(2,1)S(1)}, bf16[192,1152]{1,0:T(8,128)(2,1)}, u32[]{:S(2)}, u32[]{:S(2)}) collective-permute-start(bf16[192,1152]{1,0:T(8,128)(2,1)S(1)} %get-tuple-element.493), channel_id=1, source_target_pairs={{8,0},{16,8},{24,16},{28,24},{20,28},{12,20},{4,12},{0,4},{9,1},{1... | collective-permute-start | bytes 1327112 | tf_op jit(solution)/shard_map/ppermute | solution.py:61
  670.4 38.7 %collective-permute-start.89 = (bf16[256,1536]{1,0:T(8,128)(2,1)S(1)}, bf16[256,1536]{1,0:T(8,128)(2,1)S(1)}, u32[]{:S(2)}, u32[]{:S(2)}) collective-permute-start(bf16[256,1536]{1,0:T(8,128)(2,1)S(1)} %get-tuple-element.490), channel_id=1, source_target_pairs={{0,2},{1,3},{2,0},{3,1},{4,6},{5,7},{6,4},{7,5},{8,10},{9,11},{10,... | collective-permute-start | bytes 2359304 | tf_op jit(solution)/shard_map/ppermute | solution.py:23
  703.1 31.3 %collective-permute-start.95 = (bf16[192,1152]{1,0:T(8,128)(2,1)S(1)}, bf16[192,1152]{1,0:T(8,128)(2,1)S(1)}, u32[]{:S(2)}, u32[]{:S(2)}) collective-permute-start(bf16[192,1152]{1,0:T(8,128)(2,1)S(1)} %get-tuple-element.505), channel_id=1, source_target_pairs={{8,0},{16,8},{24,16},{28,24},{20,28},{12,20},{4,12},{0,4},{9,1},{1... | collective-permute-start | bytes 1327112 | tf_op jit(solution)/shard_map/ppermute | solution.py:61
  707.2 29.9 %collective-permute-start.96 = (f32[6,1536]{1,0:T(8,128)S(1)}, f32[6,1536]{1,0:T(8,128)S(1)}, u32[]{:S(2)}, u32[]{:S(2)}) collective-permute-start(f32[6,1536]{1,0:T(8,128)S(1)} %get-tuple-element.511.refs_0_), channel_id=1, source_target_pairs={{0,16},{4,20},{8,24},{12,28},{16,0},{20,4},{24,8},{28,12},{1,17},{... | collective-permute-start | bytes 110600 | tf_op jit(solution)/shard_map/ppermute | solution.py:230
  (184 other events, 1714.2 us)
Sparse Core Ops, SparseCore 0:
  350.5 94.6 reduce-scatter.5
  448.8 95.0 reduce-scatter.7
  596.3 140.6 reduce-scatter.3

commit v4 on v2

--- a/solution.py
+++ b/solution.py
@@ -119,8 +119,9 @@
 
 def ring_body(kind, rows, count, sides, split, *refs):
     table, wholes = refs[0], refs[1 : 1 + count]
-    came = refs[1 + count : -len(sides) - count - 1]
-    outs, own, sems = refs[-len(sides) - count - 1 : -count - 1], refs[-count - 1 : -1], refs[-1]
+    out_count = count if kind == "end" else len(sides)
+    came = refs[1 + count : -out_count - count - 1]
+    outs, own, sems = refs[-out_count - count - 1 : -count - 1], refs[-count - 1 : -1], refs[-1]
     copies = []
     for side, (entry, first, last) in enumerate(sides):
         begin = pl.multiple_of(table[entry] * rows + first, rows // 2)
@@ -153,14 +154,14 @@
             else:
                 total = came[0][:, cols].astype(F32) + came[1][:, cols].astype(F32)
                 total += mine.astype(F32)
-                if split is None:
-                    outs[side][:, cols] = total
+                if k:
+                    outs[k][...] = total
                 else:
                     outer, inner = split
                     size = total.shape[1] // (outer * inner)
                     for at in range(outer * inner):
                         to = pl.ds(at // inner * size, size)
-                        outs[side][at % inner, :, to] = total[:, at * size : (at + 1) * size]
+                        outs[k][at % inner, :, to] = total[:, at * size : (at + 1) * size]
 
 
 class RingSum:
@@ -183,10 +184,10 @@
         else:
             sides = [(middle + step, 0, rows), (middle - step, 0, rows)]
         size = half if kind == "begin" else rows
-        shape = (size, sum(widths))
-        if split is not None:
-            shape = (split[1], size, shape[1] // split[1])
-        out = (shape, F32 if kind == "end" else BF16)
+        outs = [((size, sum(widths)), BF16)] * len(sides)
+        if kind == "end":
+            outs = [((split[1], rows, widths[0] // split[1]), F32)]
+            outs += [((rows, cols), F32) for cols in widths[1:]]
         hbm = pl.BlockSpec(memory_space=pltpu.HBM)
         return call(
             functools.partial(ring_body, kind, rows, len(widths), sides, split),
@@ -195,8 +196,8 @@
             [pl.BlockSpec(memory_space=pltpu.SMEM)]
             + [hbm] * len(widths)
             + [whole_spec(v.shape) for v in self.came],
-            [out] * len(sides),
-            [whole_spec(out[0])] * len(sides),
+            outs,
+            [whole_spec(shape) for shape, _ in outs],
             [pltpu.VMEM((len(sides), rows, cols), BF16) for cols in widths]
             + [pltpu.SemaphoreType.DMA((len(sides), len(widths)))],
             wait=wait,
@@ -213,17 +214,17 @@
         self.came = (send_next(up, self.n), send_prev(down, self.n))
         self.left -= 1
 
-    def total(self, split=None):
+    def totals(self, split):
         if self.direct:
-            whole = jnp.concatenate(self.wholes, 1)
-            total = lax.psum_scatter(whole, "fsdp", scatter_dimension=0, tiled=True).astype(F32)
-            if split is not None:
-                total = total.reshape(total.shape[0], *split, -1).transpose(2, 0, 1, 3)
-                total = total.reshape(*total.shape[:2], -1)
-            return total
+            totals = [
+                lax.psum_scatter(v, "fsdp", scatter_dimension=0, tiled=True).astype(F32)
+                for v in self.wholes
+            ]
+            first = totals[0].reshape(totals[0].shape[0], *split, -1).transpose(2, 0, 1, 3)
+            return [first.reshape(*first.shape[:2], -1)] + totals[1:]
         while self.left:
             self.step()
-        return self.run("end", 0, split=split)[0]
+        return self.run("end", 0, split=split)
 
 
 def swap_fsdp(values, n, bit):
@@ -298,9 +299,9 @@
     return [jnp.where(m, block, zero) for m in masks]
 
 
-def rows_call(body, ins, outs, sums=(), wait=(), shifts=None):
+def rows_call(body, ins, outs, sums=(), wait=(), shifts=None, most=128):
     rows = outs[0][0][0]
-    block = next((v for v in (128, 96) if rows % v == 0), rows)
+    block = next((v for v in (most, 96) if rows % v == 0), rows)
     steps = rows // block
     shifts = shifts or [0] * len(ins)
     in_specs = []
@@ -499,8 +500,8 @@
     refs[-1][...] = total_of(refs[:-1]).astype(BF16)
 
 
-def sum_terms(terms, shape):
-    return rows_call(sum_terms_body, terms, [(shape, BF16)])[0]
+def sum_terms(terms, shape, most=128):
+    return rows_call(sum_terms_body, terms, [(shape, BF16)], most=most)[0]
 
 
 def self_forward_body(
@@ -1020,11 +1021,11 @@
     ]
 
     raw_swapped = [swap_chip(audio_states[c]) for c in both]
-    cross_came, raw_swapped[0] = self_ring.turn([cross_came, raw_swapped[0]], params)
+    cross_came, raw_swapped[0] = self_ring.turn([cross_came, raw_swapped[0]])
     cross_shard = jnp.concatenate((cross_own, cross_came, cross_kv[0], cross_kv[1]), axis=1)
     raw = gather_rows(audio_states[0], raw_swapped[0])
+    self_ring.turn()
     full_self = [norm_pair(0, raw, params)]
-    self_ring.turn()
     raw_swapped[1:] = self_ring.turn(raw_swapped[1:])
     raw = [gather_rows(audio_states[c], raw_swapped[c]) for c in range(1, clips)]
     full_self += [norm_pair(0, v, params) for v in raw]
@@ -1037,8 +1038,8 @@
     for c in both:
         rows, attn, log, keep, send = self_forward(*full_self[c], self_w, units)
         if c == 0:
-            send, *out_swapped = cross_ring.turn([send, *out_swapped])
-            seen_out = [gather_rows(out_grad[k], out_swapped[k]) for k in both]
+            send, out_swapped[0] = cross_ring.turn([send, out_swapped[0]])
+            seen_out = [gather_rows(out_grad[0], out_swapped[0])]
         else:
             keep_0, seen_0, other_0 = mid_terms[0][1:]
             send, other_0 = cross_ring.turn([send, other_0])
@@ -1069,7 +1070,8 @@
             send, came = early_gather.turn([send, came])
             full_ffn.append(gather_rows(normed_late, came))
         else:
-            (send,) = early_gather.turn([send])
+            send, *out_swapped[1:] = early_gather.turn([send, *out_swapped[1:]])
+            seen_out += [gather_rows(out_grad[k], out_swapped[k]) for k in range(1, clips)]
         cross_q.append(queries)
         cross_attn.append(attn)
         stream, normed = norm_forward(2, (stream_mid[c], keep, swap_core(send)), params, share)
@@ -1166,7 +1168,7 @@
         if c == 0:
             send, kv_came = tick([send, kv_came])
         else:
-            send, cross_came, text_came = tick([send, cross_came, text_came])
+            send, text_came = tick([send, text_came])
         in_terms.append(sum_over_tp(keep, send))
         self_grads.append(grads)
         if c == 0:
@@ -1178,11 +1180,10 @@
             quarter = text_keep.shape[1] // 2
             text_seen = text_keep + swap_core(text_send).astype(F32)
             text_came = swap_chip(text_seen[:, quarter:].astype(BF16))
-        else:
-            cross_total = sum_clips(sum_terms((cross_shares[0], cross_came), cross_came.shape))
     text_grad = text_seen[:, :quarter] + text_came.astype(F32)
     grad = weight_grad((sum(full_self, ()), self_grads))
-    qkv_sum = RingSum([grad], n, table)
+    cross_g = sum_terms((cross_shares[0], cross_came), cross_came.shape, most=256)
+    ring = RingSum([grad, cross_g], n, table)
     late_terms = [sum_over_tp(*out_terms[c]) for c in both]
     audio_grad, layer_out = [], []
     for c in both:
@@ -1190,20 +1191,20 @@
         norm_sums[0].append(sums)
         audio_grad.append(grad)
         if c == 0:
-            qkv_sum.step()
+            ring.step()
     norm_total = SmallSum(jnp.concatenate([sum(v)[:2] for v in norm_sums], 0), n)
     audio_grad = join(audio_grad)
-    qkv_sum.step()
-    norm_total.step()
+    ring.step()
     norm_total.step()
     layer_out.append(sum_terms((stream_late[0], *late_terms[0]), (share, width)))
-    qkv_sum.step([out_total])
     norm_total.step()
+    ring.step()
     norm_total.step()
     for c in range(1, clips):
         layer_out.append(sum_terms((stream_late[c], *late_terms[c]), (share, width)))
+    norm_total.step()
     layer_out = join(layer_out)
-    qkv_total = qkv_sum.total(split=(pairs, 3))
+    qkv_total, cross_total = ring.totals((pairs, 3))
     norm_total = norm_total.total()
 
     def cut(total, begin, count=1):
@@ -1215,9 +1216,9 @@
         text_grad.astype(BF16),
         qkv_total,
         cut(out_total, 0).astype(F32).T,
-        cut(cross_total, 0).astype(F32),
+        cut(cross_total, 0),
         jnp.stack((cut(out_total, 1), cut(out_total, 2))).astype(F32),
-        cut(cross_total, 1).astype(F32).T,
+        cut(cross_total, 1).T,
         jnp.concatenate([v[:, :part] for v in ffn_totals], 1).astype(F32),
         jnp.concatenate([v[:, part:] for v in ffn_totals], 1).astype(F32).T,
         norm_total[0::2],

time: 742 us -> 732 us (0.987)
  waiting for transfers between devices: 176 us -> 157 us
  starting transfers between devices: 74.3 us -> 85.3 us
    ppermute x20, waiting for transfers between devices: 40.2 us -> 19.1 us  [send_next(): lax.ppermute(values, 'fsdp', [(ring[k], ring[(k + 1) % n]) for k in range...]
    reduce_scatter x4 -> x3, waiting for transfers between devices: 19.4 us -> 0.01 us  [sum_clips(): return lax.psum_scatter(grad, 'fsdp', scatter_dimension=0, tiled=True)]
    ppermute x6, waiting for transfers between devices: 19.2 us -> 34.6 us  [swap_fsdp(): return lax.ppermute(values, 'fsdp', [(i, i ^ bit) for i in range(n)])]
    ppermute x23, waiting for transfers between devices: 50.5 us -> 60.3 us  [swap_chip(): return lax.ppermute(values, 'tp', [(t, t ^ 2) for t in range(4)])]
    unnamed x240 -> x214, local copies, waits for them, and re-layouts: 42.7 us -> 41.2 us
  transfers between devices with their start and end apart: 100 -> 99, of which waited for: 45 -> 41; matrix products, arithmetic and copies ran while one was open for 3% -> 3% of each run, Pallas kernels for 53% -> 54%
where the time goes in v4:
time: 732 us; the launch traced here: 723 us
  Pallas kernels  393 us (54%)
  waiting for transfers between devices  157 us (21%)
  starting transfers between devices  85.3 us (12%)
  local copies, waits for them, and re-layouts  55.2 us (8%)
  other arithmetic  16.4 us (2%)
  between operations  15.5 us (2%)
    pallas_call x79, Pallas kernels, call(): pl.pallas_call(run, grid=grid, in_specs=list(in_specs) + [hbm] * len(wait...  393 us
    ppermute x23, waiting for transfers between devices, swap_chip(): return lax.ppermute(values, 'tp', [(t, t ^ 2) for t in range(4)])  60.3 us
    unnamed x214, local copies, waits for them, and re-layouts  41.2 us
    ppermute x6, waiting for transfers between devices, swap_fsdp(): return lax.ppermute(values, 'fsdp', [(i, i ^ bit) for i in range(n)])  34.6 us
    ppermute x23, starting transfers between devices, swap_chip(): return lax.ppermute(values, 'tp', [(t, t ^ 2) for t in range(4)])  28.3 us
    ppermute x20, starting transfers between devices, send_next(): lax.ppermute(values, 'fsdp', [(ring[k], ring[(k + 1) % n]) for k in range...  27.1 us
    ppermute x27, waiting for transfers between devices, swap_core(): return lax.ppermute(values, 'tp', [(t, t ^ 1) for t in range(4)])  25.5 us
    ppermute x20, waiting for transfers between devices, send_next(): lax.ppermute(values, 'fsdp', [(ring[k], ring[(k + 1) % n]) for k in range...  19.1 us
  transfers between devices with their start and end apart: 99, of which 41 were waited for; matrix products, arithmetic and copies ran while one was open for 3% of the time, Pallas kernels for 54%

profile of v4, /device:TPU:0, one launch (start us, length us, event | category | flops | bytes accessed | tf_op | source)
XLA Modules:
  0.0 722.7 jit_solution(15761916758037205127)
XLA Ops:
  18.8 16.8 %collective-permute-done.2.refs_2_ = bf16[192,768]{1,0:T(8,128)(2,1)S(1)} collective-permute-done((bf16[192,768]{1,0:T(8,128)(2,1)S(1)}, bf16[192,768]{1,0:T(8,128)(2,1)S(1)}, u32[]{:S(2)}, u32[]{:S(2)}) %collective-permute-start.2) | collective-permute-done | bytes 294944 | tf_op jit(solution)/shard_map/ppermute | solution.py:23
  44.3 10.7 %collective-permute-done.5 = bf16[1,6,192]{2,1,0:T(8,128)(2,1)S(1)} collective-permute-done((bf16[1,6,192]{2,1,0:T(8,128)(2,1)S(1)}, bf16[1,6,192]{2,1,0:T(8,128)(2,1)S(1)}, u32[]{:S(2)}, u32[]{:S(2)}) %collective-permute-start.5) | collective-permute-done | bytes 2336 | tf_op jit(solution)/shard_map/ppermute | solution.py:231
  59.3 4.3 collective-permute-start.7
  63.6 13.0 %collective-permute-done.7 = bf16[4,6,192]{2,1,0:T(8,128)(2,1)S(1)} collective-permute-done((bf16[4,6,192]{2,1,0:T(8,128)(2,1)S(1)}, bf16[4,6,192]{2,1,0:T(8,128)(2,1)S(1)}, u32[]{:S(2)}, u32[]{:S(2)}) %collective-permute-start.7) | collective-permute-done | bytes 9248 | tf_op jit(solution)/shard_map/ppermute | solution.py:231
  77.3 4.7 norm_pair_body.2
  89.6 4.8 norm_pair_body.3
  104.4 22.6 %self_forward_body.2 = (bf16[1024,1152]{1,0:T(8,128)(2,1)}, bf16[1024,384]{1,0:T(8,128)(2,1)S(1)}, f32[24,1024]{1,0:T(8,128)S(1)}, f32[512,1536]{1,0:T(8,128)}, ...) custom-call(bf16[512,1536]{1,0:T(8,128)(2,1)} %copy-done.7, bf16[512,1536]{1,0:T(8,128)(2,1)} %get-tuple-element.268.refs_1_, ...), custom_call_target="tpu_custom_call" | custom-call | flops 1000 | tf_op jit(solution)/shard_map/self_forward_body/pallas_call | solution.py:276
  135.9 22.4 %self_forward_body.3 = (bf16[1024,1152]{1,0:T(8,128)(2,1)}, bf16[1024,384]{1,0:T(8,128)(2,1)S(1)}, f32[24,1024]{1,0:T(8,128)S(1)}, f32[512,1536]{1,0:T(8,128)}, ...) custom-call(bf16[512,1536]{1,0:T(8,128)(2,1)} %copy-done.9, bf16[512,1536]{1,0:T(8,128)(2,1)} %get-tuple-element.289.refs_1_.refs_3_, ...), custom_call_target="tpu_custom_call" | custom-call | flops 1000 | tf_op jit(solution)/shard_map/self_forward_body/pallas_call | solution.py:276
  173.1 8.6 %collective-permute-done.25.refs_0_ = bf16[192,2304]{1,0:T(8,128)(2,1)S(1)} collective-permute-done((bf16[192,2304]{1,0:T(8,128)(2,1)S(1)}, bf16[192,2304]{1,0:T(8,128)(2,1)S(1)}, u32[]{:S(2)}, u32[]{:S(2)}) %collective-permute-start.25) | collective-permute-done | bytes 884768 | tf_op jit(solution)/shard_map/ppermute | solution.py:56
  199.1 6.3 place_pieces_body.5
  209.6 4.7 collective-permute-done.34.refs_2_
  217.4 10.3 %cross_forward_body.2 = (bf16[512,768]{1,0:T(8,128)(2,1)S(1)}, bf16[512,768]{1,0:T(8,128)(2,1)S(1)}, f32[256,1536]{1,0:T(8,128)}, bf16[256,1536]{1,0:T(8,128)(2,1)}, f32[8,128]{1,0:T(8,128)S(1)}) custom-call(bf16[256,1536]{1,0:T(8,128)(2,1)} %copy-done.29, bf16[256,1536]{1,0:T(8,128)(2,1)} %copy-done.32, ...), custom_call_target="tpu_custom_call" | custom-call | flops 1000 | tf_op jit(solution)/shard_map/cross_forward_body/pallas_call | solution.py:276
  243.2 10.3 %cross_forward_body.3 = (bf16[512,768]{1,0:T(8,128)(2,1)S(1)}, bf16[512,768]{1,0:T(8,128)(2,1)S(1)}, f32[256,1536]{1,0:T(8,128)}, bf16[256,1536]{1,0:T(8,128)(2,1)}, f32[8,128]{1,0:T(8,128)S(1)}) custom-call(bf16[256,1536]{1,0:T(8,128)(2,1)} %copy-done.31, bf16[256,1536]{1,0:T(8,128)(2,1)} %copy-done.81, ...), custom_call_target="tpu_custom_call" | custom-call | flops 1000 | tf_op jit(solution)/shard_map/cross_forward_body/pallas_call | solution.py:276
  277.4 16.6 %ffn_first_body.2 = (bf16[1024,768]{1,0:T(8,128)(2,1)S(1)}, bf16[1024,768]{1,0:T(8,128)(2,1)}, f32[1024,1536]{1,0:T(8,128)}, f32[1024,1536]{1,0:T(8,128)}, f32[8,128]{1,0:T(8,128)S(1)}) custom-call(bf16[512,1536]{1,0:T(8,128)(2,1)} %copy-done, bf16[512,1536]{1,0:T(8,128)(2,1)} %collective-permute-done.43.refs_1_, ...), custom_call_target="tpu_custom_call" | custom-call | flops 1000 | tf_op jit(solution)/shard_map/ffn_first_body/pallas_call | solution.py:276
  300.3 16.6 %ffn_first_body.3 = (bf16[1024,768]{1,0:T(8,128)(2,1)S(1)}, bf16[1024,768]{1,0:T(8,128)(2,1)}, f32[1024,1536]{1,0:T(8,128)}, f32[1024,1536]{1,0:T(8,128)}, f32[8,128]{1,0:T(8,128)S(1)}) custom-call(bf16[512,1536]{1,0:T(8,128)(2,1)} %constant_dynamic-update-slice_fusion.5.refs_0_.refs_2_, bf16[512,1536]{1,0:T(8,128)(2,1)} %copy-done.64, ...), custom_call_target="tpu_custom_call" | custom-call | flops 1000 | tf_op jit(solution)/shard_map/ffn_first_body/pallas_call | solution.py:276
  320.2 15.7 %weight_grad_body.5 = (bf16[1536,1536]{1,0:T(8,128)(2,1)}, f32[8,128]{1,0:T(8,128)S(1)}) custom-call(bf16[512,1536]{1,0:T(8,128)(2,1)S(1)} %copy-done.1, bf16[512,1536]{1,0:T(8,128)(2,1)} %collective-permute-done.43.refs_1_, bf16[512,1536]{1,0:T(8,128)(2,1)} %constant_dynamic-update-slice_fusion.5.refs_0_.refs_2_, bf16[512,1536]{1,0:T(8,128)(2,1)} %copy-done.64, ...), custom_call_target="tpu_custom_call" | custom-call | flops 1000 | tf_op jit(solution)/shard_map/weight_grad_body/pallas_call | solution.py:276
  338.1 6.7 collective-permute-done.58.refs_8_
  348.7 19.1 %ffn_second_body.2 = (bf16[1024,768]{1,0:T(8,128)(2,1)S(1)}, bf16[1024,768]{1,0:T(8,128)(2,1)}, f32[512,1536]{1,0:T(8,128)}, bf16[512,1536]{1,0:T(8,128)(2,1)}, ...) custom-call(bf16[512,1536]{1,0:T(8,128)(2,1)} %copy-done, ...), custom_call_target="tpu_custom_call" | custom-call | flops 1000 | tf_op jit(solution)/shard_map/ffn_second_body/pallas_call | solution.py:276
  377.1 19.3 %ffn_second_body.3 = (bf16[1024,768]{1,0:T(8,128)(2,1)S(1)}, bf16[1024,768]{1,0:T(8,128)(2,1)}, f32[512,1536]{1,0:T(8,128)}, bf16[512,1536]{1,0:T(8,128)(2,1)}, ...) custom-call(bf16[512,1536]{1,0:T(8,128)(2,1)} %constant_dynamic-update-slice_fusion.5.refs_0_.refs_2_, ...), custom_call_target="tpu_custom_call" | custom-call | flops 1000 | tf_op jit(solution)/shard_map/ffn_second_body/pallas_call | solution.py:276
  408.9 16.1 %weight_grad_body.6 = (bf16[1536,1536]{1,0:T(8,128)(2,1)}, f32[8,128]{1,0:T(8,128)S(1)}) custom-call(bf16[512,1536]{1,0:T(8,128)(2,1)S(1)} %copy-done.2, bf16[512,1536]{1,0:T(8,128)(2,1)} %collective-permute-done.43.refs_1_, bf16[512,1536]{1,0:T(8,128)(2,1)} %constant_dynamic-update-slice_fusion.5.refs_0_.refs_2_, bf16[512,1536]{1,0:T(8,128)(2,1)} %copy-done.64, ...), custom_call_target="tpu_custom_call" | custom-call | flops 1000 | tf_op jit(solution)/shard_map/weight_grad_body/pallas_call | solution.py:276
  430.5 11.4 %cross_backward_body.2 = (bf16[512,768]{1,0:T(8,128)(2,1)S(1)}, f32[64,768]{1,0:T(8,128)S(1)}, bf16[64,768]{1,0:T(8,128)(2,1)S(1)}, f32[256,1536]{1,0:T(8,128)},...) custom-call(bf16[256,1536]{1,0:T(8,128)(2,1)} %copy-done.34, bf16[256,1536]{1,0:T(8,128)(2,1)} %copy-done.82, ...), custom_call_target="tpu_custom_call" | custom-call | flops 1000 | tf_op jit(solution)/shard_map/cross_backward_body/pallas_call | solution.py:276
  452.1 11.6 %cross_backward_body.3 = (bf16[512,768]{1,0:T(8,128)(2,1)S(1)}, f32[64,768]{1,0:T(8,128)S(1)}, bf16[64,768]{1,0:T(8,128)(2,1)S(1)}, f32[256,1536]{1,0:T(8,128)},...) custom-call(bf16[256,1536]{1,0:T(8,128)(2,1)} %copy-done.35, bf16[256,1536]{1,0:T(8,128)(2,1)} %copy-done.83, ...), custom_call_target="tpu_custom_call" | custom-call | flops 1000 | tf_op jit(solution)/shard_map/cross_backward_body/pallas_call | solution.py:276
  470.2 10.3 %weight_grad_body.7 = (bf16[1536,768]{1,0:T(8,128)(2,1)}, bf16[1536,768]{1,0:T(8,128)(2,1)}, f32[8,128]{1,0:T(8,128)S(1)}) custom-call(bf16[256,1536]{1,0:T(8,128)(2,1)S(1)} %copy-done.30, bf16[256,1536]{1,0:T(8,128)(2,1)S(1)} %copy-done.33, bf16[256,1536]{1,0:T(8,128)(2,1)} %copy-done.31, bf16[256,1536]{1,0:T(8,128)(2,1)} %copy-done.81, ...), custom_call_target="tpu_custom_call" | custom-call | flops 1000 | tf_op jit(solution)/shard_map/weight_grad_body/pallas_call | solution.py:276
  488.5 28.4 %self_backward_body.2 = (bf16[1024,1152]{1,0:T(8,128)(2,1)}, f32[512,1536]{1,0:T(8,128)}, bf16[512,1536]{1,0:T(8,128)(2,1)}, f32[8,128]{1,0:T(8,128)S(1)}) custom-call(bf16[512,1536]{1,0:T(8,128)(2,1)} %copy-done.65, bf16[512,1536]{1,0:T(8,128)(2,1)} %copy-done.73, bf16[1536,1536]{1,0:T(8,128)(2,1)} %get-tuple-element.279.refs_2_.refs_3_, ...), custom_call_target="tpu_custom_call" | custom-call | flops 1000 | tf_op jit(solution)/shard_map/self_backward_body/pallas_call | solution.py:276
  526.6 8.8 %weight_grad_body.8 = (bf16[1536,1152]{1,0:T(8,128)(2,1)}, f32[8,128]{1,0:T(8,128)S(1)}) custom-call(bf16[512,1536]{1,0:T(8,128)(2,1)} %copy-done.65, bf16[512,1536]{1,0:T(8,128)(2,1)} %copy-done.73, bf16[512,1536]{1,0:T(8,128)(2,1)} %copy-done.66, bf16[512,1536]{1,0:T(8,128)(2,1)} %copy-done.74, bf16[128,1536]{1,0:T(8,128)(2,1)S(1)} %bitcast.45, ...), custom_call_target="tpu_custom_call" | custom-call | flops 1000 | tf_op jit(solution)/shard_map/weight_grad_body/pallas_call | solution.py:276
  541.7 28.6 %self_backward_body.3 = (bf16[1024,1152]{1,0:T(8,128)(2,1)}, f32[512,1536]{1,0:T(8,128)}, bf16[512,1536]{1,0:T(8,128)(2,1)}, f32[8,128]{1,0:T(8,128)S(1)}) custom-call(bf16[512,1536]{1,0:T(8,128)(2,1)} %copy-done.66, bf16[512,1536]{1,0:T(8,128)(2,1)} %copy-done.74, bf16[1536,1536]{1,0:T(8,128)(2,1)} %get-tuple-element.279.refs_2_.refs_3_, ...), custom_call_target="tpu_custom_call" | custom-call | flops 1000 | tf_op jit(solution)/shard_map/self_backward_body/pallas_call | solution.py:276
  570.3 20.8 %collective-permute-done.75.refs_1_ = bf16[2,16,1536]{2,1,0:T(8,128)(2,1)S(1)} collective-permute-done((bf16[2,16,1536]{2,1,0:T(8,128)(2,1)S(1)}, bf16[2,16,1536]{2,1,0:T(8,128)(2,1)S(1)}, u32[]{:S(2)}, u32[]{:S(2)}) %collective-permute-start.75) | collective-permute-done | bytes 98336 | tf_op jit(solution)/shard_map/ppermute | solution.py:23
  597.0 13.0 %weight_grad_body.9 = (bf16[1536,1152]{1,0:T(8,128)(2,1)}, f32[8,128]{1,0:T(8,128)S(1)}) custom-call(bf16[512,1536]{1,0:T(8,128)(2,1)S(1)} %copy-done.8, bf16[512,1536]{1,0:T(8,128)(2,1)} %get-tuple-element.268.refs_1_, bf16[512,1536]{1,0:T(8,128)(2,1)} %copy-done.9, bf16[512,1536]{1,0:T(8,128)(2,1)} %get-tuple-element.289.refs_1_.refs_3_, ...), custom_call_target="tpu_custom_call" | custom-call | flops 1000 | tf_op jit(solution)/shard_map/weight_grad_body/pallas_call | solution.py:276
  610.1 5.5 sum_terms_body.3
  644.5 8.0 %collective-permute-done.85.refs_3_ = bf16[192,1920]{1,0:T(8,128)(2,1)S(1)} collective-permute-done((bf16[192,1920]{1,0:T(8,128)(2,1)S(1)}, bf16[192,1920]{1,0:T(8,128)(2,1)S(1)}, u32[]{:S(2)}, u32[]{:S(2)}) %collective-permute-start.85) | collective-permute-done | bytes 737312 | tf_op jit(solution)/shard_map/ppermute | solution.py:56
  665.0 8.4 %collective-permute-done.88.refs_1_ = f32[6,1536]{1,0:T(8,128)S(1)} collective-permute-done((f32[6,1536]{1,0:T(8,128)S(1)}, f32[6,1536]{1,0:T(8,128)S(1)}, u32[]{:S(2)}, u32[]{:S(2)}) %collective-permute-start.88) | collective-permute-done | bytes 36896 | tf_op jit(solution)/shard_map/ppermute | solution.py:23
  688.0 10.9 %collective-permute-done.92.refs_1_ = f32[6,1536]{1,0:T(8,128)S(1)} collective-permute-done((f32[6,1536]{1,0:T(8,128)S(1)}, f32[6,1536]{1,0:T(8,128)S(1)}, u32[]{:S(2)}, u32[]{:S(2)}) %collective-permute-start.92) | collective-permute-done | bytes 36896 | tf_op jit(solution)/shard_map/ppermute | solution.py:231
  (524 shorter events, 291.9 us)
Async XLA Ops:
  7.2 676.8 %reduce-scatter.6.cloned.1.call-start = ((), (), s32[]{:S(2)}) async-start(), calls=%async_computation.4 | async-start | bytes 5308416 | tf_op jit(solution)/shard_map/reduce_scatter | solution.py:1100
  8.8 26.9 %collective-permute-start.3 = (bf16[256,1536]{1,0:T(8,128)(2,1)S(1)}, bf16[256,1536]{1,0:T(8,128)(2,1)S(1)}, u32[]{:S(2)}, u32[]{:S(2)}) collective-permute-start(bf16[256,1536]{1,0:T(8,128)(2,1)S(1)} %get-tuple-element.515.refs_0_), channel_id=1, source_target_pairs={{0,2},{1,3},{2,0},{3,1},{4,6},{5,7},{6,4},{7,5},{8,10},{9,11},{10,... | collective-permute-start | bytes 2359304 | tf_op jit(solution)/shard_map/ppermute | solution.py:23
  38.9 38.4 %collective-permute-start.4 = (bf16[512,1536]{1,0:T(8,128)(2,1)}, bf16[512,1536]{1,0:T(8,128)(2,1)}, u32[]{:S(2)}, u32[]{:S(2)}) collective-permute-start(bf16[512,1536]{1,0:T(8,128)(2,1)} %pad_maximum_fusion.refs_0_), channel_id=1, source_target_pairs={{0,1},{1,0},{2,3},{3,2},{4,5},{5,4},{6,7},{7,6},{8,9},{9,8},{10,11... | collective-permute-start | bytes 4718600 | tf_op jit(solution)/shard_map/ppermute | solution.py:27
  42.8 40.4 %collective-permute-start.12 = (bf16[256,1536]{1,0:T(8,128)(2,1)S(1)}, bf16[256,1536]{1,0:T(8,128)(2,1)}, u32[]{:S(2)}, u32[]{:S(2)}) collective-permute-start(bf16[256,1536]{1,0:T(8,128)(2,1)S(1)} %get-tuple-element.514.refs_0_), channel_id=1, source_target_pairs={{0,2},{1,3},{2,0},{3,1},{4,6},{5,7},{6,4},{7,5},{8,10},{9,11},{10,... | collective-permute-start | bytes 2359304 | tf_op jit(solution)/shard_map/ppermute | solution.py:23
  57.2 26.0 %collective-permute-start.10 = (bf16[192,1536]{1,0:T(8,128)(2,1)}, bf16[192,1536]{1,0:T(8,128)(2,1)S(1)}, u32[]{:S(2)}, u32[]{:S(2)}) collective-permute-start(bf16[192,1536]{1,0:T(8,128)(2,1)} %get-tuple-element.269.refs_3_), channel_id=1, source_target_pairs={{0,8},{8,16},{16,24},{24,28},{28,20},{20,12},{12,4},{4,0},{1,9},{9... | collective-permute-start | bytes 1769480 | tf_op jit(solution)/shard_map/ppermute | solution.py:56
  58.8 24.4 %collective-permute-start.11 = (bf16[192,1536]{1,0:T(8,128)(2,1)}, bf16[192,1536]{1,0:T(8,128)(2,1)S(1)}, u32[]{:S(2)}, u32[]{:S(2)}) collective-permute-start(bf16[192,1536]{1,0:T(8,128)(2,1)} %copy-done.38), channel_id=1, source_target_pairs={{8,0},{16,8},{24,16},{28,24},{20,28},{12,20},{4,12},{0,4},{9,1},{1... | collective-permute-start | bytes 1769480 | tf_op jit(solution)/shard_map/ppermute | solution.py:61
  96.8 30.8 %collective-permute-start.17 = (bf16[192,2304]{1,0:T(8,128)(2,1)S(1)}, bf16[192,2304]{1,0:T(8,128)(2,1)S(1)}, u32[]{:S(2)}, u32[]{:S(2)}) collective-permute-start(bf16[192,2304]{1,0:T(8,128)(2,1)S(1)} %get-tuple-element.282.refs_0_), channel_id=1, source_target_pairs={{8,0},{16,8},{24,16},{28,24},{20,28},{12,20},{4,12},{0,4},{9,1},{1... | collective-permute-start | bytes 2654216 | tf_op jit(solution)/shard_map/ppermute | solution.py:61
  96.9 30.7 %collective-permute-start.16 = (bf16[192,2304]{1,0:T(8,128)(2,1)S(1)}, bf16[192,2304]{1,0:T(8,128)(2,1)S(1)}, u32[]{:S(2)}, u32[]{:S(2)}) collective-permute-start(bf16[192,2304]{1,0:T(8,128)(2,1)S(1)} %get-tuple-element.282.refs_0_), channel_id=1, source_target_pairs={{0,8},{8,16},{16,24},{24,28},{28,20},{20,12},{12,4},{4,0},{1,9},{9... | collective-permute-start | bytes 2654216 | tf_op jit(solution)/shard_map/ppermute | solution.py:56
  99.1 28.6 %collective-permute-start.18 = (bf16[256,1536]{1,0:T(8,128)(2,1)S(1)}, bf16[256,1536]{1,0:T(8,128)(2,1)S(1)}, u32[]{:S(2)}, u32[]{:S(2)}) collective-permute-start(bf16[256,1536]{1,0:T(8,128)(2,1)S(1)} %get-tuple-element.513.refs_1_), channel_id=1, source_target_pairs={{0,2},{1,3},{2,0},{3,1},{4,6},{5,7},{6,4},{7,5},{8,10},{9,11},{10,... | collective-permute-start | bytes 2359304 | tf_op jit(solution)/shard_map/ppermute | solution.py:23
  128.9 29.5 %collective-permute-start.20 = (bf16[192,2304]{1,0:T(8,128)(2,1)S(1)}, bf16[192,2304]{1,0:T(8,128)(2,1)S(1)}, u32[]{:S(2)}, u32[]{:S(2)}) collective-permute-start(bf16[192,2304]{1,0:T(8,128)(2,1)S(1)} %get-tuple-element.286.refs_1_), channel_id=1, source_target_pairs={{0,8},{8,16},{16,24},{24,28},{28,20},{20,12},{12,4},{4,0},{1,9},{9... | collective-permute-start | bytes 2654216 | tf_op jit(solution)/shard_map/ppermute | solution.py:56
  129.7 28.8 %collective-permute-start.21 = (bf16[192,2304]{1,0:T(8,128)(2,1)}, bf16[192,2304]{1,0:T(8,128)(2,1)S(1)}, u32[]{:S(2)}, u32[]{:S(2)}) collective-permute-start(bf16[192,2304]{1,0:T(8,128)(2,1)} %get-tuple-element.287.refs_2_), channel_id=1, source_target_pairs={{8,0},{16,8},{24,16},{28,24},{20,28},{12,20},{4,12},{0,4},{9,1},{1... | collective-permute-start | bytes 2654216 | tf_op jit(solution)/shard_map/ppermute | solution.py:61
  135.3 23.1 %collective-permute-start.22 = (bf16[256,1536]{1,0:T(8,128)(2,1)S(1)}, bf16[256,1536]{1,0:T(8,128)(2,1)S(1)}, u32[]{:S(2)}, u32[]{:S(2)}) collective-permute-start(bf16[256,1536]{1,0:T(8,128)(2,1)S(1)} %get-tuple-element.293), channel_id=1, source_target_pairs={{0,2},{1,3},{2,0},{3,1},{4,6},{5,7},{6,4},{7,5},{8,10},{9,11},{10,... | collective-permute-start | bytes 2359304 | tf_op jit(solution)/shard_map/ppermute | solution.py:23
  159.6 22.1 %collective-permute-start.25 = (bf16[192,2304]{1,0:T(8,128)(2,1)S(1)}, bf16[192,2304]{1,0:T(8,128)(2,1)S(1)}, u32[]{:S(2)}, u32[]{:S(2)}) collective-permute-start(bf16[192,2304]{1,0:T(8,128)(2,1)S(1)} %get-tuple-element.302.refs_3_), channel_id=1, source_target_pairs={{0,8},{8,16},{16,24},{24,28},{28,20},{20,12},{12,4},{4,0},{1,9},{9... | collective-permute-start | bytes 2654216 | tf_op jit(solution)/shard_map/ppermute | solution.py:56
  166.2 22.7 %collective-permute-start.29 = (bf16[256,1536]{1,0:T(8,128)(2,1)S(1)}, bf16[256,1536]{1,0:T(8,128)(2,1)S(1)}, u32[]{:S(2)}, u32[]{:S(2)}) collective-permute-start(bf16[256,1536]{1,0:T(8,128)(2,1)S(1)} %get-tuple-element.307), channel_id=1, source_target_pairs={{0,2},{1,3},{2,0},{3,1},{4,6},{5,7},{6,4},{7,5},{8,10},{9,11},{10,... | collective-permute-start | bytes 2359304 | tf_op jit(solution)/shard_map/ppermute | solution.py:23
  242.3 35.1 %collective-permute-start.44 = (bf16[512,1536]{1,0:T(8,128)(2,1)}, bf16[512,1536]{1,0:T(8,128)(2,1)}, u32[]{:S(2)}, u32[]{:S(2)}) collective-permute-start(bf16[512,1536]{1,0:T(8,128)(2,1)} %pad_maximum_fusion.2.refs_2_.refs_4_), channel_id=1, source_target_pairs={{0,1},{1,0},{2,3},{3,2},{4,5},{5,4},{6,7},{7,6},{8,9},{9,8},{10,11... | collective-permute-start | bytes 4718600 | tf_op jit(solution)/shard_map/ppermute | solution.py:27
  264.7 29.3 %collective-permute-start.50 = (bf16[256,1536]{1,0:T(8,128)(2,1)S(1)}, bf16[256,1536]{1,0:T(8,128)(2,1)S(1)}, u32[]{:S(2)}, u32[]{:S(2)}) collective-permute-start(bf16[256,1536]{1,0:T(8,128)(2,1)S(1)} %get-tuple-element.343), channel_id=1, source_target_pairs={{0,2},{1,3},{2,0},{3,1},{4,6},{5,7},{6,4},{7,5},{8,10},{9,11},{10,... | collective-permute-start | bytes 2359304 | tf_op jit(solution)/shard_map/ppermute | solution.py:23
  269.4 24.7 %collective-permute-start.49 = (bf16[192,1536]{1,0:T(8,128)(2,1)S(1)}, bf16[192,1536]{1,0:T(8,128)(2,1)S(1)}, u32[]{:S(2)}, u32[]{:S(2)}) collective-permute-start(bf16[192,1536]{1,0:T(8,128)(2,1)S(1)} %get-tuple-element.342.refs_0_), channel_id=1, source_target_pairs={{8,0},{16,8},{24,16},{28,24},{20,28},{12,20},{4,12},{0,4},{9,1},{1... | collective-permute-start | bytes 1769480 | tf_op jit(solution)/shard_map/ppermute | solution.py:61
  269.8 24.3 %collective-permute-start.48 = (bf16[192,1536]{1,0:T(8,128)(2,1)S(1)}, bf16[192,1536]{1,0:T(8,128)(2,1)S(1)}, u32[]{:S(2)}, u32[]{:S(2)}) collective-permute-start(bf16[192,1536]{1,0:T(8,128)(2,1)S(1)} %get-tuple-element.342.refs_0_), channel_id=1, source_target_pairs={{0,8},{8,16},{16,24},{24,28},{28,20},{20,12},{12,4},{4,0},{1,9},{9... | collective-permute-start | bytes 1769480 | tf_op jit(solution)/shard_map/ppermute | solution.py:56
  295.9 22.2 %collective-permute-start.51 = (bf16[192,1536]{1,0:T(8,128)(2,1)S(1)}, bf16[192,1536]{1,0:T(8,128)(2,1)S(1)}, u32[]{:S(2)}, u32[]{:S(2)}) collective-permute-start(bf16[192,1536]{1,0:T(8,128)(2,1)S(1)} %get-tuple-element.348.refs_1_), channel_id=1, source_target_pairs={{0,8},{8,16},{16,24},{24,28},{28,20},{20,12},{12,4},{4,0},{1,9},{9... | collective-permute-start | bytes 1769480 | tf_op jit(solution)/shard_map/ppermute | solution.py:56
  348.7 361.0 %reduce-scatter.8.cloned.1.call-start = ((), (), s32[]{:S(2)}) async-start(), calls=%async_computation.5 | async-start | bytes 5308416 | tf_op jit(solution)/shard_map/reduce_scatter | solution.py:1100
  375.5 22.1 %collective-permute-start.61 = (bf16[256,1536]{1,0:T(8,128)(2,1)S(1)}, bf16[256,1536]{1,0:T(8,128)(2,1)S(1)}, u32[]{:S(2)}, u32[]{:S(2)}) collective-permute-start(bf16[256,1536]{1,0:T(8,128)(2,1)S(1)} %get-tuple-element.376), channel_id=1, source_target_pairs={{0,2},{1,3},{2,0},{3,1},{4,6},{5,7},{6,4},{7,5},{8,10},{9,11},{10,... | collective-permute-start | bytes 2359304 | tf_op jit(solution)/shard_map/ppermute | solution.py:23
  425.9 287.1 %reduce-scatter.4.cloned.1.call-start = ((), (), s32[]{:S(2)}) async-start(), calls=%async_computation.3 | async-start | bytes 3981312 | tf_op jit(solution)/shard_map/reduce_scatter | solution.py:1100
  483.8 34.7 %collective-permute-start.70 = (bf16[256,1536]{1,0:T(8,128)(2,1)S(1)}, bf16[256,1536]{1,0:T(8,128)(2,1)S(1)}, u32[]{:S(2)}, u32[]{:S(2)}) collective-permute-start(bf16[256,1536]{1,0:T(8,128)(2,1)S(1)} %get-tuple-element.424), channel_id=1, source_target_pairs={{0,2},{1,3},{2,0},{3,1},{4,6},{5,7},{6,4},{7,5},{8,10},{9,11},{10,... | collective-permute-start | bytes 2359304 | tf_op jit(solution)/shard_map/ppermute | solution.py:23
  485.2 31.7 %collective-permute-start.72 = (bf16[2,64,768]{2,1,0:T(8,128)(2,1)S(1)}, bf16[2,64,768]{2,1,0:T(8,128)(2,1)S(1)}, u32[]{:S(2)}, u32[]{:S(2)}) collective-permute-start(bf16[2,64,768]{2,1,0:T(8,128)(2,1)S(1)} %pad_maximum_fusion.10), channel_id=1, source_target_pairs={{0,2},{1,3},{2,0},{3,1},{4,6},{5,7},{6,4},{7,5},{8,10},{9,11},{10,... | collective-permute-start | bytes 589832 | tf_op jit(solution)/shard_map/ppermute | solution.py:23
  535.4 74.7 %collective-permute-start.77 = (bf16[1536,768]{1,0:T(8,128)(2,1)}, bf16[1536,768]{1,0:T(8,128)(2,1)}, u32[]{:S(2)}, u32[]{:S(2)}) collective-permute-start(bf16[1536,768]{1,0:T(8,128)(2,1)} %get-tuple-element.452), channel_id=1, source_target_pairs={{0,2},{1,3},{2,0},{3,1},{4,6},{5,7},{6,4},{7,5},{8,10},{9,11},{10,... | collective-permute-start | bytes 7077896 | tf_op jit(solution)/shard_map/ppermute | solution.py:23
  540.9 50.2 %collective-permute-start.75 = (bf16[2,16,1536]{2,1,0:T(8,128)(2,1)S(1)}, bf16[2,16,1536]{2,1,0:T(8,128)(2,1)S(1)}, u32[]{:S(2)}, u32[]{:S(2)}) collective-permute-start(bf16[2,16,1536]{2,1,0:T(8,128)(2,1)S(1)} %slice.210), channel_id=1, source_target_pairs={{0,2},{1,3},{2,0},{3,1},{4,6},{5,7},{6,4},{7,5},{8,10},{9,11},{10,... | collective-permute-start | bytes 294920 | tf_op jit(solution)/shard_map/ppermute | solution.py:23
  591.2 28.4 %collective-permute-start.59 = (bf16[512,1536]{1,0:T(8,128)(2,1)}, bf16[512,1536]{1,0:T(8,128)(2,1)}, u32[]{:S(2)}, u32[]{:S(2)}) collective-permute-start(bf16[512,1536]{1,0:T(8,128)(2,1)} %get-tuple-element.372), channel_id=1, source_target_pairs={{0,1},{1,0},{2,3},{3,2},{4,5},{5,4},{6,7},{7,6},{8,9},{9,8},{10,11... | collective-permute-start | bytes 4718600 | tf_op jit(solution)/shard_map/ppermute | solution.py:27
  591.7 30.9 %collective-permute-start.80 = (bf16[512,1536]{1,0:T(8,128)(2,1)}, bf16[512,1536]{1,0:T(8,128)(2,1)}, u32[]{:S(2)}, u32[]{:S(2)}) collective-permute-start(bf16[512,1536]{1,0:T(8,128)(2,1)} %get-tuple-element.461), channel_id=1, source_target_pairs={{0,1},{1,0},{2,3},{3,2},{4,5},{5,4},{6,7},{7,6},{8,9},{9,8},{10,11... | collective-permute-start | bytes 4718600 | tf_op jit(solution)/shard_map/ppermute | solution.py:27
  591.7 33.3 %collective-permute-start.79 = (bf16[256,1536]{1,0:T(8,128)(2,1)}, bf16[256,1536]{1,0:T(8,128)(2,1)}, u32[]{:S(2)}, u32[]{:S(2)}) collective-permute-start(bf16[256,1536]{1,0:T(8,128)(2,1)} %get-tuple-element.459), channel_id=1, source_target_pairs={{0,2},{1,3},{2,0},{3,1},{4,6},{5,7},{6,4},{7,5},{8,10},{9,11},{10,... | collective-permute-start | bytes 2359304 | tf_op jit(solution)/shard_map/ppermute | solution.py:23
  636.2 26.5 %collective-permute-start.78 = (bf16[256,1536]{1,0:T(8,128)(2,1)S(1)}, bf16[256,1536]{1,0:T(8,128)(2,1)S(1)}, u32[]{:S(2)}, u32[]{:S(2)}) collective-permute-start(bf16[256,1536]{1,0:T(8,128)(2,1)S(1)} %get-tuple-element.457), channel_id=1, source_target_pairs={{0,2},{1,3},{2,0},{3,1},{4,6},{5,7},{6,4},{7,5},{8,10},{9,11},{10,... | collective-permute-start | bytes 2359304 | tf_op jit(solution)/shard_map/ppermute | solution.py:23
  637.7 48.1 %collective-permute-start.87 = (bf16[256,1536]{1,0:T(8,128)(2,1)}, bf16[256,1536]{1,0:T(8,128)(2,1)S(1)}, u32[]{:S(2)}, u32[]{:S(2)}) collective-permute-start(bf16[256,1536]{1,0:T(8,128)(2,1)} %get-tuple-element.485), channel_id=1, source_target_pairs={{0,2},{1,3},{2,0},{3,1},{4,6},{5,7},{6,4},{7,5},{8,10},{9,11},{10,... | collective-permute-start | bytes 2359304 | tf_op jit(solution)/shard_map/ppermute | solution.py:23
  680.8 22.5 %collective-permute-start.93 = (bf16[192,1920]{1,0:T(8,128)(2,1)}, bf16[192,1920]{1,0:T(8,128)(2,1)}, u32[]{:S(2)}, u32[]{:S(2)}) collective-permute-start(bf16[192,1920]{1,0:T(8,128)(2,1)} %get-tuple-element.501), channel_id=1, source_target_pairs={{0,8},{8,16},{16,24},{24,28},{28,20},{20,12},{12,4},{4,0},{1,9},{9... | collective-permute-start | bytes 2211848 | tf_op jit(solution)/shard_map/ppermute | solution.py:56
  (170 other events, 1589.2 us)
Sparse Core Ops, SparseCore 0:
  348.8 94.8 reduce-scatter.5
  447.4 95.0 reduce-scatter.7
  546.1 79.2 reduce-scatter.3

commit v5 on v4

--- a/solution.py
+++ b/solution.py
@@ -818,7 +818,7 @@
 
 def ffn_products(x, grad, up_ref, down_ref, active_ref, hidden_ref):
     units = up_ref.shape[1]
-    size = units // 3 if units % (3 * 128) == 0 else units
+    size = units // 2 if units % (2 * 128) == 0 else units
     out = back = 0.0
     for begin in range(0, units, size):
         cols = slice(begin, begin + size)
@@ -951,6 +951,27 @@
     return outs[0] if split == 1 else outs
 
 
+def finish_body(early_ref, late_ref, out_ref, up_ref, down_ref, mixed_ref, kv_ref):
+    half = early_ref.shape[1] // 2
+    for k, ref in enumerate((early_ref, late_ref)):
+        cols = slice(k * half, (k + 1) * half)
+        up_ref[:, cols] = ref[:, :half].astype(F32)
+        down_ref[:, cols] = ref[:, half:].astype(F32)
+    units = out_ref.shape[1] // 3
+    mixed_ref[...] = out_ref[:, :units].astype(F32)
+    for k in range(2):
+        kv_ref[k] = out_ref[:, (k + 1) * units : (k + 2) * units].astype(F32)
+
+
+def finish(early, late, out):
+    rows, wide = early.shape
+    units = out.shape[1] // 3
+    ins = (early, late, out)
+    outs = [((rows, wide), F32), ((rows, wide), F32), ((rows, units), F32), ((2, rows, units), F32)]
+    specs = [whole_spec(v.shape) for v in ins]
+    return call(finish_body, (1,), ins, specs, outs, [whole_spec(s) for s, _ in outs])
+
+
 def text_project_body(text_ref, weight_ref, out_ref):
     out_ref[...] = times(text_ref[...], weight_ref[...]).astype(BF16)
 
@@ -1021,11 +1042,11 @@
     ]
 
     raw_swapped = [swap_chip(audio_states[c]) for c in both]
-    cross_came, raw_swapped[0] = self_ring.turn([cross_came, raw_swapped[0]])
+    (raw_swapped[0],) = self_ring.turn(raw_swapped[:1], params)
+    raw = gather_rows(audio_states[0], raw_swapped[0])
+    full_self = [norm_pair(0, raw, params)]
+    (cross_came,) = self_ring.turn([cross_came])
     cross_shard = jnp.concatenate((cross_own, cross_came, cross_kv[0], cross_kv[1]), axis=1)
-    raw = gather_rows(audio_states[0], raw_swapped[0])
-    self_ring.turn()
-    full_self = [norm_pair(0, raw, params)]
     raw_swapped[1:] = self_ring.turn(raw_swapped[1:])
     raw = [gather_rows(audio_states[c], raw_swapped[c]) for c in range(1, clips)]
     full_self += [norm_pair(0, v, params) for v in raw]
@@ -1168,7 +1189,7 @@
         if c == 0:
             send, kv_came = tick([send, kv_came])
         else:
-            send, text_came = tick([send, text_came])
+            (send,) = tick([send])
         in_terms.append(sum_over_tp(keep, send))
         self_grads.append(grads)
         if c == 0:
@@ -1180,10 +1201,11 @@
             quarter = text_keep.shape[1] // 2
             text_seen = text_keep + swap_core(text_send).astype(F32)
             text_came = swap_chip(text_seen[:, quarter:].astype(BF16))
-    text_grad = text_seen[:, :quarter] + text_came.astype(F32)
     grad = weight_grad((sum(full_self, ()), self_grads))
     cross_g = sum_terms((cross_shares[0], cross_came), cross_came.shape, most=256)
     ring = RingSum([grad, cross_g], n, table)
+    (text_came,) = tick([text_came])
+    text_grad = text_seen[:, :quarter] + text_came.astype(F32)
     late_terms = [sum_over_tp(*out_terms[c]) for c in both]
     audio_grad, layer_out = [], []
     for c in both:
@@ -1204,6 +1226,7 @@
         layer_out.append(sum_terms((stream_late[c], *late_terms[c]), (share, width)))
     norm_total.step()
     layer_out = join(layer_out)
+    finished = finish(*ffn_totals, out_total)
     qkv_total, cross_total = ring.totals((pairs, 3))
     norm_total = norm_total.total()
 
@@ -1215,12 +1238,12 @@
         audio_grad,
         text_grad.astype(BF16),
         qkv_total,
-        cut(out_total, 0).astype(F32).T,
+        finished[2].T,
         cut(cross_total, 0),
-        jnp.stack((cut(out_total, 1), cut(out_total, 2))).astype(F32),
+        finished[3],
         cut(cross_total, 1).T,
-        jnp.concatenate([v[:, :part] for v in ffn_totals], 1).astype(F32),
-        jnp.concatenate([v[:, part:] for v in ffn_totals], 1).astype(F32).T,
+        finished[0],
+        finished[1].T,
         norm_total[0::2],
         norm_total[1::2],
     )

time: 732 us -> 721 us (0.985)
  Pallas kernels: 393 us -> 404 us
  other arithmetic: 16.4 us -> 6.5 us
    ppermute x23, waiting for transfers between devices: 60.3 us -> 37.2 us  [swap_chip(): return lax.ppermute(values, 'tp', [(t, t ^ 2) for t in range(4)])]
    ppermute x20, waiting for transfers between devices: 19.1 us -> 29.9 us  [send_next(): lax.ppermute(values, 'fsdp', [(ring[k], ring[(k + 1) % n]) for k in range...]
    pallas_call x79 -> x81, Pallas kernels: 393 us -> 404 us  [call(): pl.pallas_call(run, grid=grid, in_specs=list(in_specs) + [hbm] * len(wait...]
    ppermute x20, waiting for transfers between devices: 17.2 us -> 25.7 us  [send_prev(): lax.ppermute(values, 'fsdp', [(ring[(k + 1) % n], ring[k]) for k in range...]
    unnamed x214 -> x228, local copies, waits for them, and re-layouts: 41.2 us -> 40.1 us
  transfers between devices with their start and end apart: 99 -> 99, of which waited for: 41 -> 46; matrix products, arithmetic and copies ran while one was open for 3% -> 2% of each run, Pallas kernels for 54% -> 56%
where the time goes in v5:
time: 721 us; the launch traced here: 711 us
  Pallas kernels  404 us (56%)
  waiting for transfers between devices  155 us (21%)
  starting transfers between devices  81 us (11%)
  local copies, waits for them, and re-layouts  48.9 us (7%)
  between operations  15.6 us (2%)
    pallas_call x81, Pallas kernels, call(): pl.pallas_call(run, grid=grid, in_specs=list(in_specs) + [hbm] * len(wait...  404 us
    unnamed x228, local copies, waits for them, and re-layouts  40.1 us
    ppermute x23, waiting for transfers between devices, swap_chip(): return lax.ppermute(values, 'tp', [(t, t ^ 2) for t in range(4)])  37.2 us
    ppermute x6, waiting for transfers between devices, swap_fsdp(): return lax.ppermute(values, 'fsdp', [(i, i ^ bit) for i in range(n)])  33.6 us
    ppermute x20, waiting for transfers between devices, send_next(): lax.ppermute(values, 'fsdp', [(ring[k], ring[(k + 1) % n]) for k in range...  29.9 us
    ppermute x27, waiting for transfers between devices, swap_core(): return lax.ppermute(values, 'tp', [(t, t ^ 1) for t in range(4)])  28.8 us
    ppermute x23, starting transfers between devices, swap_chip(): return lax.ppermute(values, 'tp', [(t, t ^ 2) for t in range(4)])  27.7 us
    ppermute x20, waiting for transfers between devices, send_prev(): lax.ppermute(values, 'fsdp', [(ring[(k + 1) % n], ring[k]) for k in range...  25.7 us
  transfers between devices with their start and end apart: 99, of which 46 were waited for; matrix products, arithmetic and copies ran while one was open for 2% of the time, Pallas kernels for 56%

profile of v5, /device:TPU:0, one launch (start us, length us, event | category | flops | bytes accessed | tf_op | source)
XLA Modules:
  0.0 710.8 jit_solution(15862113791501863030)
XLA Ops:
  18.0 9.8 %collective-permute-done.3 = bf16[1,6,192]{2,1,0:T(8,128)(2,1)S(1)} collective-permute-done((bf16[1,6,192]{2,1,0:T(8,128)(2,1)S(1)}, bf16[1,6,192]{2,1,0:T(8,128)(2,1)S(1)}, u32[]{:S(2)}, u32[]{:S(2)}) %collective-permute-start.3) | collective-permute-done | bytes 2336 | tf_op jit(solution)/shard_map/ppermute | solution.py:231
  42.5 4.7 norm_pair_body.2
  55.2 9.8 %collective-permute-done.12.refs_2_ = bf16[256,1536]{1,0:T(8,128)(2,1)S(1)} collective-permute-done((bf16[256,1536]{1,0:T(8,128)(2,1)S(1)}, bf16[256,1536]{1,0:T(8,128)(2,1)S(1)}, u32[]{:S(2)}, u32[]{:S(2)}) %collective-permute-start.12) | collective-permute-done | bytes 786464 | tf_op jit(solution)/shard_map/ppermute | solution.py:23
  74.0 4.8 norm_pair_body.3
  88.8 22.5 %self_forward_body.2 = (bf16[1024,1152]{1,0:T(8,128)(2,1)}, bf16[1024,384]{1,0:T(8,128)(2,1)S(1)}, f32[24,1024]{1,0:T(8,128)S(1)}, f32[512,1536]{1,0:T(8,128)}, ...) custom-call(bf16[512,1536]{1,0:T(8,128)(2,1)} %copy-done.7, bf16[512,1536]{1,0:T(8,128)(2,1)} %get-tuple-element.271.refs_1_, ...), custom_call_target="tpu_custom_call" | custom-call | flops 1000 | tf_op jit(solution)/shard_map/self_forward_body/pallas_call | solution.py:276
  119.5 22.5 %self_forward_body.3 = (bf16[1024,1152]{1,0:T(8,128)(2,1)}, bf16[1024,384]{1,0:T(8,128)(2,1)S(1)}, f32[24,1024]{1,0:T(8,128)S(1)}, f32[512,1536]{1,0:T(8,128)}, ...) custom-call(bf16[512,1536]{1,0:T(8,128)(2,1)} %copy-done.9, bf16[512,1536]{1,0:T(8,128)(2,1)} %get-tuple-element.295.refs_1_.refs_3_, ...), custom_call_target="tpu_custom_call" | custom-call | flops 1000 | tf_op jit(solution)/shard_map/self_forward_body/pallas_call | solution.py:276
  155.0 10.3 %collective-permute-done.25.refs_0_ = bf16[192,2304]{1,0:T(8,128)(2,1)S(1)} collective-permute-done((bf16[192,2304]{1,0:T(8,128)(2,1)S(1)}, bf16[192,2304]{1,0:T(8,128)(2,1)S(1)}, u32[]{:S(2)}, u32[]{:S(2)}) %collective-permute-start.25) | collective-permute-done | bytes 884768 | tf_op jit(solution)/shard_map/ppermute | solution.py:56
  182.7 6.3 place_pieces_body.5
  193.3 4.7 collective-permute-done.34.refs_2_
  201.0 10.3 %cross_forward_body.2 = (bf16[512,768]{1,0:T(8,128)(2,1)S(1)}, bf16[512,768]{1,0:T(8,128)(2,1)S(1)}, f32[256,1536]{1,0:T(8,128)}, bf16[256,1536]{1,0:T(8,128)(2,1)}, f32[8,128]{1,0:T(8,128)S(1)}) custom-call(bf16[256,1536]{1,0:T(8,128)(2,1)} %copy-done.29, bf16[256,1536]{1,0:T(8,128)(2,1)} %copy-done.32, ...), custom_call_target="tpu_custom_call" | custom-call | flops 1000 | tf_op jit(solution)/shard_map/cross_forward_body/pallas_call | solution.py:276
  226.8 10.4 %cross_forward_body.3 = (bf16[512,768]{1,0:T(8,128)(2,1)S(1)}, bf16[512,768]{1,0:T(8,128)(2,1)S(1)}, f32[256,1536]{1,0:T(8,128)}, bf16[256,1536]{1,0:T(8,128)(2,1)}, f32[8,128]{1,0:T(8,128)S(1)}) custom-call(bf16[256,1536]{1,0:T(8,128)(2,1)} %copy-done.31, bf16[256,1536]{1,0:T(8,128)(2,1)} %copy-done.87, ...), custom_call_target="tpu_custom_call" | custom-call | flops 1000 | tf_op jit(solution)/shard_map/cross_forward_body/pallas_call | solution.py:276
  259.6 18.6 %ffn_first_body.2 = (bf16[1024,768]{1,0:T(8,128)(2,1)S(1)}, bf16[1024,768]{1,0:T(8,128)(2,1)}, f32[1024,1536]{1,0:T(8,128)}, f32[1024,1536]{1,0:T(8,128)}, f32[8,128]{1,0:T(8,128)S(1)}) custom-call(bf16[512,1536]{1,0:T(8,128)(2,1)} %copy-done, bf16[512,1536]{1,0:T(8,128)(2,1)} %collective-permute-done.43.refs_1_, ...), custom_call_target="tpu_custom_call" | custom-call | flops 1000 | tf_op jit(solution)/shard_map/ffn_first_body/pallas_call | solution.py:276
  284.1 18.8 %ffn_first_body.3 = (bf16[1024,768]{1,0:T(8,128)(2,1)S(1)}, bf16[1024,768]{1,0:T(8,128)(2,1)}, f32[1024,1536]{1,0:T(8,128)}, f32[1024,1536]{1,0:T(8,128)}, f32[8,128]{1,0:T(8,128)S(1)}) custom-call(bf16[512,1536]{1,0:T(8,128)(2,1)} %copy-done.70, bf16[512,1536]{1,0:T(8,128)(2,1)} %copy-done.71, bf16[512,1536]{1,0:T(8,128)(2,1)} %pad_maximum_fusion.3.refs_2_.refs_6_, ...), custom_call_target="tpu_custom_call" | custom-call | flops 1000 | tf_op jit(solution)/shard_map/ffn_first_body/pallas_call | solution.py:276
  306.2 15.7 %weight_grad_body.5 = (bf16[1536,1536]{1,0:T(8,128)(2,1)}, f32[8,128]{1,0:T(8,128)S(1)}) custom-call(bf16[512,1536]{1,0:T(8,128)(2,1)S(1)} %copy-done.1, bf16[512,1536]{1,0:T(8,128)(2,1)} %collective-permute-done.43.refs_1_, bf16[512,1536]{1,0:T(8,128)(2,1)} %copy-done.70, bf16[512,1536]{1,0:T(8,128)(2,1)} %copy-done.71, ...), custom_call_target="tpu_custom_call" | custom-call | flops 1000 | tf_op jit(solution)/shard_map/weight_grad_body/pallas_call | solution.py:276
  324.1 6.7 collective-permute-done.58.refs_8_
  335.6 21.5 %ffn_second_body.2 = (bf16[1024,768]{1,0:T(8,128)(2,1)S(1)}, bf16[1024,768]{1,0:T(8,128)(2,1)}, f32[512,1536]{1,0:T(8,128)}, bf16[512,1536]{1,0:T(8,128)(2,1)}, ...) custom-call(bf16[512,1536]{1,0:T(8,128)(2,1)} %copy-done, ...), custom_call_target="tpu_custom_call" | custom-call | flops 1000 | tf_op jit(solution)/shard_map/ffn_second_body/pallas_call | solution.py:276
  366.4 21.6 %ffn_second_body.3 = (bf16[1024,768]{1,0:T(8,128)(2,1)S(1)}, bf16[1024,768]{1,0:T(8,128)(2,1)}, f32[512,1536]{1,0:T(8,128)}, bf16[512,1536]{1,0:T(8,128)(2,1)}, ...) custom-call(bf16[512,1536]{1,0:T(8,128)(2,1)} %copy-done.70, bf16[512,1536]{1,0:T(8,128)(2,1)} %copy-done.71, ...), custom_call_target="tpu_custom_call" | custom-call | flops 1000 | tf_op jit(solution)/shard_map/ffn_second_body/pallas_call | solution.py:276
  400.4 16.0 %weight_grad_body.6 = (bf16[1536,1536]{1,0:T(8,128)(2,1)}, f32[8,128]{1,0:T(8,128)S(1)}) custom-call(bf16[512,1536]{1,0:T(8,128)(2,1)S(1)} %copy-done.2, bf16[512,1536]{1,0:T(8,128)(2,1)} %collective-permute-done.43.refs_1_, bf16[512,1536]{1,0:T(8,128)(2,1)} %copy-done.70, bf16[512,1536]{1,0:T(8,128)(2,1)} %copy-done.71, ...), custom_call_target="tpu_custom_call" | custom-call | flops 1000 | tf_op jit(solution)/shard_map/weight_grad_body/pallas_call | solution.py:276
  421.9 11.4 %cross_backward_body.2 = (bf16[512,768]{1,0:T(8,128)(2,1)S(1)}, f32[64,768]{1,0:T(8,128)S(1)}, bf16[64,768]{1,0:T(8,128)(2,1)S(1)}, f32[256,1536]{1,0:T(8,128)},...) custom-call(bf16[256,1536]{1,0:T(8,128)(2,1)} %copy-done.34, bf16[256,1536]{1,0:T(8,128)(2,1)} %copy-done.88, ...), custom_call_target="tpu_custom_call" | custom-call | flops 1000 | tf_op jit(solution)/shard_map/cross_backward_body/pallas_call | solution.py:276
  442.7 11.3 %cross_backward_body.3 = (bf16[512,768]{1,0:T(8,128)(2,1)S(1)}, f32[64,768]{1,0:T(8,128)S(1)}, bf16[64,768]{1,0:T(8,128)(2,1)S(1)}, f32[256,1536]{1,0:T(8,128)},...) custom-call(bf16[256,1536]{1,0:T(8,128)(2,1)} %copy-done.35, bf16[256,1536]{1,0:T(8,128)(2,1)} %copy-done.89, ...), custom_call_target="tpu_custom_call" | custom-call | flops 1000 | tf_op jit(solution)/shard_map/cross_backward_body/pallas_call | solution.py:276
  460.5 10.2 %weight_grad_body.7 = (bf16[1536,768]{1,0:T(8,128)(2,1)}, bf16[1536,768]{1,0:T(8,128)(2,1)}, f32[8,128]{1,0:T(8,128)S(1)}) custom-call(bf16[256,1536]{1,0:T(8,128)(2,1)S(1)} %copy-done.30, bf16[256,1536]{1,0:T(8,128)(2,1)S(1)} %copy-done.33, bf16[256,1536]{1,0:T(8,128)(2,1)} %copy-done.31, bf16[256,1536]{1,0:T(8,128)(2,1)} %copy-done.87, ...), custom_call_target="tpu_custom_call" | custom-call | flops 1000 | tf_op jit(solution)/shard_map/weight_grad_body/pallas_call | solution.py:276
  478.7 28.5 %self_backward_body.2 = (bf16[1024,1152]{1,0:T(8,128)(2,1)}, f32[512,1536]{1,0:T(8,128)}, bf16[512,1536]{1,0:T(8,128)(2,1)}, f32[8,128]{1,0:T(8,128)S(1)}) custom-call(bf16[512,1536]{1,0:T(8,128)(2,1)} %copy-done.72, bf16[512,1536]{1,0:T(8,128)(2,1)} %copy-done.81, bf16[1536,1536]{1,0:T(8,128)(2,1)} %get-tuple-element.285.refs_2_.refs_3_, ...), custom_call_target="tpu_custom_call" | custom-call | flops 1000 | tf_op jit(solution)/shard_map/self_backward_body/pallas_call | solution.py:276
  516.2 8.8 %weight_grad_body.8 = (bf16[1536,1152]{1,0:T(8,128)(2,1)}, f32[8,128]{1,0:T(8,128)S(1)}) custom-call(bf16[512,1536]{1,0:T(8,128)(2,1)} %copy-done.72, bf16[512,1536]{1,0:T(8,128)(2,1)} %copy-done.81, bf16[512,1536]{1,0:T(8,128)(2,1)} %copy-done.73, bf16[512,1536]{1,0:T(8,128)(2,1)} %copy-done.82, bf16[128,1536]{1,0:T(8,128)(2,1)S(1)} %bitcast.39, ...), custom_call_target="tpu_custom_call" | custom-call | flops 1000 | tf_op jit(solution)/shard_map/weight_grad_body/pallas_call | solution.py:276
  530.1 28.5 %self_backward_body.3 = (bf16[1024,1152]{1,0:T(8,128)(2,1)}, f32[512,1536]{1,0:T(8,128)}, bf16[512,1536]{1,0:T(8,128)(2,1)}, f32[8,128]{1,0:T(8,128)S(1)}) custom-call(bf16[512,1536]{1,0:T(8,128)(2,1)} %copy-done.73, bf16[512,1536]{1,0:T(8,128)(2,1)} %copy-done.82, bf16[1536,1536]{1,0:T(8,128)(2,1)} %get-tuple-element.285.refs_2_.refs_3_, ...), custom_call_target="tpu_custom_call" | custom-call | flops 1000 | tf_op jit(solution)/shard_map/self_backward_body/pallas_call | solution.py:276
  559.7 7.5 %collective-permute-done.74 = bf16[2,32,1536]{2,1,0:T(8,128)(2,1)} collective-permute-done((bf16[2,32,1536]{2,1,0:T(8,128)(2,1)}, bf16[2,32,1536]{2,1,0:T(8,128)(2,1)}, u32[]{:S(2)}, u32[]{:S(2)}) %collective-permute-start.74) | collective-permute-done | bytes 196640 | tf_op jit(solution)/shard_map/ppermute | solution.py:27
  572.5 13.0 %weight_grad_body.9 = (bf16[1536,1152]{1,0:T(8,128)(2,1)}, f32[8,128]{1,0:T(8,128)S(1)}) custom-call(bf16[512,1536]{1,0:T(8,128)(2,1)S(1)} %copy-done.8, bf16[512,1536]{1,0:T(8,128)(2,1)} %get-tuple-element.271.refs_1_, bf16[512,1536]{1,0:T(8,128)(2,1)} %copy-done.9, bf16[512,1536]{1,0:T(8,128)(2,1)} %get-tuple-element.295.refs_1_.refs_3_, ...), custom_call_target="tpu_custom_call" | custom-call | flops 1000 | tf_op jit(solution)/shard_map/weight_grad_body/pallas_call | solution.py:276
  585.5 5.5 sum_terms_body.3
  593.5 4.3 collective-permute-done.75.refs_0_
  609.0 9.6 %collective-permute-done.83.refs_4_ = bf16[96,1920]{1,0:T(8,128)(2,1)S(1)} collective-permute-done((bf16[96,1920]{1,0:T(8,128)(2,1)S(1)}, bf16[96,1920]{1,0:T(8,128)(2,1)S(1)}, u32[]{:S(2)}, u32[]{:S(2)}) %collective-permute-start.83) | collective-permute-done | bytes 368672 | tf_op jit(solution)/shard_map/ppermute | solution.py:61
  631.1 8.7 %collective-permute-done.85.refs_3_ = bf16[192,1920]{1,0:T(8,128)(2,1)S(1)} collective-permute-done((bf16[192,1920]{1,0:T(8,128)(2,1)S(1)}, bf16[192,1920]{1,0:T(8,128)(2,1)S(1)}, u32[]{:S(2)}, u32[]{:S(2)}) %collective-permute-start.85) | collective-permute-done | bytes 737312 | tf_op jit(solution)/shard_map/ppermute | solution.py:56
  651.2 9.1 %collective-permute-done.88.refs_1_ = f32[6,1536]{1,0:T(8,128)S(1)} collective-permute-done((f32[6,1536]{1,0:T(8,128)S(1)}, f32[6,1536]{1,0:T(8,128)S(1)}, u32[]{:S(2)}, u32[]{:S(2)}) %collective-permute-start.88) | collective-permute-done | bytes 36896 | tf_op jit(solution)/shard_map/ppermute | solution.py:23
  670.2 14.6 %collective-permute-done.89.refs_1_ = f32[6,1536]{1,0:T(8,128)S(1)} collective-permute-done((f32[6,1536]{1,0:T(8,128)S(1)}, f32[6,1536]{1,0:T(8,128)S(1)}, u32[]{:S(2)}, u32[]{:S(2)}) %collective-permute-start.89) | collective-permute-done | bytes 36896 | tf_op jit(solution)/shard_map/ppermute | solution.py:231
  (534 shorter events, 289.0 us)
Async XLA Ops:
  7.2 685.5 %reduce-scatter.4.cloned.1.call-start = ((), (), s32[]{:S(2)}) async-start(), calls=%async_computation.3 | async-start | bytes 5308416 | tf_op jit(solution)/shard_map/reduce_scatter | solution.py:1121
  9.8 27.1 %collective-permute-start.1 = (bf16[192,1536]{1,0:T(8,128)(2,1)S(1)}, bf16[192,1536]{1,0:T(8,128)(2,1)}, u32[]{:S(2)}, u32[]{:S(2)}) collective-permute-start(bf16[192,1536]{1,0:T(8,128)(2,1)S(1)} %pad_maximum_fusion.4.refs_0_), channel_id=1, source_target_pairs={{8,0},{16,8},{24,16},{28,24},{20,28},{12,20},{4,12},{0,4},{9,1},{1... | collective-permute-start | bytes 1769480 | tf_op jit(solution)/shard_map/ppermute | solution.py:61
  12.8 24.1 %collective-permute-start = (bf16[192,1536]{1,0:T(8,128)(2,1)S(1)}, bf16[192,1536]{1,0:T(8,128)(2,1)}, u32[]{:S(2)}, u32[]{:S(2)}) collective-permute-start(bf16[192,1536]{1,0:T(8,128)(2,1)S(1)} %pad_maximum_fusion.4.refs_0_), channel_id=1, source_target_pairs={{0,8},{8,16},{16,24},{24,28},{28,20},{20,12},{12,4},{4,0},{1,9},{9... | collective-permute-start | bytes 1769480 | tf_op jit(solution)/shard_map/ppermute | solution.py:56
  40.8 24.2 %collective-permute-start.12 = (bf16[256,1536]{1,0:T(8,128)(2,1)S(1)}, bf16[256,1536]{1,0:T(8,128)(2,1)S(1)}, u32[]{:S(2)}, u32[]{:S(2)}) collective-permute-start(bf16[256,1536]{1,0:T(8,128)(2,1)S(1)} %get-tuple-element.526.refs_0_), channel_id=1, source_target_pairs={{0,2},{1,3},{2,0},{3,1},{4,6},{5,7},{6,4},{7,5},{8,10},{9,11},{10,... | collective-permute-start | bytes 2359304 | tf_op jit(solution)/shard_map/ppermute | solution.py:23
  81.2 30.1 %collective-permute-start.17 = (bf16[192,2304]{1,0:T(8,128)(2,1)S(1)}, bf16[192,2304]{1,0:T(8,128)(2,1)S(1)}, u32[]{:S(2)}, u32[]{:S(2)}) collective-permute-start(bf16[192,2304]{1,0:T(8,128)(2,1)S(1)} %get-tuple-element.288.refs_0_), channel_id=1, source_target_pairs={{8,0},{16,8},{24,16},{28,24},{20,28},{12,20},{4,12},{0,4},{9,1},{1... | collective-permute-start | bytes 2654216 | tf_op jit(solution)/shard_map/ppermute | solution.py:61
  82.0 29.3 %collective-permute-start.16 = (bf16[192,2304]{1,0:T(8,128)(2,1)S(1)}, bf16[192,2304]{1,0:T(8,128)(2,1)S(1)}, u32[]{:S(2)}, u32[]{:S(2)}) collective-permute-start(bf16[192,2304]{1,0:T(8,128)(2,1)S(1)} %get-tuple-element.288.refs_0_), channel_id=1, source_target_pairs={{0,8},{8,16},{16,24},{24,28},{28,20},{20,12},{12,4},{4,0},{1,9},{9... | collective-permute-start | bytes 2654216 | tf_op jit(solution)/shard_map/ppermute | solution.py:56
  83.5 27.8 %collective-permute-start.18 = (bf16[256,1536]{1,0:T(8,128)(2,1)S(1)}, bf16[256,1536]{1,0:T(8,128)(2,1)S(1)}, u32[]{:S(2)}, u32[]{:S(2)}) collective-permute-start(bf16[256,1536]{1,0:T(8,128)(2,1)S(1)} %get-tuple-element.525.refs_1_), channel_id=1, source_target_pairs={{0,2},{1,3},{2,0},{3,1},{4,6},{5,7},{6,4},{7,5},{8,10},{9,11},{10,... | collective-permute-start | bytes 2359304 | tf_op jit(solution)/shard_map/ppermute | solution.py:23
  112.5 29.6 %collective-permute-start.20 = (bf16[192,2304]{1,0:T(8,128)(2,1)S(1)}, bf16[192,2304]{1,0:T(8,128)(2,1)S(1)}, u32[]{:S(2)}, u32[]{:S(2)}) collective-permute-start(bf16[192,2304]{1,0:T(8,128)(2,1)S(1)} %get-tuple-element.292.refs_1_), channel_id=1, source_target_pairs={{0,8},{8,16},{16,24},{24,28},{28,20},{20,12},{12,4},{4,0},{1,9},{9... | collective-permute-start | bytes 2654216 | tf_op jit(solution)/shard_map/ppermute | solution.py:56
  113.9 28.1 %collective-permute-start.21 = (bf16[192,2304]{1,0:T(8,128)(2,1)}, bf16[192,2304]{1,0:T(8,128)(2,1)S(1)}, u32[]{:S(2)}, u32[]{:S(2)}) collective-permute-start(bf16[192,2304]{1,0:T(8,128)(2,1)} %get-tuple-element.293.refs_2_), channel_id=1, source_target_pairs={{8,0},{16,8},{24,16},{28,24},{20,28},{12,20},{4,12},{0,4},{9,1},{1... | collective-permute-start | bytes 2654216 | tf_op jit(solution)/shard_map/ppermute | solution.py:61
  118.9 23.2 %collective-permute-start.22 = (bf16[256,1536]{1,0:T(8,128)(2,1)S(1)}, bf16[256,1536]{1,0:T(8,128)(2,1)S(1)}, u32[]{:S(2)}, u32[]{:S(2)}) collective-permute-start(bf16[256,1536]{1,0:T(8,128)(2,1)S(1)} %get-tuple-element.299), channel_id=1, source_target_pairs={{0,2},{1,3},{2,0},{3,1},{4,6},{5,7},{6,4},{7,5},{8,10},{9,11},{10,... | collective-permute-start | bytes 2359304 | tf_op jit(solution)/shard_map/ppermute | solution.py:23
  149.8 22.7 %collective-permute-start.29 = (bf16[256,1536]{1,0:T(8,128)(2,1)S(1)}, bf16[256,1536]{1,0:T(8,128)(2,1)S(1)}, u32[]{:S(2)}, u32[]{:S(2)}) collective-permute-start(bf16[256,1536]{1,0:T(8,128)(2,1)S(1)} %get-tuple-element.313), channel_id=1, source_target_pairs={{0,2},{1,3},{2,0},{3,1},{4,6},{5,7},{6,4},{7,5},{8,10},{9,11},{10,... | collective-permute-start | bytes 2359304 | tf_op jit(solution)/shard_map/ppermute | solution.py:23
  225.9 33.6 %collective-permute-start.44 = (bf16[512,1536]{1,0:T(8,128)(2,1)}, bf16[512,1536]{1,0:T(8,128)(2,1)}, u32[]{:S(2)}, u32[]{:S(2)}) collective-permute-start(bf16[512,1536]{1,0:T(8,128)(2,1)} %pad_maximum_fusion.2.refs_2_.refs_4_), channel_id=1, source_target_pairs={{0,1},{1,0},{2,3},{3,2},{4,5},{5,4},{6,7},{7,6},{8,9},{9,8},{10,11... | collective-permute-start | bytes 4718600 | tf_op jit(solution)/shard_map/ppermute | solution.py:27
  247.5 30.8 %collective-permute-start.50 = (bf16[256,1536]{1,0:T(8,128)(2,1)S(1)}, bf16[256,1536]{1,0:T(8,128)(2,1)S(1)}, u32[]{:S(2)}, u32[]{:S(2)}) collective-permute-start(bf16[256,1536]{1,0:T(8,128)(2,1)S(1)} %get-tuple-element.349), channel_id=1, source_target_pairs={{0,2},{1,3},{2,0},{3,1},{4,6},{5,7},{6,4},{7,5},{8,10},{9,11},{10,... | collective-permute-start | bytes 2359304 | tf_op jit(solution)/shard_map/ppermute | solution.py:23
  252.4 25.9 %collective-permute-start.49 = (bf16[192,1536]{1,0:T(8,128)(2,1)S(1)}, bf16[192,1536]{1,0:T(8,128)(2,1)S(1)}, u32[]{:S(2)}, u32[]{:S(2)}) collective-permute-start(bf16[192,1536]{1,0:T(8,128)(2,1)S(1)} %get-tuple-element.348.refs_0_), channel_id=1, source_target_pairs={{8,0},{16,8},{24,16},{28,24},{20,28},{12,20},{4,12},{0,4},{9,1},{1... | collective-permute-start | bytes 1769480 | tf_op jit(solution)/shard_map/ppermute | solution.py:61
  253.7 24.6 %collective-permute-start.48 = (bf16[192,1536]{1,0:T(8,128)(2,1)S(1)}, bf16[192,1536]{1,0:T(8,128)(2,1)S(1)}, u32[]{:S(2)}, u32[]{:S(2)}) collective-permute-start(bf16[192,1536]{1,0:T(8,128)(2,1)S(1)} %get-tuple-element.348.refs_0_), channel_id=1, source_target_pairs={{0,8},{8,16},{16,24},{24,28},{28,20},{20,12},{12,4},{4,0},{1,9},{9... | collective-permute-start | bytes 1769480 | tf_op jit(solution)/shard_map/ppermute | solution.py:56
  279.9 24.2 %collective-permute-start.51 = (bf16[192,1536]{1,0:T(8,128)(2,1)S(1)}, bf16[192,1536]{1,0:T(8,128)(2,1)S(1)}, u32[]{:S(2)}, u32[]{:S(2)}) collective-permute-start(bf16[192,1536]{1,0:T(8,128)(2,1)S(1)} %get-tuple-element.354.refs_1_), channel_id=1, source_target_pairs={{0,8},{8,16},{16,24},{24,28},{28,20},{20,12},{12,4},{4,0},{1,9},{9... | collective-permute-start | bytes 1769480 | tf_op jit(solution)/shard_map/ppermute | solution.py:56
  281.2 22.9 %collective-permute-start.52 = (bf16[192,1536]{1,0:T(8,128)(2,1)S(1)}, bf16[192,1536]{1,0:T(8,128)(2,1)S(1)}, u32[]{:S(2)}, u32[]{:S(2)}) collective-permute-start(bf16[192,1536]{1,0:T(8,128)(2,1)S(1)} %get-tuple-element.355.refs_2_), channel_id=1, source_target_pairs={{8,0},{16,8},{24,16},{28,24},{20,28},{12,20},{4,12},{0,4},{9,1},{1... | collective-permute-start | bytes 1769480 | tf_op jit(solution)/shard_map/ppermute | solution.py:61
  335.5 357.2 %reduce-scatter.6.cloned.1.call-start = ((), (), s32[]{:S(2)}) async-start(), calls=%async_computation.4 | async-start | bytes 5308416 | tf_op jit(solution)/shard_map/reduce_scatter | solution.py:1121
  364.7 24.4 %collective-permute-start.61 = (bf16[256,1536]{1,0:T(8,128)(2,1)S(1)}, bf16[256,1536]{1,0:T(8,128)(2,1)S(1)}, u32[]{:S(2)}, u32[]{:S(2)}) collective-permute-start(bf16[256,1536]{1,0:T(8,128)(2,1)S(1)} %get-tuple-element.382), channel_id=1, source_target_pairs={{0,2},{1,3},{2,0},{3,1},{4,6},{5,7},{6,4},{7,5},{8,10},{9,11},{10,... | collective-permute-start | bytes 2359304 | tf_op jit(solution)/shard_map/ppermute | solution.py:23
  417.3 275.4 %reduce-scatter.8.cloned.1.call-start = ((), (), s32[]{:S(2)}) async-start(), calls=%async_computation.5 | async-start | bytes 3981312 | tf_op jit(solution)/shard_map/reduce_scatter | solution.py:1121
  474.1 34.9 %collective-permute-start.71 = (bf16[256,1536]{1,0:T(8,128)(2,1)S(1)}, bf16[256,1536]{1,0:T(8,128)(2,1)S(1)}, u32[]{:S(2)}, u32[]{:S(2)}) collective-permute-start(bf16[256,1536]{1,0:T(8,128)(2,1)S(1)} %get-tuple-element.436), channel_id=1, source_target_pairs={{0,2},{1,3},{2,0},{3,1},{4,6},{5,7},{6,4},{7,5},{8,10},{9,11},{10,... | collective-permute-start | bytes 2359304 | tf_op jit(solution)/shard_map/ppermute | solution.py:23
  475.6 31.6 %collective-permute-start.70 = (bf16[2,64,768]{2,1,0:T(8,128)(2,1)S(1)}, bf16[2,64,768]{2,1,0:T(8,128)(2,1)S(1)}, u32[]{:S(2)}, u32[]{:S(2)}) collective-permute-start(bf16[2,64,768]{2,1,0:T(8,128)(2,1)S(1)} %pad_maximum_fusion.10), channel_id=1, source_target_pairs={{0,2},{1,3},{2,0},{3,1},{4,6},{5,7},{6,4},{7,5},{8,10},{9,11},{10,... | collective-permute-start | bytes 589832 | tf_op jit(solution)/shard_map/ppermute | solution.py:23
  525.1 60.5 %collective-permute-start.77 = (bf16[1536,768]{1,0:T(8,128)(2,1)}, bf16[1536,768]{1,0:T(8,128)(2,1)}, u32[]{:S(2)}, u32[]{:S(2)}) collective-permute-start(bf16[1536,768]{1,0:T(8,128)(2,1)} %get-tuple-element.458), channel_id=1, source_target_pairs={{0,2},{1,3},{2,0},{3,1},{4,6},{5,7},{6,4},{7,5},{8,10},{9,11},{10,... | collective-permute-start | bytes 7077896 | tf_op jit(solution)/shard_map/ppermute | solution.py:23
  558.7 40.2 %collective-permute-start.59 = (bf16[512,1536]{1,0:T(8,128)(2,1)}, bf16[512,1536]{1,0:T(8,128)(2,1)}, u32[]{:S(2)}, u32[]{:S(2)}) collective-permute-start(bf16[512,1536]{1,0:T(8,128)(2,1)} %get-tuple-element.378), channel_id=1, source_target_pairs={{0,1},{1,0},{2,3},{3,2},{4,5},{5,4},{6,7},{7,6},{8,9},{9,8},{10,11... | collective-permute-start | bytes 4718600 | tf_op jit(solution)/shard_map/ppermute | solution.py:27
  559.2 42.8 %collective-permute-start.80 = (bf16[512,1536]{1,0:T(8,128)(2,1)}, bf16[512,1536]{1,0:T(8,128)(2,1)}, u32[]{:S(2)}, u32[]{:S(2)}) collective-permute-start(bf16[512,1536]{1,0:T(8,128)(2,1)} %get-tuple-element.468), channel_id=1, source_target_pairs={{0,1},{1,0},{2,3},{3,2},{4,5},{5,4},{6,7},{7,6},{8,9},{9,8},{10,11... | collective-permute-start | bytes 4718600 | tf_op jit(solution)/shard_map/ppermute | solution.py:27
  567.2 37.2 %collective-permute-start.79 = (bf16[256,1536]{1,0:T(8,128)(2,1)S(1)}, bf16[256,1536]{1,0:T(8,128)(2,1)S(1)}, u32[]{:S(2)}, u32[]{:S(2)}) collective-permute-start(bf16[256,1536]{1,0:T(8,128)(2,1)S(1)} %copy-done.69), channel_id=1, source_target_pairs={{0,2},{1,3},{2,0},{3,1},{4,6},{5,7},{6,4},{7,5},{8,10},{9,11},{10,... | collective-permute-start | bytes 2359304 | tf_op jit(solution)/shard_map/ppermute | solution.py:23
  568.6 29.1 %collective-permute-start.75 = (bf16[2,16,1536]{2,1,0:T(8,128)(2,1)S(1)}, bf16[2,16,1536]{2,1,0:T(8,128)(2,1)S(1)}, u32[]{:S(2)}, u32[]{:S(2)}) collective-permute-start(bf16[2,16,1536]{2,1,0:T(8,128)(2,1)S(1)} %slice.172), channel_id=1, source_target_pairs={{0,2},{1,3},{2,0},{3,1},{4,6},{5,7},{6,4},{7,5},{8,10},{9,11},{10,... | collective-permute-start | bytes 294920 | tf_op jit(solution)/shard_map/ppermute | solution.py:23
  598.9 26.6 %collective-permute-start.81 = (bf16[256,1536]{1,0:T(8,128)(2,1)S(1)}, bf16[256,1536]{1,0:T(8,128)(2,1)S(1)}, u32[]{:S(2)}, u32[]{:S(2)}) collective-permute-start(bf16[256,1536]{1,0:T(8,128)(2,1)S(1)} %get-tuple-element.473), channel_id=1, source_target_pairs={{0,2},{1,3},{2,0},{3,1},{4,6},{5,7},{6,4},{7,5},{8,10},{9,11},{10,... | collective-permute-start | bytes 2359304 | tf_op jit(solution)/shard_map/ppermute | solution.py:23
  623.5 25.4 %collective-permute-start.78 = (bf16[256,1536]{1,0:T(8,128)(2,1)S(1)}, bf16[256,1536]{1,0:T(8,128)(2,1)S(1)}, u32[]{:S(2)}, u32[]{:S(2)}) collective-permute-start(bf16[256,1536]{1,0:T(8,128)(2,1)S(1)} %get-tuple-element.464), channel_id=1, source_target_pairs={{0,2},{1,3},{2,0},{3,1},{4,6},{5,7},{6,4},{7,5},{8,10},{9,11},{10,... | collective-permute-start | bytes 2359304 | tf_op jit(solution)/shard_map/ppermute | solution.py:23
  625.0 60.0 %collective-permute-start.87 = (bf16[256,1536]{1,0:T(8,128)(2,1)}, bf16[256,1536]{1,0:T(8,128)(2,1)S(1)}, u32[]{:S(2)}, u32[]{:S(2)}) collective-permute-start(bf16[256,1536]{1,0:T(8,128)(2,1)} %get-tuple-element.492), channel_id=1, source_target_pairs={{0,2},{1,3},{2,0},{3,1},{4,6},{5,7},{6,4},{7,5},{8,10},{9,11},{10,... | collective-permute-start | bytes 2359304 | tf_op jit(solution)/shard_map/ppermute | solution.py:23
  667.2 30.5 %collective-permute-start.93 = (bf16[192,1920]{1,0:T(8,128)(2,1)}, bf16[192,1920]{1,0:T(8,128)(2,1)S(1)}, u32[]{:S(2)}, u32[]{:S(2)}) collective-permute-start(bf16[192,1920]{1,0:T(8,128)(2,1)} %get-tuple-element.508), channel_id=1, source_target_pairs={{0,8},{8,16},{16,24},{24,28},{28,20},{20,12},{12,4},{4,0},{1,9},{9... | collective-permute-start | bytes 2211848 | tf_op jit(solution)/shard_map/ppermute | solution.py:56
  669.0 28.7 %collective-permute-start.94 = (bf16[192,1920]{1,0:T(8,128)(2,1)}, bf16[192,1920]{1,0:T(8,128)(2,1)}, u32[]{:S(2)}, u32[]{:S(2)}) collective-permute-start(bf16[192,1920]{1,0:T(8,128)(2,1)} %get-tuple-element.509), channel_id=1, source_target_pairs={{8,0},{16,8},{24,16},{28,24},{20,28},{12,20},{4,12},{0,4},{9,1},{1... | collective-permute-start | bytes 2211848 | tf_op jit(solution)/shard_map/ppermute | solution.py:61
  (177 other events, 1626.8 us)
Sparse Core Ops, SparseCore 0:
  335.6 95.5 reduce-scatter.3
  434.9 95.0 reduce-scatter.5
  533.6 86.4 reduce-scatter.7
